TPU v7x, 32 devices: a whole 2x2x4 slice. The times are simulated.
32 devices in a mesh: dp: 4 (over z), expert: 4 (over y, x), pair: 2 (over core).
Axes of the slice: x: 2, y: 2, z: 4, core: 2. Of those that a mesh axis runs over, the one named last changes fastest.
Arguments:
- tokens: bfloat16 [2048, 2048], P(('dp', 'expert'), 'pair'), may hold values from -6 to 6
- grad_out: bfloat16 [2048, 2048], P(('dp', 'expert'), 'pair'), may hold values from -6 to 6
- routes: int32 [2048, 2], P(('dp', 'expert')), may hold values from 0 to 3, all different within a row; in each aligned block of 128 rows (0 to 127, 128 to 255, ...) at most 96 rows name the same one
- gate_probs: float32 [2048, 2], P(('dp', 'expert')), may hold values from 0.1 to 1
- gate_weight: bfloat16 [4, 2048, 768], P('expert', None, 'pair'), may hold values from -0.125 to 0.125
- up_weight: bfloat16 [4, 2048, 768], P('expert', None, 'pair'), may hold values from -0.125 to 0.125
- down_weight: bfloat16 [4, 768, 2048], P('expert', 'pair'), may hold values from -0.21875 to 0.21875
Outputs:
- grad_input: bfloat16 [2048, 2048], P(('dp', 'expert'), 'pair')
- grad_probs: float32 [2048, 2], P(('dp', 'expert'))
- grad_down: float32 [4, 2048, 768], P('expert', 'dp', 'pair')
Inputs may be any that keep to these rules, and one draw needn't show every extreme that they name: `routes`: each row names 2 different experts. In each aligned block of 128 rows (the tokens of one device) no expert is named by more than 96 rows, a bound that some block reaches.
All inputs are finite; a program needn't handle non-finite values.
Results may differ from a plain program's by a relative error of at most 0.02.
Values may be sent and summed in bfloat16 or wider, within the bound.
No kernel may reach another device: no remote copies, remote signals or barrier semaphores. Data moves between devices by JAX's collectives and lax.ppermute only.
A program may use at most 64 MiB of HBM per device.

v0:
```python
import jax
import jax.numpy as jnp
from jax import lax
from jax.sharding import PartitionSpec as P


def on_device(tokens, grad_out, routes, gate_probs, gate_weight, up_weight, down_weight):
    local_count = tokens.shape[0]
    half_width = tokens.shape[1]
    fanout = routes.shape[1]
    experts = lax.axis_size("expert")
    capacity = 3 * local_count * fanout // (2 * experts)
    expert_ids = jnp.arange(experts, dtype=jnp.int32)
    hits = jnp.sum((routes[:, :, None] == expert_ids[None, None, :]).astype(jnp.int32), axis=1)
    before = jnp.cumsum(hits, axis=0) - hits
    position = jnp.take_along_axis(before, routes, axis=1)
    target = (routes * capacity + position).reshape(-1)
    buffer_rows = experts * capacity
    sent_x = (
        jnp.zeros((buffer_rows, half_width), jnp.bfloat16)
        .at[target]
        .set(jnp.repeat(tokens, fanout, axis=0))
    )
    sent_dy = (
        jnp.zeros((buffer_rows, half_width), jnp.bfloat16)
        .at[target]
        .set(jnp.repeat(grad_out, fanout, axis=0))
    )
    sent_prob = jnp.zeros((buffer_rows,), jnp.float32).at[target].set(gate_probs.reshape(-1))
    sent_x = sent_x.reshape(experts, capacity, half_width)
    sent_dy = sent_dy.reshape(experts, capacity, half_width)
    sent_prob = sent_prob.reshape(experts, capacity)
    recv_x, recv_dy, recv_prob = (
        lax.all_to_all(sent_x, "expert", split_axis=0, concat_axis=0, tiled=True),
        lax.all_to_all(sent_dy, "expert", split_axis=0, concat_axis=0, tiled=True),
        lax.all_to_all(
            sent_prob.astype(jnp.bfloat16), "expert", split_axis=0, concat_axis=0, tiled=True
        ).astype(sent_prob.dtype),
    )
    full_x, full_dy = (
        lax.all_gather(recv_x, "pair", axis=2, tiled=True),
        lax.all_gather(recv_dy, "pair", axis=2, tiled=True),
    )
    model_width = full_x.shape[2]
    inputs = full_x.reshape(buffer_rows, model_width)
    upstream = full_dy.reshape(buffer_rows, model_width)
    weight_row = recv_prob.reshape(buffer_rows)
    gate_mat = gate_weight[0]
    up_mat = up_weight[0]
    down_mat = down_weight[0]
    contract_last = (((1,), (1,)), ((), ()))
    gate_pre = jnp.dot(inputs, gate_mat, preferred_element_type=jnp.float32)
    up_pre = jnp.dot(inputs, up_mat, preferred_element_type=jnp.float32)
    sigma = jax.nn.sigmoid(gate_pre)
    active = gate_pre * sigma
    hidden = active * up_pre
    back = lax.dot_general(upstream, down_mat, contract_last, preferred_element_type=jnp.float32)
    prob_part = jnp.sum(hidden * back, axis=1)
    scaled = (weight_row[:, None] * upstream.astype(jnp.float32)).astype(jnp.bfloat16)
    weight_term = lax.dot_general(
        scaled,
        hidden.astype(jnp.bfloat16),
        (((0,), (0,)), ((), ())),
        preferred_element_type=jnp.float32,
    )
    grad_down = lax.psum_scatter(weight_term[None], "dp", scatter_dimension=1, tiled=True)
    grad_hidden = weight_row[:, None] * back
    grad_gate = (grad_hidden * up_pre * sigma * (1.0 + gate_pre * (1.0 - sigma))).astype(
        jnp.bfloat16
    )
    grad_up = (grad_hidden * active).astype(jnp.bfloat16)
    partial_value = lax.dot_general(
        grad_gate, gate_mat, contract_last, preferred_element_type=jnp.float32
    )
    partial_value = partial_value + lax.dot_general(
        grad_up, up_mat, contract_last, preferred_element_type=jnp.float32
    )
    summed = lax.psum_scatter(
        partial_value.reshape(experts, capacity, model_width).astype(jnp.bfloat16),
        "pair",
        scatter_dimension=2,
        tiled=True,
    ).astype(jnp.float32)
    prob_sum = lax.psum(prob_part.reshape(experts, capacity), "pair")
    returned, returned_prob = (
        lax.all_to_all(
            summed.astype(jnp.bfloat16), "expert", split_axis=0, concat_axis=0, tiled=True
        ).astype(summed.dtype),
        lax.all_to_all(
            prob_sum.astype(jnp.bfloat16), "expert", split_axis=0, concat_axis=0, tiled=True
        ).astype(prob_sum.dtype),
    )
    flat_back = returned.reshape(buffer_rows, half_width)
    collected = jnp.take(flat_back, target, axis=0).reshape(local_count, fanout, half_width)
    grad_input = jnp.sum(collected, axis=1).astype(jnp.bfloat16)
    grad_probs = jnp.take(returned_prob.reshape(buffer_rows), target, axis=0).reshape(
        local_count, fanout
    )
    return (grad_input, grad_probs, grad_down)


def solution(mesh):
    return jax.shard_map(
        on_device,
        mesh=mesh,
        in_specs=(
            P(("dp", "expert"), "pair"),
            P(("dp", "expert"), "pair"),
            P(("dp", "expert"), None),
            P(("dp", "expert"), None),
            P("expert", None, "pair"),
            P("expert", None, "pair"),
            P("expert", "pair", None),
        ),
        out_specs=(
            P(("dp", "expert"), "pair"),
            P(("dp", "expert"), None),
            P("expert", "dp", "pair"),
        ),
        check_vma=False,
    )
```

profile of v0, /device:TPU:0, one launch (start us, length us, event | category | flops | bytes accessed | tf_op | source)
XLA Modules:
  0.0 145.1 jit_solution(3397671920026032027)
XLA Ops:
  7.2 0.8 bitcast_or_fusion
  8.0 0.7 convert_reduce_fusion
  9.3 1.9 %gather_fusion.2 = s32[256]{0:T(256)S(1)} fusion(s32[128,4]{1,0:T(8,128)S(1)} %sub.6, s32[256]{0:T(256)S(1)} %reshape.152), kind=kCustom, calls=%fused_computation.2 | custom fusion | bytes 4096 | tf_op jit(solution)/shard_map/jit(take_along_axis)/gather | solution.py:16
  11.8 0.3 broadcast_in_dim.41
  12.0 0.2 reshape.178
  12.3 1.9 %scatter_custom_fusion.2 = bf16[384,1024]{1,0:T(8,128)(2,1)S(1)} fusion(s32[256]{0:T(256)S(1)} %bitcast.43, bf16[256,1024]{1,0:T(8,128)(2,1)S(1)} %reshape.178, bf16[]{:T(256)} %constant.55.clone.1), kind=kCustom, calls=%fused_computation.26 | custom fusion | bytes 786434 | tf_op jit(solution)/shard_map/scatter | solution.py:22
  14.2 16.4 %all_to_all.30 = bf16[4,96,1024]{2,1,0:T(8,128)(2,1)} all-to-all(bf16[4,96,1024]{2,1,0:T(8,128)(2,1)S(1)} %bitcast.41), channel_id=1, replica_groups=mesh['dp'=4,'expert'=4,'pair'=2] {'expert'}, dimensions={0} | all-to-all | bytes 1572864 | tf_op jit(solution)/shard_map/all_to_all | solution.py:34
  30.7 0.3 broadcast_in_dim.40
  30.9 0.2 reshape.170
  31.2 1.9 %scatter_custom_fusion.1 = bf16[384,1024]{1,0:T(8,128)(2,1)S(1)} fusion(s32[256]{0:T(256)S(1)} %bitcast.44, bf16[256,1024]{1,0:T(8,128)(2,1)S(1)} %reshape.170, bf16[]{:T(256)} %constant.55.clone.1), kind=kCustom, calls=%fused_computation.28 | custom fusion | bytes 786434 | tf_op jit(solution)/shard_map/scatter | solution.py:27
  33.1 13.2 %all_to_all.31 = bf16[4,96,1024]{2,1,0:T(8,128)(2,1)} all-to-all(bf16[4,96,1024]{2,1,0:T(8,128)(2,1)S(1)} %bitcast.40), channel_id=1, replica_groups=mesh['dp'=4,'expert'=4,'pair'=2] {'expert'}, dimensions={0} | all-to-all | bytes 1572864 | tf_op jit(solution)/shard_map/all_to_all | solution.py:35
  46.6 1.4 scatter_custom_fusion
  48.1 7.0 %all_to_all.32 = bf16[4,1,96]{2,1,0:T(2,128)(2,1)S(1)} all-to-all(bf16[4,1,96]{2,1,0:T(2,128)(2,1)S(1)} %convert_element_type.81), channel_id=1, replica_groups=mesh['dp'=4,'expert'=4,'pair'=2] {'expert'}, dimensions={0} | all-to-all | bytes 1536 | tf_op jit(solution)/shard_map/all_to_all | solution.py:36
  55.2 2.6 %fusion.2 = f32[384,384]{0,1:T(8,128)S(1)} fusion(bf16[384,2048]{1,0:T(8,128)(2,1)} %bitcast.49, bf16[1,2048,384]{2,1,0:T(8,128)(2,1)S(1)} %copy-done), kind=kOutput, calls=%fused_computation.11 | convolution fusion | flops 603979776 | bytes 3735552 | tf_op jit(solution)/shard_map/dot_general | solution.py:52
  57.8 1.0 fusion.5
  58.9 2.9 %multiply_reduce_fusion = (f32[384]{0:T(512)S(1)}, f32[384,384]{0,1:T(8,128)S(1)}) fusion(f32[384,384]{0,1:T(8,128)S(1)} %fusion.5, f32[384,384]{0,1:T(8,128)S(1)} %fusion.2, bf16[384,2048]{1,0:T(8,128)(2,1)} %bitcast.47, bf16[1,384,2048]{2,1,0:T(8,128)(2,1)} %param.13), kind=kOutput, calls=%fused_computation.21 | convolution fusion | flops 605011584 | bytes 4916736 | tf_op jit(solution)/shard_map/dot_general | solution.py:57
  61.8 1.1 fusion
  62.9 0.2 copy-done.2
  63.2 2.3 %add_convert_fusion = bf16[384,2048]{1,0:T(8,128)(2,1)} fusion(f32[384,2048]{1,0:T(8,128)S(1)} %fusion, bf16[1,2048,384]{2,1,0:T(8,128)(2,1)S(1)} %copy-done.2, f32[384,384]{0,1:T(8,128)S(1)} %get-tuple-element.18, f32[384]{0:T(512)S(1)} %reshape.132, f32[384,384]{0,1:T(8,128)S(1)} %fusion.2), kind=kOutput, calls=%fused_computation.7 | convolution fusion | flops 606584832 | bytes 7472640 | tf_op jit(solution)/shard_map/dot_general | solution.py:75
  65.5 0.2 reduce-scatter.5.cloned.1.call-start
  65.7 4.3 %convolution_bitcast_fusion = f32[1,2048,384]{2,1,0:T(8,128)} fusion(bf16[384,2048]{1,0:T(8,128)(2,1)} %bitcast.48, f32[384]{0:T(512)S(1)} %reshape.132, f32[384,384]{0,1:T(8,128)S(1)} %fusion.5, f32[384,384]{0,1:T(8,128)S(1)} %fusion.2), kind=kOutput, calls=%fused_computation.8 | convolution fusion | flops 607223808 | bytes 5899776 | tf_op jit(solution)/shard_map/dot_general | solution.py:60
  70.1 2.5 %psum.7 = bf16[4,96]{1,0:T(4,128)(2,1)S(1)} all-reduce(f32[4,96]{1,0:T(4,128)S(1)} %reshape.131), channel_id=1, replica_groups=mesh['dp'=4,'expert'=4,'pair'=2] {'pair'}, use_global_device_ids=true, to_apply=%region_8.9 | all-reduce | flops 384 | bytes 2304 | tf_op jit(solution)/shard_map/psum | solution.py:84
  72.6 7.0 %all_to_all.33 = bf16[4,1,96]{2,1,0:T(2,128)(2,1)S(1)} all-to-all(bf16[4,1,96]{2,1,0:T(2,128)(2,1)S(1)} %copy.66), channel_id=1, replica_groups=mesh['dp'=4,'expert'=4,'pair'=2] {'expert'}, dimensions={0} | all-to-all | bytes 1536 | tf_op jit(solution)/shard_map/all_to_all | solution.py:89
  79.6 4.2 %all-to-all-start.3 = ((bf16[4,96,1024]{2,1,0:T(8,128)(2,1)}), bf16[4,96,1024]{2,1,0:T(8,128)(2,1)}, u32[]{:S(2)}, u32[]{:S(2)}) async-start(bf16[4,96,1024]{2,1,0:T(8,128)(2,1)} %reduce-scatter.3.cloned.1.call-done), calls=%async_computation.4 | async-start | bytes 1572864 | tf_op jit(solution)/shard_map/all_to_all | solution.py:86
  83.9 1.9 %gather_fusion.1 = f32[256]{0:T(256)S(1)} fusion(f32[384]{0:T(512)S(1)} %reshape.135, s32[1024]{0:T(1024)S(1)} %pad_clamp_fusion), kind=kCustom, calls=%fused_computation.1 | custom fusion | bytes 3072 | tf_op jit(solution)/shard_map/jit(_take)/gather | solution.py:96
  86.1 0.6 broadcast_select_fusion
  86.8 7.3 %all-to-all-done.3 = bf16[4,96,1024]{2,1,0:T(8,128)(2,1)} async-done(((bf16[4,96,1024]{2,1,0:T(8,128)(2,1)}), bf16[4,96,1024]{2,1,0:T(8,128)(2,1)}, u32[]{:S(2)}, u32[]{:S(2)}) %all-to-all-start.3) | async-done | bytes 786464 | tf_op jit(solution)/shard_map/all_to_all | solution.py:86
  94.1 1.3 bitcast_convert_fusion
  95.4 2.0 %gather_fusion = f32[256,1024]{1,0:T(8,128)} fusion(f32[384,1024]{1,0:T(8,128)S(1)} %bitcast_convert_fusion, s32[1024]{0:T(1024)S(1)} %pad_clamp_fusion), kind=kCustom, calls=%fused_computation | custom fusion | bytes 2098176 | tf_op jit(solution)/shard_map/jit(_take)/gather | solution.py:94
  97.5 1.8 %gather.18 = f32[128,2,1024]{2,1,0:T(2,128)S(1)} reshape(f32[256,1024]{1,0:T(8,128)} %gather_fusion) | data formatting | bytes 2097152 | tf_op jit(solution)/shard_map/jit(_take)/gather | solution.py:94
  99.3 2.2 %select_reduce_fusion = bf16[128,1024]{1,0:T(8,128)(2,1)} fusion(f32[128,2,1024]{2,1,0:T(2,128)S(1)} %gather.18, pred[128,2]{1,0:T(8,128)(4,1)S(1)} %copy.62), kind=kLoop, calls=%fused_computation.19 | loop fusion | flops 393216 | bytes 1310976 | tf_op jit(solution)/shard_map/reduce_sum | solution.py:95
  101.5 37.1 %reduce-scatter.5.cloned.1.call-done = f32[1,512,384]{2,1,0:T(8,128)} async-done(((f32[1,2048,384]{2,1,0:T(8,128)}), f32[1,512,384]{2,1,0:T(8,128)}) %reduce-scatter.5.cloned.1.call-update) | async-done | bytes 786448 | tf_op jit(solution)/shard_map/reduce_scatter | solution.py:66
  (50 shorter events, 2.3 us)
Async XLA Ops:
  7.2 48.0 %copy-start = (bf16[1,2048,384]{2,1,0:T(8,128)(2,1)S(1)}, bf16[1,2048,384]{2,1,0:T(8,128)(2,1)}, u32[]{:S(2)}) copy-start(bf16[1,2048,384]{2,1,0:T(8,128)(2,1)} %param.11) | copy-start | bytes 4718596
  7.2 48.0 %all-gather.5.cloned.1.call-start = ((), (), s32[]{:S(2)}) async-start(), calls=%async_computation.8 | async-start | bytes 2359296 | tf_op jit(solution)/shard_map/all_gather | solution.py:41
  9.3 2.2 %copy-start.5 = (s32[128,2]{0,1:T(2,128)S(1)}, s32[128,2]{0,1:T(2,128)}, u32[]{:S(2)}) copy-start(s32[128,2]{0,1:T(2,128)} %param.9) | copy-start | bytes 3076
  9.3 2.5 %copy-start.3 = (bf16[128,1024]{1,0:T(8,128)(2,1)S(1)}, bf16[128,1024]{1,0:T(8,128)(2,1)}, u32[]{:S(2)}) copy-start(bf16[128,1024]{1,0:T(8,128)(2,1)} %param.7) | copy-start | bytes 786436
  12.2 18.4 %copy-start.4 = (bf16[128,1024]{1,0:T(8,128)(2,1)S(1)}, bf16[128,1024]{1,0:T(8,128)(2,1)}, u32[]{:S(2)}) copy-start(bf16[128,1024]{1,0:T(8,128)(2,1)} %param.8) | copy-start | bytes 786436
  30.6 28.3 %all-gather.3.cloned.1.call-start = ((), (), s32[]{:S(2)}) async-start(), calls=%async_computation.7 | async-start | bytes 2359296 | tf_op jit(solution)/shard_map/all_gather | solution.py:42
  31.1 15.2 %copy-start.6 = (f32[128,2]{0,1:T(2,128)S(1)}, f32[128,2]{0,1:T(2,128)}, u32[]{:S(2)}) copy-start(f32[128,2]{0,1:T(2,128)} %param.10) | copy-start | bytes 3076
  46.3 33.3 %reduce-scatter.3.cloned.1.call-start = ((), (), s32[]{:S(2)}) async-start(), calls=%async_computation.9 | async-start | bytes 2359296 | tf_op jit(solution)/shard_map/reduce_scatter | solution.py:78
  55.2 2.6 %copy-start.1 = (bf16[1,2048,384]{2,1,0:T(8,128)(2,1)S(1)}, bf16[1,2048,384]{2,1,0:T(8,128)(2,1)}, u32[]{:S(2)}) copy-start(bf16[1,2048,384]{2,1,0:T(8,128)(2,1)} %param.12) | copy-start | bytes 4718596
  55.2 2.6 %copy-start.7 = (bf16[4,96,2048]{2,1,0:T(8,128)(2,1)S(1)}, bf16[4,96,2048]{2,1,0:T(8,128)(2,1)}, u32[]{:S(2)}) copy-start(bf16[4,96,2048]{2,1,0:T(8,128)(2,1)} %all-gather.5.cloned.1.call-done) | copy-start | bytes 4718596
  61.8 1.4 copy-start.2
  65.5 73.1 %reduce-scatter.5.cloned.1.call-start = ((), (), s32[]{:S(2)}) async-start(), calls=%async_computation.10 | async-start | bytes 3932160 | tf_op jit(solution)/shard_map/reduce_scatter | solution.py:66
  79.6 14.6 %all-to-all-start.3 = ((bf16[4,96,1024]{2,1,0:T(8,128)(2,1)}), bf16[4,96,1024]{2,1,0:T(8,128)(2,1)}, u32[]{:S(2)}, u32[]{:S(2)}) async-start(bf16[4,96,1024]{2,1,0:T(8,128)(2,1)} %reduce-scatter.3.cloned.1.call-done), calls=%async_computation.4 | async-start | bytes 1572864 | tf_op jit(solution)/shard_map/all_to_all | solution.py:86
Sparse Core Ops, SparseCore 0:
  30.7 9.5 all-gather.4
  46.4 9.5 all-gather.2
  65.6 8.5 reduce-scatter.2
  77.0 61.4 reduce-scatter.4
where the time goes:
time: 146 us; the launch traced here: 145 us
  blocking collectives  46 us (32%)
  waiting for transfers between devices  44.5 us (30%)
  local copies, waits for them, and re-layouts  16 us (11%)
  matrix products  14.2 us (10%)
  between operations  14.1 us (10%)
  other arithmetic  5.8 us (4%)
  starting transfers between devices  4.54 us (3%)
    reduce_scatter x1, waiting for transfers between devices, on_device(): lax.psum_scatter(weight_term[None], 'dp', scatter_dimension=1, tiled=True)  37.1 us
    all_to_all x1, blocking collectives, on_device(): lax.all_to_all(sent_x, 'expert', split_axis=0, concat_axis=0, tiled=True)  16.4 us
    all_to_all x1, blocking collectives, on_device(): lax.all_to_all(sent_dy, 'expert', split_axis=0, concat_axis=0, tiled=True)  13.2 us
    all_to_all x1, waiting for transfers between devices, on_device(): lax.all_to_all(summed.astype(jnp.bfloat16), 'expert', split_axis=0, conca...  7.34 us
    all_to_all x1, blocking collectives, on_device(): lax.all_to_all(sent_prob.astype(jnp.bfloat16), 'expert', split_axis=0, co...  6.98 us
    all_to_all x1, blocking collectives, on_device(): lax.all_to_all(prob_sum.astype(jnp.bfloat16), 'expert', split_axis=0, con...  6.97 us
    dot_general x1, matrix products, on_device(): lax.dot_general(scaled, hidden.astype(jnp.bfloat16), (((0,), (0,)), ((),...  4.33 us
    all_to_all x1, starting transfers between devices, on_device(): lax.all_to_all(summed.astype(jnp.bfloat16), 'expert', split_axis=0, conca...  4.2 us
  transfers between devices with their start and end apart: 5, of which 2 were waited for; matrix products, arithmetic and copies ran while one was open for 16% of the time, Pallas kernels for 0%

commit v1 on v0

v1 whole, which is shorter than its diff:
```python
import functools

import jax
import jax.numpy as jnp
from jax import lax
from jax.experimental import pallas as pl
from jax.experimental.pallas import tpu as pltpu
from jax.sharding import PartitionSpec as P

F32 = jnp.float32
BF16 = jnp.bfloat16
NT = (((1,), (1,)), ((), ()))
TN = (((0,), (0,)), ((), ()))
VMEM_LIMIT = 48 * 1024 * 1024


def dot(a, b, dims=(((1,), (0,)), ((), ()))):
    return lax.dot_general(a, b, dims, preferred_element_type=F32)


def call(body, out_shape, operands, scalars=None):
    in_specs = [pl.BlockSpec(memory_space=pltpu.VMEM)] * len(operands)
    if scalars is not None:
        operands = [scalars] + list(operands)
        in_specs = [pl.BlockSpec(memory_space=pltpu.SMEM)] + in_specs
    return pl.pallas_call(
        body,
        out_shape=out_shape,
        in_specs=in_specs,
        out_specs=jax.tree.map(lambda _: pl.BlockSpec(memory_space=pltpu.VMEM), out_shape),
        compiler_params=pltpu.CompilerParams(vmem_limit_bytes=VMEM_LIMIT),
    )(*operands)


def struct(shape, dtype):
    return jax.ShapeDtypeStruct(shape, dtype)


def pack_body(experts, cap, sc, routes_ref, probs_ref, tok_ref, dy_ref, *outs):
    x_out, a_out, b_out, s_out = outs[:experts], outs[experts:2 * experts], outs[2 * experts:3 * experts], outs[3 * experts]
    me, pair = sc[0], sc[1]
    fanout, count = routes_ref.shape
    half = dy_ref.shape[1] // 2
    off_a = pl.multiple_of(pair * half, half)
    off_b = pl.multiple_of((1 - pair) * half, half)
    routes = routes_ref[...]
    probs = probs_ref[...]
    row = lax.broadcasted_iota(jnp.int32, (8, count), 0)
    hits = jnp.zeros((8, count), F32)
    weights = jnp.zeros((8, count), F32)
    for k in range(fanout):
        same = routes[k:k + 1, :] == (row ^ me)
        hits = hits + jnp.where(same, 1.0, 0.0)
        weights = weights + jnp.where(same, probs[k:k + 1, :], 0.0)
    earlier = lax.broadcasted_iota(jnp.int32, (count, count), 0) < lax.broadcasted_iota(jnp.int32, (count, count), 1)
    before = dot(hits.astype(BF16), jnp.where(earlier, 1.0, 0.0).astype(BF16)).astype(jnp.int32)
    slot = lax.broadcasted_iota(jnp.int32, (cap, count), 0)
    tok = tok_ref[...]
    for m in range(experts):
        chosen = (slot == before[m:m + 1, :]) & (hits[m:m + 1, :] > 0.5)
        pick = jnp.where(chosen, 1.0, 0.0)
        pick_b = pick.astype(BF16)
        s_out[m * cap:(m + 1) * cap, :] = pick_b
        x_out[m][...] = dot(pick_b, tok).astype(BF16)
        p_col = jnp.sum(pick * weights[m:m + 1, :], axis=1, keepdims=True)
        a_out[m][...] = (p_col * dot(pick_b, dy_ref[:, pl.ds(off_a, half)])).astype(BF16)
        b_out[m][...] = (p_col * dot(pick_b, dy_ref[:, pl.ds(off_b, half)])).astype(BF16)


def rows_of(refs):
    return jnp.concatenate([r[...] for r in refs], axis=0)


def forward_body(experts, sc, *refs):
    own, oth = refs[:experts], refs[experts:2 * experts]
    gw, uw, hid_ref, hid_b_ref, dgate_ref, act_ref = refs[2 * experts:]
    pair = sc[1]
    half = own[0].shape[1]
    mine = pl.ds(pl.multiple_of(pair * half, half), half)
    other = pl.ds(pl.multiple_of((1 - pair) * half, half), half)
    x_own, x_oth = rows_of(own), rows_of(oth)
    gate = dot(x_own, gw[mine, :]) + dot(x_oth, gw[other, :])
    up = dot(x_own, uw[mine, :]) + dot(x_oth, uw[other, :])
    sig = jax.nn.sigmoid(gate)
    act = gate * sig
    hid = act * up
    hid_ref[...] = hid
    hid_b_ref[...] = hid.astype(BF16)
    dgate_ref[...] = up * sig * (1.0 + gate * (1.0 - sig))
    act_ref[...] = act


def weight_body(experts, flag_at, want, sc, *refs):
    own, oth = refs[:experts], refs[experts:2 * experts]
    hid_b, out = refs[2 * experts:]
    use_own = sc[flag_at] == want

    @pl.when(use_own)
    def _():
        out[...] = dot(rows_of(own), hid_b[...], TN).astype(out.dtype)

    @pl.when(jnp.logical_not(use_own))
    def _():
        out[...] = dot(rows_of(oth), hid_b[...], TN).astype(out.dtype)


def backward_body(experts, sc, *refs):
    a_own, a_oth, b_own, b_oth = (refs[i * experts:(i + 1) * experts] for i in range(4))
    dw, gw, uw, hid_ref, dgate_ref, act_ref, keep_ref, send_ref, q_ref = refs[4 * experts:]
    pair = sc[1]
    quarter = a_own[0].shape[1]
    half = 2 * quarter

    def cols(index):
        return pl.ds(pl.multiple_of(index * quarter, quarter), quarter)

    back = dot(rows_of(a_own), dw[:, cols(3 * pair)], NT)
    back = back + dot(rows_of(a_oth), dw[:, cols(3 - 3 * pair)], NT)
    back = back + dot(rows_of(b_own), dw[:, cols(1 + pair)], NT)
    back = back + dot(rows_of(b_oth), dw[:, cols(2 - pair)], NT)
    g_gate = (back * dgate_ref[...]).astype(BF16)
    g_up = (back * act_ref[...]).astype(BF16)
    q = jnp.sum(back * hid_ref[...], axis=1, keepdims=True)
    other = pl.ds(pl.multiple_of((1 - pair) * half, half), half)
    mine = pl.ds(pl.multiple_of(pair * half, half), half)
    send_ref[:, :half] = (dot(g_gate, gw[other, :], NT) + dot(g_up, uw[other, :], NT)).astype(BF16)
    send_ref[:, half:] = split_columns(q)
    keep_ref[...] = (dot(g_gate, gw[mine, :], NT) + dot(g_up, uw[mine, :], NT)).astype(BF16)
    q_ref[...] = jnp.broadcast_to(q, q_ref.shape)


def split_columns(q):
    high = q.astype(BF16)
    low = (q - high.astype(F32)).astype(BF16)
    lane = lax.broadcasted_iota(jnp.int32, (q.shape[0], 128), 1)
    return jnp.where(lane == 0, high.astype(F32), jnp.where(lane == 1, low.astype(F32), 0.0)).astype(BF16)


def merge_body(experts, keep_ref, q_ref, recv_ref, *outs):
    cap, wide = outs[0].shape
    half = wide - 128
    for m in range(experts):
        rows = slice(m * cap, (m + 1) * cap)
        outs[m][:, :half] = (keep_ref[rows, :].astype(F32) + recv_ref[rows, :half].astype(F32)).astype(BF16)
        tail = recv_ref[rows, half:].astype(F32)
        outs[m][:, half:] = split_columns(q_ref[rows, 0:1] + tail[:, 0:1] + tail[:, 1:2])


def combine_body(experts, sc, pick_ref, routes_ref, probs_ref, *refs):
    parts, (out, gp_out) = refs[:experts], refs[experts:]
    cap, wide = parts[0].shape
    half = wide - 128
    me = sc[0]
    routes = routes_ref[...]
    total = None
    gp = jnp.zeros(gp_out.shape, F32)
    for m in range(experts):
        rows = dot(pick_ref[m * cap:(m + 1) * cap, :], parts[m][...], TN)
        total = rows[:, :half] if total is None else total + rows[:, :half]
        q = rows[:, half:half + 1] + rows[:, half + 1:half + 2]
        gp = gp + jnp.where(routes == (me ^ m), q, 0.0)
    out[...] = total.astype(BF16)
    gp_out[...] = gp / probs_ref[...]


def on_device(tokens, grad_out, routes, gate_probs, gate_weight, up_weight, down_weight):
    count, half = tokens.shape
    fanout = routes.shape[1]
    experts = lax.axis_size("expert")
    groups = lax.axis_size("dp")
    units = gate_weight.shape[2]
    cap = 3 * count * fanout // (2 * experts)
    slots = experts * cap
    quarter = half // 2
    gw, uw, dw = gate_weight[0], up_weight[0], down_weight[0]
    me, pair, group = lax.axis_index("expert"), lax.axis_index("pair"), lax.axis_index("dp")
    scalars = jnp.stack([me, pair, (group + pair) % 2]).astype(jnp.int32)

    def swap(value):
        return lax.ppermute(value, "pair", [(0, 1), (1, 0)])

    def cross(values):
        return [values[0]] + [
            lax.ppermute(values[m], "expert", [(i, i ^ m) for i in range(experts)]) for m in range(1, experts)
        ]

    packed = call(
        functools.partial(pack_body, experts, cap),
        [struct((cap, half), BF16)] * experts
        + [struct((cap, quarter), BF16)] * (2 * experts)
        + [struct((slots, count), BF16)],
        [routes.T, gate_probs.T, tokens, grad_out],
        scalars,
    )
    x_send, a_send, b_send = packed[:experts], packed[experts:2 * experts], packed[2 * experts:3 * experts]
    pick = packed[3 * experts]

    x_own = cross(x_send)
    a_own = cross(a_send)
    b_own = cross(b_send)
    x_oth = [swap(v) for v in x_own]
    a_oth = [swap(v) for v in a_own]
    b_oth = [swap(v) for v in b_own]

    square = struct((slots, units), F32)
    hid, hid_b, dgate, act = call(
        functools.partial(forward_body, experts),
        [square, struct((slots, units), BF16), square, square],
        [*x_own, *x_oth, gw, uw],
        scalars,
    )

    def block(own, oth, want, dtype):
        return call(
            functools.partial(weight_body, experts, 2, want),
            struct((2 * quarter // 2, units), dtype),
            [*own, *oth, hid_b],
            scalars,
        )

    if groups == 4:
        first = block(a_own, a_oth, 1, BF16)
        from_near = lax.ppermute(first, "dp", [(0, 1), (1, 0), (2, 3), (3, 2)])
        a_rest = block(a_own, a_oth, 0, F32)
        second = block(b_own, b_oth, 0, BF16)
        b_rest = block(b_own, b_oth, 1, F32)
        from_mid = lax.ppermute(second, "dp", [(1, 2), (2, 1)])
        from_end = lax.ppermute(second, "dp", [(0, 1), (3, 2)])
        inner = (group == 1) | (group == 2)
        third = jnp.where(inner, a_rest + from_near.astype(F32), b_rest).astype(BF16)
        from_far = lax.ppermute(third, "dp", [(0, 2), (2, 0), (1, 3), (3, 1)])
        grad_down = jnp.where(
            inner,
            b_rest + from_mid.astype(F32) + from_end.astype(F32),
            a_rest + from_near.astype(F32),
        ) + from_far.astype(F32)
        grad_down = grad_down[None]
    else:
        a_one, a_two = block(a_own, a_oth, 1, F32), block(a_own, a_oth, 0, F32)
        b_one, b_two = block(b_own, b_oth, 0, F32), block(b_own, b_oth, 1, F32)
        odd = group % 2 == 1
        whole = jnp.concatenate(
            [
                jnp.where(odd, a_one, a_two),
                jnp.where(odd, b_two, b_one),
                jnp.where(odd, b_one, b_two),
                jnp.where(odd, a_two, a_one),
            ],
            axis=0,
        )
        grad_down = lax.psum_scatter(whole[None], "dp", scatter_dimension=1, tiled=True)

    keep, send, q_own = call(
        functools.partial(backward_body, experts),
        [struct((slots, half), BF16), struct((slots, half + 128), BF16), struct((slots, 128), F32)],
        [*a_own, *a_oth, *b_own, *b_oth, dw, gw, uw, hid, dgate, act],
        scalars,
    )
    merged = call(
        functools.partial(merge_body, experts),
        [struct((cap, half + 128), BF16)] * experts,
        [keep, q_own, swap(send)],
    )
    returned = cross(merged)
    grad_input, grad_probs = call(
        functools.partial(combine_body, experts),
        [struct((count, half), BF16), struct((count, fanout), F32)],
        [pick, routes, gate_probs, *returned],
        scalars,
    )
    return grad_input, grad_probs, grad_down


def solution(mesh):
    return jax.shard_map(
        on_device,
        mesh=mesh,
        in_specs=(
            P(("dp", "expert"), "pair"),
            P(("dp", "expert"), "pair"),
            P(("dp", "expert"), None),
            P(("dp", "expert"), None),
            P("expert", None, "pair"),
            P("expert", None, "pair"),
            P("expert", "pair", None),
        ),
        out_specs=(
            P(("dp", "expert"), "pair"),
            P(("dp", "expert"), None),
            P("expert", "dp", "pair"),
        ),
        check_vma=False,
    )
```

time: 146 us -> 87.1 us (0.60)
  blocking collectives: 46 us -> 0 us
  starting transfers between devices: 4.54 us -> 27.5 us
  Pallas kernels: 0 us -> 17.4 us
  waiting for transfers between devices: 44.5 us -> 27.9 us
  matrix products: 14.2 us -> 0 us
  between operations: 14.1 us -> 0.81 us
  local copies, waits for them, and re-layouts: 16 us -> 8.67 us
    all_to_all x4 -> x0, blocking collectives: 43.5 us -> none  [the longest x1 16.4 us: on_device(): lax.all_to_all(sent_x, 'expert', split_axis=0, concat_axis=0, tiled=True)]
    reduce_scatter x2 -> x0, waiting for transfers between devices: 37.1 us -> none  [the longest x1 37.1 us: on_device(): lax.psum_scatter(weight_term[None], 'dp', scatter_dimension=1, tiled=True)]
    ppermute x0 -> x29, waiting for transfers between devices: none -> 27.9 us  [the longest x1 17.4 us: on_device(): from_far = lax.ppermute(third, 'dp', [(0, 2), (2, 0), (1, 3), (3, 1)])]
    ppermute x0 -> x29, starting transfers between devices: none -> 27.5 us  [the longest x12 16.6 us: cross(): lax.ppermute(values[m], 'expert', [(i, i ^ m) for i in range(experts)])]
    pallas_call x0 -> x9, Pallas kernels: none -> 17.4 us  [call(): pl.pallas_call(body, out_shape=out_shape, in_specs=in_specs, out_specs=ja...]
    dot_general x6 -> x0, matrix products: 14.2 us -> none  [the longest x1 4.33 us: on_device(): lax.dot_general(scaled, hidden.astype(jnp.bfloat16), (((0,), (0,)), ((),...]
    gather x10 -> x0, local copies, waits for them, and re-layouts: 8.4 us -> none  [the longest x2 3.87 us: on_device(): jnp.take(flat_back, target, axis=0).reshape(local_count, fanout, half_width)]
    unnamed x17 -> x29, local copies, waits for them, and re-layouts: 0.41 us -> 8.67 us
  transfers between devices with their start and end apart: 5 -> 29, of which waited for: 2 -> 8; matrix products, arithmetic and copies ran while one was open for 16% -> 5% of each run, Pallas kernels for 0% -> 17%
where the time goes in v1:
time: 87.1 us; the launch traced here: 86.8 us
  waiting for transfers between devices  27.9 us (32%)
  starting transfers between devices  27.5 us (32%)
  Pallas kernels  17.4 us (20%)
  local copies, waits for them, and re-layouts  8.67 us (10%)
  other arithmetic  4.45 us (5%)
    pallas_call x9, Pallas kernels, call(): pl.pallas_call(body, out_shape=out_shape, in_specs=in_specs, out_specs=ja...  17.4 us
    ppermute x1, waiting for transfers between devices, on_device(): from_far = lax.ppermute(third, 'dp', [(0, 2), (2, 0), (1, 3), (3, 1)])  17.4 us
    ppermute x12, starting transfers between devices, cross(): lax.ppermute(values[m], 'expert', [(i, i ^ m) for i in range(experts)])  16.6 us
    unnamed x29, local copies, waits for them, and re-layouts  8.67 us
    ppermute x12, waiting for transfers between devices, cross(): lax.ppermute(values[m], 'expert', [(i, i ^ m) for i in range(experts)])  8.21 us
    ppermute x13, starting transfers between devices, swap(): return lax.ppermute(value, 'pair', [(0, 1), (1, 0)])  3.23 us
    ppermute x1, starting transfers between devices, on_device(): from_end = lax.ppermute(second, 'dp', [(0, 1), (3, 2)])  2.93 us
    broadcast_in_dim x1, other arithmetic, on_device(): grad_down = grad_down[None]  2.46 us
  transfers between devices with their start and end apart: 29, of which 8 were waited for; matrix products, arithmetic and copies ran while one was open for 5% of the time, Pallas kernels for 17%

profile of v1, /device:TPU:0, one launch (start us, length us, event | category | flops | bytes accessed | tf_op | source)
XLA Modules:
  0.0 86.8 jit_solution(11448263624100910244)
XLA Ops:
  0.7 0.9 %copy-done.3 = bf16[128,1024]{1,0:T(8,128)(2,1)S(1)} copy-done((bf16[128,1024]{1,0:T(8,128)(2,1)S(1)}, bf16[128,1024]{1,0:T(8,128)(2,1)}, u32[]{:S(2)}) %copy-start.3) | copy-done | bytes 262168
  1.7 0.9 %copy-done.4 = bf16[128,1024]{1,0:T(8,128)(2,1)S(1)} copy-done((bf16[128,1024]{1,0:T(8,128)(2,1)S(1)}, bf16[128,1024]{1,0:T(8,128)(2,1)}, u32[]{:S(2)}) %copy-start.4) | copy-done | bytes 262168
  2.6 0.7 copy-done.9
  4.0 1.2 %shard_map.94 = (bf16[96,1024]{1,0:T(8,128)(2,1)S(1)}, bf16[96,1024]{1,0:T(8,128)(2,1)S(1)}, bf16[96,1024]{1,0:T(8,128)(2,1)S(1)}, bf16[96,1024]{1,0:T(8,128)(2,...) custom-call(s32[3]{0:T(128)S(1)} %pad_add_fusion.sc, ...), custom_call_target="tpu_custom_call" | custom-call | tf_op jit(solution)/shard_map/pallas_call | solution.py:26
  5.9 2.9 %collective-permute-start = (bf16[96,512]{1,0:T(8,128)(2,1)S(1)}, bf16[96,512]{1,0:T(8,128)(2,1)S(1)}, u32[]{:S(2)}, u32[]{:S(2)}) collective-permute-start(bf16[96,512]{1,0:T(8,128)(2,1)S(1)} %get-tuple-element.31), channel_id=1, source_target_pairs={{0,2},{2,0},{4,6},{6,4},{1,3},{3,1},{5,7},{7,5},{8,10},{10,8},{12,... | collective-permute-start | bytes 294920 | tf_op jit(solution)/shard_map/ppermute | solution.py:184
  8.9 2.0 %collective-permute-start.15 = (bf16[96,1024]{1,0:T(8,128)(2,1)S(1)}, bf16[96,1024]{1,0:T(8,128)(2,1)S(1)}, u32[]{:S(2)}, u32[]{:S(2)}) collective-permute-start(bf16[96,1024]{1,0:T(8,128)(2,1)S(1)} %get-tuple-element.40), channel_id=1, source_target_pairs={{0,4},{2,6},{4,0},{6,2},{1,5},{3,7},{5,1},{7,3},{8,12},{10,14},{12... | collective-permute-start | bytes 589832 | tf_op jit(solution)/shard_map/ppermute | solution.py:184
  10.9 1.4 %collective-permute-start.16 = (bf16[96,1024]{1,0:T(8,128)(2,1)S(1)}, bf16[96,1024]{1,0:T(8,128)(2,1)S(1)}, u32[]{:S(2)}, u32[]{:S(2)}) collective-permute-start(bf16[96,1024]{1,0:T(8,128)(2,1)S(1)} %get-tuple-element.41), channel_id=1, source_target_pairs={{0,6},{2,4},{4,2},{6,0},{1,7},{3,5},{5,3},{7,1},{8,14},{10,12},{12... | collective-permute-start | bytes 589832 | tf_op jit(solution)/shard_map/ppermute | solution.py:184
  12.3 1.5 %collective-permute-start.1 = (bf16[96,512]{1,0:T(8,128)(2,1)S(1)}, bf16[96,512]{1,0:T(8,128)(2,1)S(1)}, u32[]{:S(2)}, u32[]{:S(2)}) collective-permute-start(bf16[96,512]{1,0:T(8,128)(2,1)S(1)} %get-tuple-element.32), channel_id=1, source_target_pairs={{0,4},{2,6},{4,0},{6,2},{1,5},{3,7},{5,1},{7,3},{8,12},{10,14},{12... | collective-permute-start | bytes 294920 | tf_op jit(solution)/shard_map/ppermute | solution.py:184
  13.8 1.6 %collective-permute-start.2 = (bf16[96,512]{1,0:T(8,128)(2,1)S(1)}, bf16[96,512]{1,0:T(8,128)(2,1)S(1)}, u32[]{:S(2)}, u32[]{:S(2)}) collective-permute-start(bf16[96,512]{1,0:T(8,128)(2,1)S(1)} %get-tuple-element.33), channel_id=1, source_target_pairs={{0,6},{2,4},{4,2},{6,0},{1,7},{3,5},{5,3},{7,1},{8,14},{10,12},{12... | collective-permute-start | bytes 294920 | tf_op jit(solution)/shard_map/ppermute | solution.py:184
  15.5 8.2 %collective-permute-done.1.refs_2_ = bf16[96,512]{1,0:T(8,128)(2,1)S(1)} collective-permute-done((bf16[96,512]{1,0:T(8,128)(2,1)S(1)}, bf16[96,512]{1,0:T(8,128)(2,1)S(1)}, u32[]{:S(2)}, u32[]{:S(2)}) %collective-permute-start.1) | collective-permute-done | bytes 98336 | tf_op jit(solution)/shard_map/ppermute | solution.py:184
  25.2 1.1 %collective-permute-done.4.refs_5_ = bf16[96,512]{1,0:T(8,128)(2,1)S(1)} collective-permute-done((bf16[96,512]{1,0:T(8,128)(2,1)S(1)}, bf16[96,512]{1,0:T(8,128)(2,1)S(1)}, u32[]{:S(2)}, u32[]{:S(2)}) %collective-permute-start.4) | collective-permute-done | bytes 98336 | tf_op jit(solution)/shard_map/ppermute | solution.py:180
  26.8 1.7 %collective-permute-start.7 = (bf16[96,512]{1,0:T(8,128)(2,1)S(1)}, bf16[96,512]{1,0:T(8,128)(2,1)S(1)}, u32[]{:S(2)}, u32[]{:S(2)}) collective-permute-start(bf16[96,512]{1,0:T(8,128)(2,1)S(1)} %get-tuple-element.35), channel_id=1, source_target_pairs={{0,2},{2,0},{4,6},{6,4},{1,3},{3,1},{5,7},{7,5},{8,10},{10,8},{12,... | collective-permute-start | bytes 294920 | tf_op jit(solution)/shard_map/ppermute | solution.py:184
  28.5 1.5 %collective-permute-start.8 = (bf16[96,512]{1,0:T(8,128)(2,1)S(1)}, bf16[96,512]{1,0:T(8,128)(2,1)S(1)}, u32[]{:S(2)}, u32[]{:S(2)}) collective-permute-start(bf16[96,512]{1,0:T(8,128)(2,1)S(1)} %get-tuple-element.36), channel_id=1, source_target_pairs={{0,4},{2,6},{4,0},{6,2},{1,5},{3,7},{5,1},{7,3},{8,12},{10,14},{12... | collective-permute-start | bytes 294920 | tf_op jit(solution)/shard_map/ppermute | solution.py:184
  30.3 1.4 %copy-done = bf16[1,2048,384]{2,1,0:T(8,128)(2,1)S(1)} copy-done((bf16[1,2048,384]{2,1,0:T(8,128)(2,1)S(1)}, bf16[1,2048,384]{2,1,0:T(8,128)(2,1)}, u32[]{:S(2)}) %copy-start) | copy-done | bytes 1572888
  31.7 3.3 %shard_map.95 = (f32[384,384]{1,0:T(8,128)S(1)}, bf16[384,384]{1,0:T(8,128)(2,1)S(1)}, f32[384,384]{1,0:T(8,128)S(1)}, f32[384,384]{1,0:T(8,128)S(1)}) custom-call(s32[3]{0:T(128)S(1)} %pad_add_fusion.sc, bf16[96,1024]{1,0:T(8,128)(2,1)S(1)} %get-tuple-element.38.refs_0_, bf16[96,1024]{1,0:T(8,128)(2,1)S(1)} %collective-permute-done.14.refs_1_, ...), custom_call_target="tpu_custom_call" | custom-call | tf_op jit(solution)/shard_map/pallas_call | solution.py:26
  35.0 1.8 %shard_map.102 = bf16[512,384]{1,0:T(8,128)(2,1)} custom-call(s32[3]{0:T(128)S(1)} %pad_add_fusion.sc, bf16[96,512]{1,0:T(8,128)(2,1)S(1)} %get-tuple-element.30.refs_0_, bf16[96,512]{1,0:T(8,128)(2,1)S(1)} %collective-permute-done.refs_1_, bf16[96,512]{1,0:T(8,128)(2,1)S(1)} %collective-permute-done.1.refs_2_, ...), custom_call_target="tpu_custom_call" | custom-call | tf_op jit(solution)/shard_map/pallas_call | solution.py:26
  36.8 1.8 %collective-permute-start.27 = (bf16[512,384]{1,0:T(8,128)(2,1)}, bf16[512,384]{1,0:T(8,128)(2,1)}, u32[]{:S(2)}, u32[]{:S(2)}) collective-permute-start(bf16[512,384]{1,0:T(8,128)(2,1)} %shard_map.102), channel_id=1, source_target_pairs={{0,8},{8,0},{16,24},{24,16},{1,9},{9,1},{17,25},{25,17},{2,10},{10... | collective-permute-start | bytes 1179656 | tf_op jit(solution)/shard_map/ppermute | solution.py:223
  40.6 5.2 %shard_map.96 = (bf16[384,1024]{1,0:T(8,128)(2,1)S(1)}, bf16[384,1152]{1,0:T(8,128)(2,1)}, f32[384,128]{1,0:T(8,128)S(1)}) custom-call(s32[3]{0:T(128)S(1)} %pad_add_fusion.sc, bf16[96,512]{1,0:T(8,128)(2,1)S(1)} %get-tuple-element.30.refs_0_, bf16[96,512]{1,0:T(8,128)(2,1)S(1)} %collective-permute-done.refs_1_, ...), custom_call_target="tpu_custom_call" | custom-call | tf_op jit(solution)/shard_map/pallas_call | solution.py:26
  45.7 0.9 %copy-done.1 = bf16[384,1024]{1,0:T(8,128)(2,1)} copy-done((bf16[384,1024]{1,0:T(8,128)(2,1)}, bf16[384,1024]{1,0:T(8,128)(2,1)S(1)}, u32[]{:S(2)}) %copy-start.1) | copy-done | bytes 786456
  47.7 1.7 %shard_map.100 = bf16[512,384]{1,0:T(8,128)(2,1)} custom-call(s32[3]{0:T(128)S(1)} %pad_add_fusion.sc, bf16[96,512]{1,0:T(8,128)(2,1)S(1)} %get-tuple-element.34.refs_8_.refs_0_, bf16[96,512]{1,0:T(8,128)(2,1)S(1)} %collective-permute-done.7.refs_9_.refs_1_, bf16[96,512]{1,0:T(8,128)(2,1)S(1)} %collective-permute-done.8.refs_10_.refs_2_, ...), custom_call_target="tpu_custom_call" | custom-call | tf_op jit(solution)/shard_map/pallas_call | solution.py:26
  49.4 2.9 %collective-permute-start.26 = (bf16[512,384]{1,0:T(8,128)(2,1)}, bf16[512,384]{1,0:T(8,128)(2,1)}, u32[]{:S(2)}, u32[]{:S(2)}) collective-permute-start(bf16[512,384]{1,0:T(8,128)(2,1)} %shard_map.100), channel_id=1, source_target_pairs={{0,8},{24,16},{1,9},{25,17},{2,10},{26,18},{3,11},{27,19},{4,12},{... | collective-permute-start | bytes 1179656 | tf_op jit(solution)/shard_map/ppermute | solution.py:228
  52.3 1.4 %collective-permute-start.25 = (bf16[512,384]{1,0:T(8,128)(2,1)}, bf16[512,384]{1,0:T(8,128)(2,1)}, u32[]{:S(2)}, u32[]{:S(2)}) collective-permute-start(bf16[512,384]{1,0:T(8,128)(2,1)} %shard_map.100), channel_id=1, source_target_pairs={{8,16},{16,8},{9,17},{17,9},{10,18},{18,10},{11,19},{19,11},{12,20... | collective-permute-start | bytes 1179656 | tf_op jit(solution)/shard_map/ppermute | solution.py:227
  53.7 1.0 %shard_map.99 = f32[512,384]{1,0:T(8,128)S(1)} custom-call(s32[3]{0:T(128)S(1)} %pad_add_fusion.sc, bf16[96,512]{1,0:T(8,128)(2,1)S(1)} %get-tuple-element.34.refs_8_.refs_0_, bf16[96,512]{1,0:T(8,128)(2,1)S(1)} %collective-permute-done.7.refs_9_.refs_1_, bf16[96,512]{1,0:T(8,128)(2,1)S(1)} %collective-permute-done.8.refs_10_.refs_2_, ...), custom_call_target="tpu_custom_call" | custom-call | tf_op jit(solution)/shard_map/pallas_call | solution.py:26
  54.7 1.0 %shard_map.101 = f32[512,384]{1,0:T(8,128)S(1)} custom-call(s32[3]{0:T(128)S(1)} %pad_add_fusion.sc, bf16[96,512]{1,0:T(8,128)(2,1)S(1)} %get-tuple-element.30.refs_0_, bf16[96,512]{1,0:T(8,128)(2,1)S(1)} %collective-permute-done.refs_1_, bf16[96,512]{1,0:T(8,128)(2,1)S(1)} %collective-permute-done.1.refs_2_, ...), custom_call_target="tpu_custom_call" | custom-call | tf_op jit(solution)/shard_map/pallas_call | solution.py:26
  55.8 1.9 %select_convert_fusion = bf16[512,384]{1,0:T(8,128)(2,1)} fusion(f32[512,384]{1,0:T(8,128)S(1)} %shard_map.99, f32[512,384]{1,0:T(8,128)S(1)} %shard_map.101, bf16[512,384]{1,0:T(8,128)(2,1)} %collective-permute-done.27, pred[]{:T(512)S(6)} %or.3), kind=kLoop, calls=%fused_computation.1 | loop fusion | flops 589824 | bytes 2359297 | tf_op jit(solution)/shard_map/convert_element_type | solution.py:230
  57.7 1.5 %collective-permute-start.28 = (bf16[512,384]{1,0:T(8,128)(2,1)}, bf16[512,384]{1,0:T(8,128)(2,1)}, u32[]{:S(2)}, u32[]{:S(2)}) collective-permute-start(bf16[512,384]{1,0:T(8,128)(2,1)} %select_convert_fusion), channel_id=1, source_target_pairs={{0,16},{16,0},{8,24},{24,8},{1,17},{17,1},{9,25},{25,9},{2,18},{18... | collective-permute-start | bytes 1179656 | tf_op jit(solution)/shard_map/ppermute | solution.py:231
  59.4 0.9 %copy-done.6 = f32[384,128]{1,0:T(8,128)S(1)} copy-done((f32[384,128]{1,0:T(8,128)S(1)}, f32[384,128]{1,0:T(8,128)}, u32[]{:S(2)}) %copy-start.6) | copy-done | bytes 196632
  60.8 1.5 %collective-permute-start.22 = (bf16[96,1152]{1,0:T(8,128)(2,1)S(1)}, bf16[96,1152]{1,0:T(8,128)(2,1)S(1)}, u32[]{:S(2)}, u32[]{:S(2)}) collective-permute-start(bf16[96,1152]{1,0:T(8,128)(2,1)S(1)} %get-tuple-element.49), channel_id=1, source_target_pairs={{0,2},{2,0},{4,6},{6,4},{1,3},{3,1},{5,7},{7,5},{8,10},{10,8},{12,... | collective-permute-start | bytes 663560 | tf_op jit(solution)/shard_map/ppermute | solution.py:184
  62.3 1.5 %collective-permute-start.23 = (bf16[96,1152]{1,0:T(8,128)(2,1)S(1)}, bf16[96,1152]{1,0:T(8,128)(2,1)S(1)}, u32[]{:S(2)}, u32[]{:S(2)}) collective-permute-start(bf16[96,1152]{1,0:T(8,128)(2,1)S(1)} %get-tuple-element.50), channel_id=1, source_target_pairs={{0,4},{2,6},{4,0},{6,2},{1,5},{3,7},{5,1},{7,3},{8,12},{10,14},{12... | collective-permute-start | bytes 663560 | tf_op jit(solution)/shard_map/ppermute | solution.py:184
  64.4 17.4 %collective-permute-done.28 = bf16[512,384]{1,0:T(8,128)(2,1)} collective-permute-done((bf16[512,384]{1,0:T(8,128)(2,1)}, bf16[512,384]{1,0:T(8,128)(2,1)}, u32[]{:S(2)}, u32[]{:S(2)}) %collective-permute-start.28) | collective-permute-done | bytes 393248 | tf_op jit(solution)/shard_map/ppermute | solution.py:231
  81.8 2.5 %add_bitcast_fusion = f32[1,512,384]{2,1,0:T(8,128)} fusion(bf16[512,384]{1,0:T(8,128)(2,1)} %collective-permute-done.28, bf16[512,384]{1,0:T(8,128)(2,1)} %collective-permute-done.26, f32[512,384]{1,0:T(8,128)S(1)} %shard_map.99, bf16[512,384]{1,0:T(8,128)(2,1)} %collective-permute-done.25, f32[512,384]{1,0:T(8,128)S(1)} %shard_map.101, ...), kind=kLoop, calls=%fused_computation | loop fusion | flops 1769472 | bytes 3932161 | tf_op jit(solution)/shard_map/broadcast_in_dim | solution.py:237
  84.3 1.8 %shard_map.98 = (bf16[128,1024]{1,0:T(8,128)(2,1)}, f32[128,2]{1,0:T(8,128)S(1)}) custom-call(s32[3]{0:T(128)S(1)} %pad_add_fusion.sc, bf16[384,128]{1,0:T(8,128)(2,1)S(1)} %copy-done.8, s32[128,2]{1,0:T(8,128)S(1)} %copy.10.routes_ref, f32[128,2]{1,0:T(8,128)S(1)} %copy.11.probs_ref, bf16[96,1152]{1,0:T(8,128)(2,1)S(1)} %get-tuple-element.48.refs_0_, ...), custom_call_target="tpu_custom_call" | custom-call | tf_op jit(solution)/shard_map/pallas_call | solution.py:26
  (67 shorter events, 8.6 us)
Async XLA Ops:
  5.9 8.0 %collective-permute-start = (bf16[96,512]{1,0:T(8,128)(2,1)S(1)}, bf16[96,512]{1,0:T(8,128)(2,1)S(1)}, u32[]{:S(2)}, u32[]{:S(2)}) collective-permute-start(bf16[96,512]{1,0:T(8,128)(2,1)S(1)} %get-tuple-element.31), channel_id=1, source_target_pairs={{0,2},{2,0},{4,6},{6,4},{1,3},{3,1},{5,7},{7,5},{8,10},{10,8},{12,... | collective-permute-start | bytes 294920 | tf_op jit(solution)/shard_map/ppermute | solution.py:184
  8.8 15.3 %collective-permute-start.14 = (bf16[96,1024]{1,0:T(8,128)(2,1)S(1)}, bf16[96,1024]{1,0:T(8,128)(2,1)S(1)}, u32[]{:S(2)}, u32[]{:S(2)}) collective-permute-start(bf16[96,1024]{1,0:T(8,128)(2,1)S(1)} %get-tuple-element.39), channel_id=1, source_target_pairs={{0,2},{2,0},{4,6},{6,4},{1,3},{3,1},{5,7},{7,5},{8,10},{10,8},{12,... | collective-permute-start | bytes 589832 | tf_op jit(solution)/shard_map/ppermute | solution.py:184
  8.9 15.4 %collective-permute-start.15 = (bf16[96,1024]{1,0:T(8,128)(2,1)S(1)}, bf16[96,1024]{1,0:T(8,128)(2,1)S(1)}, u32[]{:S(2)}, u32[]{:S(2)}) collective-permute-start(bf16[96,1024]{1,0:T(8,128)(2,1)S(1)} %get-tuple-element.40), channel_id=1, source_target_pairs={{0,4},{2,6},{4,0},{6,2},{1,5},{3,7},{5,1},{7,3},{8,12},{10,14},{12... | collective-permute-start | bytes 589832 | tf_op jit(solution)/shard_map/ppermute | solution.py:184
  10.9 13.8 %collective-permute-start.16 = (bf16[96,1024]{1,0:T(8,128)(2,1)S(1)}, bf16[96,1024]{1,0:T(8,128)(2,1)S(1)}, u32[]{:S(2)}, u32[]{:S(2)}) collective-permute-start(bf16[96,1024]{1,0:T(8,128)(2,1)S(1)} %get-tuple-element.41), channel_id=1, source_target_pairs={{0,6},{2,4},{4,2},{6,0},{1,7},{3,5},{5,3},{7,1},{8,14},{10,12},{12... | collective-permute-start | bytes 589832 | tf_op jit(solution)/shard_map/ppermute | solution.py:184
  12.3 11.3 %collective-permute-start.1 = (bf16[96,512]{1,0:T(8,128)(2,1)S(1)}, bf16[96,512]{1,0:T(8,128)(2,1)S(1)}, u32[]{:S(2)}, u32[]{:S(2)}) collective-permute-start(bf16[96,512]{1,0:T(8,128)(2,1)S(1)} %get-tuple-element.32), channel_id=1, source_target_pairs={{0,4},{2,6},{4,0},{6,2},{1,5},{3,7},{5,1},{7,3},{8,12},{10,14},{12... | collective-permute-start | bytes 294920 | tf_op jit(solution)/shard_map/ppermute | solution.py:184
  13.8 9.8 %collective-permute-start.2 = (bf16[96,512]{1,0:T(8,128)(2,1)S(1)}, bf16[96,512]{1,0:T(8,128)(2,1)S(1)}, u32[]{:S(2)}, u32[]{:S(2)}) collective-permute-start(bf16[96,512]{1,0:T(8,128)(2,1)S(1)} %get-tuple-element.33), channel_id=1, source_target_pairs={{0,6},{2,4},{4,2},{6,0},{1,7},{3,5},{5,3},{7,1},{8,14},{10,12},{12... | collective-permute-start | bytes 294920 | tf_op jit(solution)/shard_map/ppermute | solution.py:184
  23.6 1.3 %collective-permute-start.3 = (bf16[96,512]{1,0:T(8,128)(2,1)S(1)}, bf16[96,512]{1,0:T(8,128)(2,1)S(1)}, u32[]{:S(2)}, u32[]{:S(2)}) collective-permute-start(bf16[96,512]{1,0:T(8,128)(2,1)S(1)} %get-tuple-element.30.refs_0_), channel_id=1, source_target_pairs={{0,1},{1,0},{2,3},{3,2},{4,5},{5,4},{6,7},{7,6},{8,9},{9,8},{10,11... | collective-permute-start | bytes 294920 | tf_op jit(solution)/shard_map/ppermute | solution.py:180
  23.6 2.9 %collective-permute-start.17 = (bf16[96,1024]{1,0:T(8,128)(2,1)S(1)}, bf16[96,1024]{1,0:T(8,128)(2,1)S(1)}, u32[]{:S(2)}, u32[]{:S(2)}) collective-permute-start(bf16[96,1024]{1,0:T(8,128)(2,1)S(1)} %get-tuple-element.38.refs_0_), channel_id=1, source_target_pairs={{0,1},{1,0},{2,3},{3,2},{4,5},{5,4},{6,7},{7,6},{8,9},{9,8},{10,11... | collective-permute-start | bytes 589832 | tf_op jit(solution)/shard_map/ppermute | solution.py:180
  24.2 2.7 %collective-permute-start.18 = (bf16[96,1024]{1,0:T(8,128)(2,1)S(1)}, bf16[96,1024]{1,0:T(8,128)(2,1)S(1)}, u32[]{:S(2)}, u32[]{:S(2)}) collective-permute-start(bf16[96,1024]{1,0:T(8,128)(2,1)S(1)} %collective-permute-done.14.refs_1_), channel_id=1, source_target_pairs={{0,1},{1,0},{2,3},{3,2},{4,5},{5,4},{6,7},{7,6},{8,9},{9,8},{10,11... | collective-permute-start | bytes 589832 | tf_op jit(solution)/shard_map/ppermute | solution.py:180
  24.2 4.3 %collective-permute-start.19 = (bf16[96,1024]{1,0:T(8,128)(2,1)S(1)}, bf16[96,1024]{1,0:T(8,128)(2,1)S(1)}, u32[]{:S(2)}, u32[]{:S(2)}) collective-permute-start(bf16[96,1024]{1,0:T(8,128)(2,1)S(1)} %collective-permute-done.15.refs_2_), channel_id=1, source_target_pairs={{0,1},{1,0},{2,3},{3,2},{4,5},{5,4},{6,7},{7,6},{8,9},{9,8},{10,11... | collective-permute-start | bytes 589832 | tf_op jit(solution)/shard_map/ppermute | solution.py:180
  24.7 5.4 %collective-permute-start.20 = (bf16[96,1024]{1,0:T(8,128)(2,1)S(1)}, bf16[96,1024]{1,0:T(8,128)(2,1)S(1)}, u32[]{:S(2)}, u32[]{:S(2)}) collective-permute-start(bf16[96,1024]{1,0:T(8,128)(2,1)S(1)} %collective-permute-done.16.refs_3_), channel_id=1, source_target_pairs={{0,1},{1,0},{2,3},{3,2},{4,5},{5,4},{6,7},{7,6},{8,9},{9,8},{10,11... | collective-permute-start | bytes 589832 | tf_op jit(solution)/shard_map/ppermute | solution.py:180
  24.9 1.4 %collective-permute-start.4 = (bf16[96,512]{1,0:T(8,128)(2,1)S(1)}, bf16[96,512]{1,0:T(8,128)(2,1)S(1)}, u32[]{:S(2)}, u32[]{:S(2)}) collective-permute-start(bf16[96,512]{1,0:T(8,128)(2,1)S(1)} %collective-permute-done.refs_1_), channel_id=1, source_target_pairs={{0,1},{1,0},{2,3},{3,2},{4,5},{5,4},{6,7},{7,6},{8,9},{9,8},{10,11... | collective-permute-start | bytes 294920 | tf_op jit(solution)/shard_map/ppermute | solution.py:180
  26.3 8.7 %collective-permute-start.5 = (bf16[96,512]{1,0:T(8,128)(2,1)S(1)}, bf16[96,512]{1,0:T(8,128)(2,1)S(1)}, u32[]{:S(2)}, u32[]{:S(2)}) collective-permute-start(bf16[96,512]{1,0:T(8,128)(2,1)S(1)} %collective-permute-done.1.refs_2_), channel_id=1, source_target_pairs={{0,1},{1,0},{2,3},{3,2},{4,5},{5,4},{6,7},{7,6},{8,9},{9,8},{10,11... | collective-permute-start | bytes 294920 | tf_op jit(solution)/shard_map/ppermute | solution.py:180
  26.6 8.4 %collective-permute-start.6 = (bf16[96,512]{1,0:T(8,128)(2,1)S(1)}, bf16[96,512]{1,0:T(8,128)(2,1)S(1)}, u32[]{:S(2)}, u32[]{:S(2)}) collective-permute-start(bf16[96,512]{1,0:T(8,128)(2,1)S(1)} %collective-permute-done.2.refs_3_), channel_id=1, source_target_pairs={{0,1},{1,0},{2,3},{3,2},{4,5},{5,4},{6,7},{7,6},{8,9},{9,8},{10,11... | collective-permute-start | bytes 294920 | tf_op jit(solution)/shard_map/ppermute | solution.py:180
  26.8 11.8 %collective-permute-start.7 = (bf16[96,512]{1,0:T(8,128)(2,1)S(1)}, bf16[96,512]{1,0:T(8,128)(2,1)S(1)}, u32[]{:S(2)}, u32[]{:S(2)}) collective-permute-start(bf16[96,512]{1,0:T(8,128)(2,1)S(1)} %get-tuple-element.35), channel_id=1, source_target_pairs={{0,2},{2,0},{4,6},{6,4},{1,3},{3,1},{5,7},{7,5},{8,10},{10,8},{12,... | collective-permute-start | bytes 294920 | tf_op jit(solution)/shard_map/ppermute | solution.py:184
  28.5 10.6 %collective-permute-start.8 = (bf16[96,512]{1,0:T(8,128)(2,1)S(1)}, bf16[96,512]{1,0:T(8,128)(2,1)S(1)}, u32[]{:S(2)}, u32[]{:S(2)}) collective-permute-start(bf16[96,512]{1,0:T(8,128)(2,1)S(1)} %get-tuple-element.36), channel_id=1, source_target_pairs={{0,4},{2,6},{4,0},{6,2},{1,5},{3,7},{5,1},{7,3},{8,12},{10,14},{12... | collective-permute-start | bytes 294920 | tf_op jit(solution)/shard_map/ppermute | solution.py:184
  30.1 9.1 %collective-permute-start.9 = (bf16[96,512]{1,0:T(8,128)(2,1)S(1)}, bf16[96,512]{1,0:T(8,128)(2,1)S(1)}, u32[]{:S(2)}, u32[]{:S(2)}) collective-permute-start(bf16[96,512]{1,0:T(8,128)(2,1)S(1)} %get-tuple-element.37), channel_id=1, source_target_pairs={{0,6},{2,4},{4,2},{6,0},{1,7},{3,5},{5,3},{7,1},{8,14},{10,12},{12... | collective-permute-start | bytes 294920 | tf_op jit(solution)/shard_map/ppermute | solution.py:184
  36.8 19.0 %collective-permute-start.27 = (bf16[512,384]{1,0:T(8,128)(2,1)}, bf16[512,384]{1,0:T(8,128)(2,1)}, u32[]{:S(2)}, u32[]{:S(2)}) collective-permute-start(bf16[512,384]{1,0:T(8,128)(2,1)} %shard_map.102), channel_id=1, source_target_pairs={{0,8},{8,0},{16,24},{24,16},{1,9},{9,1},{17,25},{25,17},{2,10},{10... | collective-permute-start | bytes 1179656 | tf_op jit(solution)/shard_map/ppermute | solution.py:223
  38.6 1.3 %collective-permute-start.10 = (bf16[96,512]{1,0:T(8,128)(2,1)S(1)}, bf16[96,512]{1,0:T(8,128)(2,1)S(1)}, u32[]{:S(2)}, u32[]{:S(2)}) collective-permute-start(bf16[96,512]{1,0:T(8,128)(2,1)S(1)} %get-tuple-element.34.refs_8_.refs_0_), channel_id=1, source_target_pairs={{0,1},{1,0},{2,3},{3,2},{4,5},{5,4},{6,7},{7,6},{8,9},{9,8},{10,11... | collective-permute-start | bytes 294920 | tf_op jit(solution)/shard_map/ppermute | solution.py:180
  38.6 1.5 %collective-permute-start.11 = (bf16[96,512]{1,0:T(8,128)(2,1)S(1)}, bf16[96,512]{1,0:T(8,128)(2,1)S(1)}, u32[]{:S(2)}, u32[]{:S(2)}) collective-permute-start(bf16[96,512]{1,0:T(8,128)(2,1)S(1)} %collective-permute-done.7.refs_9_.refs_1_), channel_id=1, source_target_pairs={{0,1},{1,0},{2,3},{3,2},{4,5},{5,4},{6,7},{7,6},{8,9},{9,8},{10,11... | collective-permute-start | bytes 294920 | tf_op jit(solution)/shard_map/ppermute | solution.py:180
  39.1 1.3 %collective-permute-start.12 = (bf16[96,512]{1,0:T(8,128)(2,1)S(1)}, bf16[96,512]{1,0:T(8,128)(2,1)S(1)}, u32[]{:S(2)}, u32[]{:S(2)}) collective-permute-start(bf16[96,512]{1,0:T(8,128)(2,1)S(1)} %collective-permute-done.8.refs_10_.refs_2_), channel_id=1, source_target_pairs={{0,1},{1,0},{2,3},{3,2},{4,5},{5,4},{6,7},{7,6},{8,9},{9,8},{10,11... | collective-permute-start | bytes 294920 | tf_op jit(solution)/shard_map/ppermute | solution.py:180
  39.2 1.4 %collective-permute-start.13 = (bf16[96,512]{1,0:T(8,128)(2,1)S(1)}, bf16[96,512]{1,0:T(8,128)(2,1)S(1)}, u32[]{:S(2)}, u32[]{:S(2)}) collective-permute-start(bf16[96,512]{1,0:T(8,128)(2,1)S(1)} %collective-permute-done.9.refs_11_.refs_3_), channel_id=1, source_target_pairs={{0,1},{1,0},{2,3},{3,2},{4,5},{5,4},{6,7},{7,6},{8,9},{9,8},{10,11... | collective-permute-start | bytes 294920 | tf_op jit(solution)/shard_map/ppermute | solution.py:180
  47.3 12.1 %collective-permute-start.21 = (bf16[384,1152]{1,0:T(8,128)(2,1)}, bf16[384,1152]{1,0:T(8,128)(2,1)S(1)}, u32[]{:S(2)}, u32[]{:S(2)}) collective-permute-start(bf16[384,1152]{1,0:T(8,128)(2,1)} %get-tuple-element.47), channel_id=1, source_target_pairs={{0,1},{1,0},{2,3},{3,2},{4,5},{5,4},{6,7},{7,6},{8,9},{9,8},{10,11... | collective-permute-start | bytes 2654216 | tf_op jit(solution)/shard_map/ppermute | solution.py:180
  49.4 14.5 %collective-permute-start.26 = (bf16[512,384]{1,0:T(8,128)(2,1)}, bf16[512,384]{1,0:T(8,128)(2,1)}, u32[]{:S(2)}, u32[]{:S(2)}) collective-permute-start(bf16[512,384]{1,0:T(8,128)(2,1)} %shard_map.100), channel_id=1, source_target_pairs={{0,8},{24,16},{1,9},{25,17},{2,10},{26,18},{3,11},{27,19},{4,12},{... | collective-permute-start | bytes 1179656 | tf_op jit(solution)/shard_map/ppermute | solution.py:228
  52.3 12.0 %collective-permute-start.25 = (bf16[512,384]{1,0:T(8,128)(2,1)}, bf16[512,384]{1,0:T(8,128)(2,1)}, u32[]{:S(2)}, u32[]{:S(2)}) collective-permute-start(bf16[512,384]{1,0:T(8,128)(2,1)} %shard_map.100), channel_id=1, source_target_pairs={{8,16},{16,8},{9,17},{17,9},{10,18},{18,10},{11,19},{19,11},{12,20... | collective-permute-start | bytes 1179656 | tf_op jit(solution)/shard_map/ppermute | solution.py:227
  55.8 3.5 %copy-start.12 = (f32[128,2]{0,1:T(2,128)S(1)}, f32[128,2]{0,1:T(2,128)}, u32[]{:S(2)}) copy-start(f32[128,2]{0,1:T(2,128)} %param.10) | copy-start | bytes 3076
  55.8 3.7 %copy-start.2 = (bf16[384,1024]{1,0:T(8,128)(2,1)S(1)}, bf16[384,1024]{1,0:T(8,128)(2,1)}, u32[]{:S(2)}) copy-start(bf16[384,1024]{1,0:T(8,128)(2,1)} %copy-done.1) | copy-start | bytes 2359300
  57.7 24.1 %collective-permute-start.28 = (bf16[512,384]{1,0:T(8,128)(2,1)}, bf16[512,384]{1,0:T(8,128)(2,1)}, u32[]{:S(2)}, u32[]{:S(2)}) collective-permute-start(bf16[512,384]{1,0:T(8,128)(2,1)} %select_convert_fusion), channel_id=1, source_target_pairs={{0,16},{16,0},{8,24},{24,8},{1,17},{17,1},{9,25},{25,9},{2,18},{18... | collective-permute-start | bytes 1179656 | tf_op jit(solution)/shard_map/ppermute | solution.py:231
  60.8 23.5 %collective-permute-start.22 = (bf16[96,1152]{1,0:T(8,128)(2,1)S(1)}, bf16[96,1152]{1,0:T(8,128)(2,1)S(1)}, u32[]{:S(2)}, u32[]{:S(2)}) collective-permute-start(bf16[96,1152]{1,0:T(8,128)(2,1)S(1)} %get-tuple-element.49), channel_id=1, source_target_pairs={{0,2},{2,0},{4,6},{6,4},{1,3},{3,1},{5,7},{7,5},{8,10},{10,8},{12,... | collective-permute-start | bytes 663560 | tf_op jit(solution)/shard_map/ppermute | solution.py:184
  62.3 21.9 %collective-permute-start.23 = (bf16[96,1152]{1,0:T(8,128)(2,1)S(1)}, bf16[96,1152]{1,0:T(8,128)(2,1)S(1)}, u32[]{:S(2)}, u32[]{:S(2)}) collective-permute-start(bf16[96,1152]{1,0:T(8,128)(2,1)S(1)} %get-tuple-element.50), channel_id=1, source_target_pairs={{0,4},{2,6},{4,0},{6,2},{1,5},{3,7},{5,1},{7,3},{8,12},{10,14},{12... | collective-permute-start | bytes 663560 | tf_op jit(solution)/shard_map/ppermute | solution.py:184
  63.9 20.4 %copy-start.8 = (bf16[384,128]{1,0:T(8,128)(2,1)S(1)}, bf16[384,128]{1,0:T(8,128)(2,1)}, u32[]{:S(2)}) copy-start(bf16[384,128]{1,0:T(8,128)(2,1)} %copy-done.7) | copy-start | bytes 294916
  63.9 20.4 %collective-permute-start.24 = (bf16[96,1152]{1,0:T(8,128)(2,1)S(1)}, bf16[96,1152]{1,0:T(8,128)(2,1)S(1)}, u32[]{:S(2)}, u32[]{:S(2)}) collective-permute-start(bf16[96,1152]{1,0:T(8,128)(2,1)S(1)} %get-tuple-element.51), channel_id=1, source_target_pairs={{0,6},{2,4},{4,2},{6,0},{1,7},{3,5},{5,3},{7,1},{8,14},{10,12},{12... | collective-permute-start | bytes 663560 | tf_op jit(solution)/shard_map/ppermute | solution.py:184
  (10 other events, 11.3 us)

commit v2 on v1

v2 whole, which is shorter than its diff:
```python
import functools

import jax
import jax.numpy as jnp
from jax import lax
from jax.experimental import pallas as pl
from jax.experimental.pallas import tpu as pltpu
from jax.sharding import PartitionSpec as P

F32 = jnp.float32
BF16 = jnp.bfloat16
NT = (((1,), (1,)), ((), ()))
TN = (((0,), (0,)), ((), ()))
VMEM_LIMIT = 20 * 1024 * 1024
PACK_VMEM = 60 * 1024 * 1024


def dot(a, b, dims=(((1,), (0,)), ((), ()))):
    return lax.dot_general(a, b, dims, preferred_element_type=F32)


def call(body, out_shape, operands, scalars=None, after=(), hbm=(), scratch=(), vmem=VMEM_LIMIT):
    vm = pl.BlockSpec(memory_space=pltpu.VMEM)
    lead = 0 if scalars is None else 1
    specs = [pl.BlockSpec(memory_space=pltpu.SMEM)] * lead
    specs += [pl.BlockSpec(memory_space=pl.ANY)] * len(after)
    specs += [pl.BlockSpec(memory_space=pltpu.HBM) if i in hbm else vm for i in range(len(operands))]

    def run(*refs):
        body(*refs[:lead], *refs[lead + len(after):])

    return pl.pallas_call(
        run,
        out_shape=out_shape,
        in_specs=specs,
        out_specs=jax.tree.map(lambda _: vm, out_shape),
        scratch_shapes=list(scratch),
        compiler_params=pltpu.CompilerParams(vmem_limit_bytes=vmem),
    )(*([] if scalars is None else [scalars]), *after, *operands)


def struct(shape, dtype):
    return jax.ShapeDtypeStruct(shape, dtype)


def slot_rows(experts, me, routes_ref, probs_ref):
    fanout, count = routes_ref.shape
    routes = routes_ref[...]
    probs = probs_ref[...]
    row = lax.broadcasted_iota(jnp.int32, (8, count), 0)
    hits = jnp.zeros((8, count), F32)
    weights = jnp.zeros((8, count), F32)
    for k in range(fanout):
        same = routes[k:k + 1, :] == (row ^ me)
        hits = hits + jnp.where(same, 1.0, 0.0)
        weights = weights + jnp.where(same, probs[k:k + 1, :], 0.0)
    earlier = lax.broadcasted_iota(jnp.int32, (count, count), 0) < lax.broadcasted_iota(jnp.int32, (count, count), 1)
    before = dot(hits.astype(BF16), jnp.where(earlier, 1.0, 0.0).astype(BF16)).astype(jnp.int32)
    return hits, before, weights


def picks(experts, cap, me, routes_ref, probs_ref):
    hits, before, weights = slot_rows(experts, me, routes_ref, probs_ref)
    slot = lax.broadcasted_iota(jnp.int32, (cap, hits.shape[1]), 0)
    found = []
    for m in range(experts):
        chosen = (slot == before[m:m + 1, :]) & (hits[m:m + 1, :] > 0.5)
        pick = jnp.where(chosen, 1.0, 0.0)
        found.append((pick.astype(BF16), jnp.sum(pick * weights[m:m + 1, :], axis=1, keepdims=True)))
    return found


def pack_body(experts, cap, sc, routes_hbm, probs_hbm, tok_hbm, dy_hbm, *rest):
    x_out, dy_out = rest[:experts], rest[experts:2 * experts]
    routes_ref, probs_ref, tok_ref, dy_ref, sems = rest[2 * experts:]
    copies = [
        pltpu.make_async_copy(source, target, sems.at[i])
        for i, (source, target) in enumerate(
            [(routes_hbm, routes_ref), (probs_hbm, probs_ref), (tok_hbm, tok_ref), (dy_hbm, dy_ref)]
        )
    ]
    for copy in copies:
        copy.start()
    copies[0].wait()
    copies[1].wait()
    found = picks(experts, cap, sc[0], routes_ref, probs_ref)
    copies[2].wait()
    tok = tok_ref[...]
    for m, (pick, _) in enumerate(found):
        x_out[m][...] = dot(pick, tok).astype(BF16)
    copies[3].wait()
    dy = dy_ref[...]
    for m, (pick, p_col) in enumerate(found):
        dy_out[m][...] = (p_col * dot(pick, dy)).astype(BF16)


def stack_body(count, *refs):
    blocks, outs = refs[:count], refs[count:]
    cap = blocks[0].shape[0]
    for m, ref in enumerate(blocks):
        rows = slice(m * cap, (m + 1) * cap)
        low = 0
        for out in outs:
            out[rows, :] = ref[:, low:low + out.shape[1]]
            low += out.shape[1]


def forward_body(sc, own, oth, gw, uw, hid_ref, hid_b_ref, dgate_ref, act_ref):
    pair = sc[1]
    half = own.shape[1]
    mine = pl.ds(pl.multiple_of(pair * half, half), half)
    other = pl.ds(pl.multiple_of((1 - pair) * half, half), half)
    gate = dot(own[...], gw[mine, :]) + dot(oth[...], gw[other, :])
    up = dot(own[...], uw[mine, :]) + dot(oth[...], uw[other, :])
    sig = jax.nn.sigmoid(gate)
    act = gate * sig
    hid = act * up
    hid_ref[...] = hid
    hid_b_ref[...] = hid.astype(BF16)
    dgate_ref[...] = up * sig * (1.0 + gate * (1.0 - sig))
    act_ref[...] = act


def weight_body(sc, own, oth, hid_b, first, second, third, fourth):
    group, pair = sc[2], sc[1]
    quarter = own.shape[1] // 2
    odd = group % 2
    hid = hid_b[...]

    def block(out, mine, index):
        columns = pl.ds(pl.multiple_of(index * quarter, quarter), quarter)

        @pl.when(mine)
        def _():
            out[...] = dot(own[:, columns], hid, TN).astype(out.dtype)

        @pl.when(jnp.logical_not(mine))
        def _():
            out[...] = dot(oth[:, columns], hid, TN).astype(out.dtype)

    same = pair == odd
    differ = jnp.logical_not(same)
    block(first, differ, 1 - odd)
    block(second, same, 1 - odd)
    block(third, same, odd)
    block(fourth, differ, odd)


def onward_body(sc, third, fourth, near, out):
    inner = (sc[2] == 1) | (sc[2] == 2)

    @pl.when(inner)
    def _():
        out[...] = (third[...] + near[...].astype(F32)).astype(BF16)

    @pl.when(jnp.logical_not(inner))
    def _():
        out[...] = fourth[...].astype(BF16)


def partial_body(sc, third, fourth, near, end, mid, out):
    inner = (sc[2] == 1) | (sc[2] == 2)

    @pl.when(inner)
    def _():
        out[...] = fourth[...] + mid[...].astype(F32) + end[...].astype(F32)

    @pl.when(jnp.logical_not(inner))
    def _():
        out[...] = third[...] + near[...].astype(F32)


def total_body(part, far, out):
    out[...] = part[...] + far[...].astype(F32)


def backward_body(sc, own, oth, dw, gw, uw, hid_ref, dgate_ref, act_ref, send_ref, grads_ref):
    pair = sc[1]
    units = hid_ref.shape[1]
    half = own.shape[1]
    mine = pl.ds(pl.multiple_of(pair * half, half), half)
    other = pl.ds(pl.multiple_of((1 - pair) * half, half), half)
    back = dot(own[...], dw[:, mine], NT) + dot(oth[...], dw[:, other], NT)
    g_gate = (back * dgate_ref[...]).astype(BF16)
    g_up = (back * act_ref[...]).astype(BF16)
    grads_ref[:, :units] = g_gate
    grads_ref[:, units:2 * units] = g_up
    tail = split_columns(jnp.sum(back * hid_ref[...], axis=1, keepdims=True))
    grads_ref[:, 2 * units:] = tail
    send_ref[:, :half] = (dot(g_gate, gw[other, :], NT) + dot(g_up, uw[other, :], NT)).astype(BF16)
    send_ref[:, half:] = tail


def keep_body(sc, grads_ref, gw, uw, keep_ref):
    units = gw.shape[1]
    half = keep_ref.shape[1] - 128
    mine = pl.ds(pl.multiple_of(sc[1] * half, half), half)
    product = dot(grads_ref[:, :units], gw[mine, :], NT) + dot(grads_ref[:, units:2 * units], uw[mine, :], NT)
    keep_ref[:, :half] = product.astype(BF16)
    keep_ref[:, half:] = grads_ref[:, 2 * units:]


def split_columns(q):
    high = q.astype(BF16)
    low = (q - high.astype(F32)).astype(BF16)
    lane = lax.broadcasted_iota(jnp.int32, (q.shape[0], 128), 1)
    return jnp.where(lane == 0, high.astype(F32), jnp.where(lane == 1, low.astype(F32), 0.0)).astype(BF16)


def merge_body(experts, keep_ref, recv_ref, *outs):
    cap, wide = outs[0].shape
    half = wide - 128
    for m in range(experts):
        rows = slice(m * cap, (m + 1) * cap)
        outs[m][:, :half] = (keep_ref[rows, :half].astype(F32) + recv_ref[rows, :half].astype(F32)).astype(BF16)
        tail = keep_ref[rows, half:].astype(F32) + recv_ref[rows, half:].astype(F32)
        outs[m][:, half:] = split_columns(tail[:, 0:1] + tail[:, 1:2])


def combine_body(experts, cap, sc, routes_ref, probs_ref, *refs):
    parts, (out, gp_out) = refs[:experts], refs[experts:]
    half = out.shape[1]
    fanout = routes_ref.shape[0]
    found = picks(experts, cap, sc[0], routes_ref, probs_ref)
    total = None
    gp = [jnp.zeros((1, out.shape[0]), F32) for _ in range(fanout)]
    for m, (pick, _) in enumerate(found):
        rows = dot(pick, parts[m][:, :half], TN)
        total = rows if total is None else total + rows
        tail = dot(parts[m][:, half:], pick, TN)
        q = tail[0:1, :] + tail[1:2, :]
        for k in range(fanout):
            gp[k] = gp[k] + jnp.where(routes_ref[k:k + 1, :] == (sc[0] ^ m), q, 0.0)
    out[...] = total.astype(BF16)
    for k in range(fanout):
        gp_out[k:k + 1, :] = gp[k] / probs_ref[k:k + 1, :]


def on_device(tokens, grad_out, routes, gate_probs, gate_weight, up_weight, down_weight):
    count, half = tokens.shape
    fanout = routes.shape[1]
    experts = lax.axis_size("expert")
    groups = lax.axis_size("dp")
    units = gate_weight.shape[2]
    cap = 3 * count * fanout // (2 * experts)
    slots = experts * cap
    quarter = half // 2
    gw, uw, dw = gate_weight[0], up_weight[0], down_weight[0]
    me, pair, group = lax.axis_index("expert"), lax.axis_index("pair"), lax.axis_index("dp")
    scalars = jnp.stack([me, pair, group]).astype(jnp.int32)

    def swap(value):
        return lax.ppermute(value, "pair", [(0, 1), (1, 0)])

    def cross(values):
        return [values[0]] + [
            lax.ppermute(values[m], "expert", [(i, i ^ m) for i in range(experts)]) for m in range(1, experts)
        ]

    row_args = [routes.T, gate_probs.T]
    packed = call(
        functools.partial(pack_body, experts, cap),
        [struct((cap, half), BF16)] * (2 * experts),
        [*row_args, tokens, grad_out],
        scalars,
        hbm=(0, 1, 2, 3),
        scratch=(
            pltpu.VMEM((fanout, count), jnp.int32),
            pltpu.VMEM((fanout, count), F32),
            pltpu.VMEM((count, half), BF16),
            pltpu.VMEM((count, half), BF16),
            pltpu.SemaphoreType.DMA((4,)),
        ),
        vmem=PACK_VMEM,
    )

    def stack(values, after=()):
        return call(functools.partial(stack_body, experts), [struct((slots, half), BF16)], values, after=after)[0]

    x_parts = cross(packed[:experts])
    dy_parts = cross(packed[experts:])
    x_own, x_oth = stack(x_parts), stack([swap(v) for v in x_parts])

    square = struct((slots, units), F32)
    hid, hid_b, dgate, act = call(
        forward_body,
        [square, struct((slots, units), BF16), square, square],
        [x_own, x_oth, gw, uw],
        scalars,
    )
    dy_own, dy_oth = stack(dy_parts, [hid_b]), stack([swap(v) for v in dy_parts])

    first, second, third, fourth = call(
        weight_body,
        [struct((quarter, units), BF16)] * 2 + [struct((quarter, units), F32)] * 2,
        [dy_own, dy_oth, hid_b],
        scalars,
    )
    if groups == 4:
        from_near = lax.ppermute(first, "dp", [(0, 1), (1, 0), (2, 3), (3, 2)])
        from_end = lax.ppermute(second, "dp", [(0, 1), (3, 2)])
        from_mid = lax.ppermute(second, "dp", [(1, 2), (2, 1)])
        block = struct((quarter, units), F32)
        onward = call(onward_body, struct((quarter, units), BF16), [third, fourth, from_near], scalars)
        from_far = lax.ppermute(onward, "dp", [(0, 2), (2, 0), (1, 3), (3, 1)])
        part = call(partial_body, block, [third, fourth, from_near, from_end, from_mid], scalars)
    else:
        odd = group % 2 == 1
        first, second = first.astype(F32), second.astype(F32)
        whole = jnp.concatenate(
            [
                jnp.where(odd, first, third),
                jnp.where(odd, fourth, second),
                jnp.where(odd, second, fourth),
                jnp.where(odd, third, first),
            ],
            axis=0,
        )
        grad_down = lax.psum_scatter(whole[None], "dp", scatter_dimension=1, tiled=True)

    send, grads = call(
        backward_body,
        [struct((slots, half + 128), BF16), struct((slots, 2 * units + 128), BF16)],
        [dy_own, dy_oth, dw, gw, uw, hid, dgate, act],
        scalars,
        after=[second] if groups == 4 else [],
    )
    received = swap(send)
    keep = call(keep_body, struct((slots, half + 128), BF16), [grads, gw, uw], scalars)
    merged = call(functools.partial(merge_body, experts), [struct((cap, half + 128), BF16)] * experts, [keep, received])
    returned = cross(merged)
    grad_input, grad_probs = call(
        functools.partial(combine_body, experts, cap),
        [struct((count, half), BF16), struct((fanout, count), F32)],
        [*row_args, *returned],
        scalars,
    )

    if groups == 4:
        grad_down = call(total_body, block, [part, from_far], after=[grad_input])[None]

    return grad_input, grad_probs.T, grad_down


def solution(mesh):
    return jax.shard_map(
        on_device,
        mesh=mesh,
        in_specs=(
            P(("dp", "expert"), "pair"),
            P(("dp", "expert"), "pair"),
            P(("dp", "expert"), None),
            P(("dp", "expert"), None),
            P("expert", None, "pair"),
            P("expert", None, "pair"),
            P("expert", "pair", None),
        ),
        out_specs=(
            P(("dp", "expert"), "pair"),
            P(("dp", "expert"), None),
            P("expert", "dp", "pair"),
        ),
        check_vma=False,
    )
```

time: 87.1 us -> 70.8 us (0.81)
  local copies, waits for them, and re-layouts: 8.67 us -> 1.91 us
  waiting for transfers between devices: 27.9 us -> 21.9 us
  other arithmetic: 4.45 us -> 0.62 us
  starting transfers between devices: 27.5 us -> 28.8 us
  Pallas kernels: 17.4 us -> 16.5 us
    ppermute x1, waiting for transfers between devices: 17.4 us -> 1.33 us  [on_device(): from_far = lax.ppermute(onward, 'dp', [(0, 2), (2, 0), (1, 3), (3, 1)])]
    ppermute x12 -> x9, waiting for transfers between devices: 8.21 us -> 18 us  [cross(): lax.ppermute(values[m], 'expert', [(i, i ^ m) for i in range(experts)])]
    unnamed x29 -> x18, local copies, waits for them, and re-layouts: 8.67 us -> 1.91 us
    ppermute x1, starting transfers between devices: 2.93 us -> 6.31 us  [on_device(): from_end = lax.ppermute(second, 'dp', [(0, 1), (3, 2)])]
    ppermute x1, waiting for transfers between devices: 0.01 us -> 2.53 us  [on_device(): from_near = lax.ppermute(first, 'dp', [(0, 1), (1, 0), (2, 3), (3, 2)])]
    broadcast_in_dim x1 -> x0, other arithmetic: 2.46 us -> none  [on_device(): grad_down = grad_down[None]]
    ppermute x13 -> x9, waiting for transfers between devices: 2.27 us -> 0.02 us  [swap(): return lax.ppermute(value, 'pair', [(0, 1), (1, 0)])]
    ppermute x1, starting transfers between devices: 1.49 us -> 3.55 us  [on_device(): from_far = lax.ppermute(onward, 'dp', [(0, 2), (2, 0), (1, 3), (3, 1)])]
  transfers between devices with their start and end apart: 29 -> 22, of which waited for: 8 -> 8; matrix products, arithmetic and copies ran while one was open for 5% -> 0% of each run, Pallas kernels for 17% -> 11%
where the time goes in v2:
time: 70.8 us; the launch traced here: 70.6 us
  starting transfers between devices  28.8 us (41%)
  waiting for transfers between devices  21.9 us (31%)
  Pallas kernels  16.5 us (23%)
  local copies, waits for them, and re-layouts  1.91 us (3%)
  between operations  0.89 us (1%)
    ppermute x9, waiting for transfers between devices, cross(): lax.ppermute(values[m], 'expert', [(i, i ^ m) for i in range(experts)])  18 us
    pallas_call x14, Pallas kernels, call(): pl.pallas_call(run, out_shape=out_shape, in_specs=specs, out_specs=jax.tr...  16.5 us
    ppermute x9, starting transfers between devices, cross(): lax.ppermute(values[m], 'expert', [(i, i ^ m) for i in range(experts)])  14.6 us
    ppermute x1, starting transfers between devices, on_device(): from_end = lax.ppermute(second, 'dp', [(0, 1), (3, 2)])  6.31 us
    ppermute x1, starting transfers between devices, on_device(): from_far = lax.ppermute(onward, 'dp', [(0, 2), (2, 0), (1, 3), (3, 1)])  3.55 us
    ppermute x1, waiting for transfers between devices, on_device(): from_near = lax.ppermute(first, 'dp', [(0, 1), (1, 0), (2, 3), (3, 2)])  2.53 us
    ppermute x9, starting transfers between devices, swap(): return lax.ppermute(value, 'pair', [(0, 1), (1, 0)])  2.16 us
    unnamed x18, local copies, waits for them, and re-layouts  1.91 us
  transfers between devices with their start and end apart: 22, of which 8 were waited for; matrix products, arithmetic and copies ran while one was open for 0% of the time, Pallas kernels for 11%

profile of v2, /device:TPU:0, one launch (start us, length us, event | category | flops | bytes accessed | tf_op | source)
XLA Modules:
  0.0 70.6 jit_solution(14143343862191820251)
XLA Ops:
  0.6 0.6 pad_add_fusion.refs_0_
  1.3 3.2 %shard_map.94 = (bf16[96,1024]{1,0:T(8,128)(2,1)}, bf16[96,1024]{1,0:T(8,128)(2,1)}, bf16[96,1024]{1,0:T(8,128)(2,1)}, bf16[96,1024]{1,0:T(8,128)(2,1)}, bf16[96...) custom-call(s32[3]{0:T(128)} %pad_add_fusion.refs_0_, ...), custom_call_target="tpu_custom_call" | custom-call | tf_op jit(solution)/shard_map/pallas_call | solution.py:32
  4.5 3.0 %collective-permute-start = (bf16[96,1024]{1,0:T(8,128)(2,1)}, bf16[96,1024]{1,0:T(8,128)(2,1)S(1)}, u32[]{:S(2)}, u32[]{:S(2)}) collective-permute-start(bf16[96,1024]{1,0:T(8,128)(2,1)} %get-tuple-element.28), channel_id=1, source_target_pairs={{0,2},{2,0},{4,6},{6,4},{1,3},{3,1},{5,7},{7,5},{8,10},{10,8},{12,... | collective-permute-start | bytes 589832 | tf_op jit(solution)/shard_map/ppermute | solution.py:257
  7.5 1.5 %collective-permute-start.1 = (bf16[96,1024]{1,0:T(8,128)(2,1)}, bf16[96,1024]{1,0:T(8,128)(2,1)S(1)}, u32[]{:S(2)}, u32[]{:S(2)}) collective-permute-start(bf16[96,1024]{1,0:T(8,128)(2,1)} %get-tuple-element.29), channel_id=1, source_target_pairs={{0,4},{2,6},{4,0},{6,2},{1,5},{3,7},{5,1},{7,3},{8,12},{10,14},{12... | collective-permute-start | bytes 589832 | tf_op jit(solution)/shard_map/ppermute | solution.py:257
  9.0 1.9 %collective-permute-start.7 = (bf16[96,1024]{1,0:T(8,128)(2,1)}, bf16[96,1024]{1,0:T(8,128)(2,1)S(1)}, u32[]{:S(2)}, u32[]{:S(2)}) collective-permute-start(bf16[96,1024]{1,0:T(8,128)(2,1)} %get-tuple-element.33), channel_id=1, source_target_pairs={{0,2},{2,0},{4,6},{6,4},{1,3},{3,1},{5,7},{7,5},{8,10},{10,8},{12,... | collective-permute-start | bytes 589832 | tf_op jit(solution)/shard_map/ppermute | solution.py:257
  11.0 1.5 %collective-permute-start.8 = (bf16[96,1024]{1,0:T(8,128)(2,1)}, bf16[96,1024]{1,0:T(8,128)(2,1)S(1)}, u32[]{:S(2)}, u32[]{:S(2)}) collective-permute-start(bf16[96,1024]{1,0:T(8,128)(2,1)} %get-tuple-element.34), channel_id=1, source_target_pairs={{0,4},{2,6},{4,0},{6,2},{1,5},{3,7},{5,1},{7,3},{8,12},{10,14},{12... | collective-permute-start | bytes 589832 | tf_op jit(solution)/shard_map/ppermute | solution.py:257
  12.5 0.9 %collective-permute-done.refs_1_ = bf16[96,1024]{1,0:T(8,128)(2,1)S(1)} collective-permute-done((bf16[96,1024]{1,0:T(8,128)(2,1)}, bf16[96,1024]{1,0:T(8,128)(2,1)S(1)}, u32[]{:S(2)}, u32[]{:S(2)}) %collective-permute-start) | collective-permute-done | bytes 196640 | tf_op jit(solution)/shard_map/ppermute | solution.py:257
  13.4 3.0 %collective-permute-start.9 = (bf16[96,1024]{1,0:T(8,128)(2,1)}, bf16[96,1024]{1,0:T(8,128)(2,1)S(1)}, u32[]{:S(2)}, u32[]{:S(2)}) collective-permute-start(bf16[96,1024]{1,0:T(8,128)(2,1)} %get-tuple-element.35), channel_id=1, source_target_pairs={{0,6},{2,4},{4,2},{6,0},{1,7},{3,5},{5,3},{7,1},{8,14},{10,12},{12... | collective-permute-start | bytes 589832 | tf_op jit(solution)/shard_map/ppermute | solution.py:257
  16.4 3.3 %collective-permute-done.1.refs_2_ = bf16[96,1024]{1,0:T(8,128)(2,1)S(1)} collective-permute-done((bf16[96,1024]{1,0:T(8,128)(2,1)}, bf16[96,1024]{1,0:T(8,128)(2,1)S(1)}, u32[]{:S(2)}, u32[]{:S(2)}) %collective-permute-start.1) | collective-permute-done | bytes 196640 | tf_op jit(solution)/shard_map/ppermute | solution.py:257
  20.2 1.6 %collective-permute-done.7.refs_2_ = bf16[96,1024]{1,0:T(8,128)(2,1)S(1)} collective-permute-done((bf16[96,1024]{1,0:T(8,128)(2,1)}, bf16[96,1024]{1,0:T(8,128)(2,1)S(1)}, u32[]{:S(2)}, u32[]{:S(2)}) %collective-permute-start.7) | collective-permute-done | bytes 196640 | tf_op jit(solution)/shard_map/ppermute | solution.py:257
  21.9 4.8 %collective-permute-done.8.refs_3_ = bf16[96,1024]{1,0:T(8,128)(2,1)S(1)} collective-permute-done((bf16[96,1024]{1,0:T(8,128)(2,1)}, bf16[96,1024]{1,0:T(8,128)(2,1)S(1)}, u32[]{:S(2)}, u32[]{:S(2)}) %collective-permute-start.8) | collective-permute-done | bytes 196640 | tf_op jit(solution)/shard_map/ppermute | solution.py:257
  27.9 0.9 %copy-done.5 = bf16[96,1024]{1,0:T(8,128)(2,1)S(1)} copy-done((bf16[96,1024]{1,0:T(8,128)(2,1)S(1)}, bf16[96,1024]{1,0:T(8,128)(2,1)}, u32[]{:S(2)}) %copy-start.5) | copy-done | bytes 196632
  29.0 2.4 %shard_map.97 = (f32[384,384]{1,0:T(8,128)S(1)}, bf16[384,384]{1,0:T(8,128)(2,1)S(1)}, f32[384,384]{1,0:T(8,128)S(1)}, f32[384,384]{1,0:T(8,128)S(1)}) custom-call(s32[3]{0:T(128)S(1)} %copy-done.6, bf16[384,1024]{1,0:T(8,128)(2,1)S(1)} %shard_map.95.refs_1_, bf16[384,1024]{1,0:T(8,128)(2,1)S(1)} %shard_map.96.refs_2_, bf16[2048,384]{1,0:T(8,128)(2,1)S(1)} %bitcast.10, ...), custom_call_target="tpu_custom_call" | custom-call | tf_op jit(solution)/shard_map/pallas_call | solution.py:32
  31.6 2.2 %shard_map.100 = (bf16[512,384]{1,0:T(8,128)(2,1)S(1)}, bf16[512,384]{1,0:T(8,128)(2,1)S(1)}, f32[512,384]{1,0:T(8,128)S(1)}, f32[512,384]{1,0:T(8,128)S(1)}) custom-call(s32[3]{0:T(128)S(1)} %copy-done.6, bf16[384,1024]{1,0:T(8,128)(2,1)S(1)} %shard_map.98.refs_1_.refs_2_, bf16[384,1024]{1,0:T(8,128)(2,1)S(1)} %shard_map.99.refs_2_.refs_3_, ...), custom_call_target="tpu_custom_call" | custom-call | tf_op jit(solution)/shard_map/pallas_call | solution.py:32
  33.8 2.4 %shard_map.101 = (bf16[384,1152]{1,0:T(8,128)(2,1)S(1)}, bf16[384,896]{1,0:T(8,128)(2,1)S(1)}) custom-call(s32[3]{0:T(128)S(1)} %copy-done.6, bf16[512,384]{1,0:T(8,128)(2,1)S(1)} %get-tuple-element.36.refs_1_, bf16[384,1024]{1,0:T(8,128)(2,1)S(1)} %shard_map.98.refs_1_.refs_2_, bf16[384,1024]{1,0:T(8,128)(2,1)S(1)} %shard_map.99.refs_2_.refs_3_, ...), custom_call_target="tpu_custom_call" | custom-call | tf_op jit(solution)/shard_map/pallas_call | solution.py:32
  36.7 1.6 %collective-permute-start.18 = (bf16[512,384]{1,0:T(8,128)(2,1)S(1)}, bf16[512,384]{1,0:T(8,128)(2,1)S(1)}, u32[]{:S(2)}, u32[]{:S(2)}) collective-permute-start(bf16[512,384]{1,0:T(8,128)(2,1)S(1)} %get-tuple-element.50), channel_id=1, source_target_pairs={{0,8},{8,0},{16,24},{24,16},{1,9},{9,1},{17,25},{25,17},{2,10},{10... | collective-permute-start | bytes 1179656 | tf_op jit(solution)/shard_map/ppermute | solution.py:300
  38.3 0.7 collective-permute-start.20
  39.0 6.3 %collective-permute-start.19 = (bf16[512,384]{1,0:T(8,128)(2,1)S(1)}, bf16[512,384]{1,0:T(8,128)(2,1)S(1)}, u32[]{:S(2)}, u32[]{:S(2)}) collective-permute-start(bf16[512,384]{1,0:T(8,128)(2,1)S(1)} %get-tuple-element.36.refs_1_), channel_id=1, source_target_pairs={{0,8},{24,16},{1,9},{25,17},{2,10},{26,18},{3,11},{27,19},{4,12},{... | collective-permute-start | bytes 1179656 | tf_op jit(solution)/shard_map/ppermute | solution.py:301
  45.3 2.5 %collective-permute-done.18.refs_3_ = bf16[512,384]{1,0:T(8,128)(2,1)S(1)} collective-permute-done((bf16[512,384]{1,0:T(8,128)(2,1)S(1)}, bf16[512,384]{1,0:T(8,128)(2,1)S(1)}, u32[]{:S(2)}, u32[]{:S(2)}) %collective-permute-start.18) | collective-permute-done | bytes 393248 | tf_op jit(solution)/shard_map/ppermute | solution.py:300
  47.8 0.6 shard_map.106
  48.4 3.5 %collective-permute-start.21 = (bf16[512,384]{1,0:T(8,128)(2,1)S(1)}, bf16[512,384]{1,0:T(8,128)(2,1)S(1)}, u32[]{:S(2)}, u32[]{:S(2)}) collective-permute-start(bf16[512,384]{1,0:T(8,128)(2,1)S(1)} %shard_map.106), channel_id=1, source_target_pairs={{0,16},{16,0},{8,24},{24,8},{1,17},{17,1},{9,25},{25,9},{2,18},{18... | collective-permute-start | bytes 1179656 | tf_op jit(solution)/shard_map/ppermute | solution.py:305
  52.0 1.5 %shard_map.102.refs_0_ = bf16[384,1152]{1,0:T(8,128)(2,1)S(1)} custom-call(s32[3]{0:T(128)S(1)} %copy-done.6, bf16[384,896]{1,0:T(8,128)(2,1)S(1)} %get-tuple-element.40.refs_1_, bf16[2048,384]{1,0:T(8,128)(2,1)S(1)} %bitcast.12, bf16[2048,384]{1,0:T(8,128)(2,1)S(1)} %bitcast.15), custom_call_target="tpu_custom_call" | custom-call | tf_op jit(solution)/shard_map/pallas_call | solution.py:32
  54.0 0.8 %collective-permute-start.15 = (bf16[96,1152]{1,0:T(8,128)(2,1)S(1)}, bf16[96,1152]{1,0:T(8,128)(2,1)S(1)}, u32[]{:S(2)}, u32[]{:S(2)}) collective-permute-start(bf16[96,1152]{1,0:T(8,128)(2,1)S(1)} %get-tuple-element.43), channel_id=1, source_target_pairs={{0,2},{2,0},{4,6},{6,4},{1,3},{3,1},{5,7},{7,5},{8,10},{10,8},{12,... | collective-permute-start | bytes 663560 | tf_op jit(solution)/shard_map/ppermute | solution.py:257
  54.8 1.3 %collective-permute-start.16 = (bf16[96,1152]{1,0:T(8,128)(2,1)S(1)}, bf16[96,1152]{1,0:T(8,128)(2,1)S(1)}, u32[]{:S(2)}, u32[]{:S(2)}) collective-permute-start(bf16[96,1152]{1,0:T(8,128)(2,1)S(1)} %get-tuple-element.44), channel_id=1, source_target_pairs={{0,4},{2,6},{4,0},{6,2},{1,5},{3,7},{5,1},{7,3},{8,12},{10,14},{12... | collective-permute-start | bytes 663560 | tf_op jit(solution)/shard_map/ppermute | solution.py:257
  56.1 1.4 %collective-permute-start.17 = (bf16[96,1152]{1,0:T(8,128)(2,1)S(1)}, bf16[96,1152]{1,0:T(8,128)(2,1)S(1)}, u32[]{:S(2)}, u32[]{:S(2)}) collective-permute-start(bf16[96,1152]{1,0:T(8,128)(2,1)S(1)} %get-tuple-element.45), channel_id=1, source_target_pairs={{0,6},{2,4},{4,2},{6,0},{1,7},{3,5},{5,3},{7,1},{8,14},{10,12},{12... | collective-permute-start | bytes 663560 | tf_op jit(solution)/shard_map/ppermute | solution.py:257
  57.6 0.6 shard_map.105.refs_1_
  58.2 3.8 %collective-permute-done.15.refs_4_ = bf16[96,1152]{1,0:T(8,128)(2,1)S(1)} collective-permute-done((bf16[96,1152]{1,0:T(8,128)(2,1)S(1)}, bf16[96,1152]{1,0:T(8,128)(2,1)S(1)}, u32[]{:S(2)}, u32[]{:S(2)}) %collective-permute-start.15) | collective-permute-done | bytes 221216 | tf_op jit(solution)/shard_map/ppermute | solution.py:257
  62.0 3.5 %collective-permute-done.16.refs_5_ = bf16[96,1152]{1,0:T(8,128)(2,1)S(1)} collective-permute-done((bf16[96,1152]{1,0:T(8,128)(2,1)S(1)}, bf16[96,1152]{1,0:T(8,128)(2,1)S(1)}, u32[]{:S(2)}, u32[]{:S(2)}) %collective-permute-start.16) | collective-permute-done | bytes 221216 | tf_op jit(solution)/shard_map/ppermute | solution.py:257
  65.5 1.9 %shard_map.104 = (bf16[128,1024]{1,0:T(8,128)(2,1)}, f32[2,128]{1,0:T(2,128)}) custom-call(s32[3]{0:T(128)S(1)} %copy-done.6, s32[2,128]{1,0:T(2,128)S(1)} %bitcast.18, f32[2,128]{1,0:T(2,128)S(1)} %bitcast.20, bf16[96,1152]{1,0:T(8,128)(2,1)S(1)} %get-tuple-element.42.refs_3_, bf16[96,1152]{1,0:T(8,128)(2,1)S(1)} %collective-permute-done.15.refs_4_, ...), custom_call_target="tpu_custom_call" | custom-call | tf_op jit(solution)/shard_map/pallas_call | solution.py:32
  67.4 1.3 %collective-permute-done.21.refs_2_ = bf16[512,384]{1,0:T(8,128)(2,1)S(1)} collective-permute-done((bf16[512,384]{1,0:T(8,128)(2,1)S(1)}, bf16[512,384]{1,0:T(8,128)(2,1)S(1)}, u32[]{:S(2)}, u32[]{:S(2)}) %collective-permute-start.21) | collective-permute-done | bytes 393248 | tf_op jit(solution)/shard_map/ppermute | solution.py:305
  68.7 0.9 %copy-done.3 = bf16[128,1024]{1,0:T(8,128)(2,1)S(1)} copy-done((bf16[128,1024]{1,0:T(8,128)(2,1)S(1)}, bf16[128,1024]{1,0:T(8,128)(2,1)}, u32[]{:S(2)}) %copy-start.3) | copy-done | bytes 262168
  69.7 0.9 %shard_map.107 = f32[512,384]{1,0:T(8,128)} custom-call(bf16[128,1024]{1,0:T(8,128)(2,1)S(1)} %copy-done.3, f32[512,384]{1,0:T(8,128)S(1)} %shard_map.105.refs_1_, bf16[512,384]{1,0:T(8,128)(2,1)S(1)} %collective-permute-done.21.refs_2_), custom_call_target="tpu_custom_call" | custom-call | tf_op jit(solution)/shard_map/pallas_call | solution.py:32
  (45 shorter events, 2.9 us)
Async XLA Ops:
  4.5 8.9 %collective-permute-start = (bf16[96,1024]{1,0:T(8,128)(2,1)}, bf16[96,1024]{1,0:T(8,128)(2,1)S(1)}, u32[]{:S(2)}, u32[]{:S(2)}) collective-permute-start(bf16[96,1024]{1,0:T(8,128)(2,1)} %get-tuple-element.28), channel_id=1, source_target_pairs={{0,2},{2,0},{4,6},{6,4},{1,3},{3,1},{5,7},{7,5},{8,10},{10,8},{12,... | collective-permute-start | bytes 589832 | tf_op jit(solution)/shard_map/ppermute | solution.py:257
  7.5 12.3 %collective-permute-start.1 = (bf16[96,1024]{1,0:T(8,128)(2,1)}, bf16[96,1024]{1,0:T(8,128)(2,1)S(1)}, u32[]{:S(2)}, u32[]{:S(2)}) collective-permute-start(bf16[96,1024]{1,0:T(8,128)(2,1)} %get-tuple-element.29), channel_id=1, source_target_pairs={{0,4},{2,6},{4,0},{6,2},{1,5},{3,7},{5,1},{7,3},{8,12},{10,14},{12... | collective-permute-start | bytes 589832 | tf_op jit(solution)/shard_map/ppermute | solution.py:257
  9.0 10.7 %collective-permute-start.2 = (bf16[96,1024]{1,0:T(8,128)(2,1)}, bf16[96,1024]{1,0:T(8,128)(2,1)S(1)}, u32[]{:S(2)}, u32[]{:S(2)}) collective-permute-start(bf16[96,1024]{1,0:T(8,128)(2,1)} %get-tuple-element.30), channel_id=1, source_target_pairs={{0,6},{2,4},{4,2},{6,0},{1,7},{3,5},{5,3},{7,1},{8,14},{10,12},{12... | collective-permute-start | bytes 589832 | tf_op jit(solution)/shard_map/ppermute | solution.py:257
  9.0 12.9 %collective-permute-start.7 = (bf16[96,1024]{1,0:T(8,128)(2,1)}, bf16[96,1024]{1,0:T(8,128)(2,1)S(1)}, u32[]{:S(2)}, u32[]{:S(2)}) collective-permute-start(bf16[96,1024]{1,0:T(8,128)(2,1)} %get-tuple-element.33), channel_id=1, source_target_pairs={{0,2},{2,0},{4,6},{6,4},{1,3},{3,1},{5,7},{7,5},{8,10},{10,8},{12,... | collective-permute-start | bytes 589832 | tf_op jit(solution)/shard_map/ppermute | solution.py:257
  11.0 15.7 %collective-permute-start.8 = (bf16[96,1024]{1,0:T(8,128)(2,1)}, bf16[96,1024]{1,0:T(8,128)(2,1)S(1)}, u32[]{:S(2)}, u32[]{:S(2)}) collective-permute-start(bf16[96,1024]{1,0:T(8,128)(2,1)} %get-tuple-element.34), channel_id=1, source_target_pairs={{0,4},{2,6},{4,0},{6,2},{1,5},{3,7},{5,1},{7,3},{8,12},{10,14},{12... | collective-permute-start | bytes 589832 | tf_op jit(solution)/shard_map/ppermute | solution.py:257
  13.4 13.3 %collective-permute-start.9 = (bf16[96,1024]{1,0:T(8,128)(2,1)}, bf16[96,1024]{1,0:T(8,128)(2,1)S(1)}, u32[]{:S(2)}, u32[]{:S(2)}) collective-permute-start(bf16[96,1024]{1,0:T(8,128)(2,1)} %get-tuple-element.35), channel_id=1, source_target_pairs={{0,6},{2,4},{4,2},{6,0},{1,7},{3,5},{5,3},{7,1},{8,14},{10,12},{12... | collective-permute-start | bytes 589832 | tf_op jit(solution)/shard_map/ppermute | solution.py:257
  19.7 7.6 %collective-permute-start.3 = (bf16[96,1024]{1,0:T(8,128)(2,1)}, bf16[96,1024]{1,0:T(8,128)(2,1)S(1)}, u32[]{:S(2)}, u32[]{:S(2)}) collective-permute-start(bf16[96,1024]{1,0:T(8,128)(2,1)} %get-tuple-element.27.refs_0_), channel_id=1, source_target_pairs={{0,1},{1,0},{2,3},{3,2},{4,5},{5,4},{6,7},{7,6},{8,9},{9,8},{10,11... | collective-permute-start | bytes 589832 | tf_op jit(solution)/shard_map/ppermute | solution.py:253
  19.7 7.6 %collective-permute-start.4 = (bf16[96,1024]{1,0:T(8,128)(2,1)S(1)}, bf16[96,1024]{1,0:T(8,128)(2,1)S(1)}, u32[]{:S(2)}, u32[]{:S(2)}) collective-permute-start(bf16[96,1024]{1,0:T(8,128)(2,1)S(1)} %collective-permute-done.refs_1_), channel_id=1, source_target_pairs={{0,1},{1,0},{2,3},{3,2},{4,5},{5,4},{6,7},{7,6},{8,9},{9,8},{10,11... | collective-permute-start | bytes 589832 | tf_op jit(solution)/shard_map/ppermute | solution.py:253
  21.9 5.9 %collective-permute-start.5 = (bf16[96,1024]{1,0:T(8,128)(2,1)S(1)}, bf16[96,1024]{1,0:T(8,128)(2,1)S(1)}, u32[]{:S(2)}, u32[]{:S(2)}) collective-permute-start(bf16[96,1024]{1,0:T(8,128)(2,1)S(1)} %collective-permute-done.1.refs_2_), channel_id=1, source_target_pairs={{0,1},{1,0},{2,3},{3,2},{4,5},{5,4},{6,7},{7,6},{8,9},{9,8},{10,11... | collective-permute-start | bytes 589832 | tf_op jit(solution)/shard_map/ppermute | solution.py:253
  26.7 2.2 %collective-permute-start.6 = (bf16[96,1024]{1,0:T(8,128)(2,1)S(1)}, bf16[96,1024]{1,0:T(8,128)(2,1)S(1)}, u32[]{:S(2)}, u32[]{:S(2)}) collective-permute-start(bf16[96,1024]{1,0:T(8,128)(2,1)S(1)} %collective-permute-done.2.refs_3_), channel_id=1, source_target_pairs={{0,1},{1,0},{2,3},{3,2},{4,5},{5,4},{6,7},{7,6},{8,9},{9,8},{10,11... | collective-permute-start | bytes 589832 | tf_op jit(solution)/shard_map/ppermute | solution.py:253
  26.7 2.2 %copy-start.6 = (s32[3]{0:T(128)S(1)}, s32[3]{0:T(128)}, u32[]{:S(2)}) copy-start(s32[3]{0:T(128)} %pad_add_fusion.refs_0_) | copy-start | bytes 40
  26.7 2.3 %copy-start = (bf16[1,2048,384]{2,1,0:T(8,128)(2,1)S(1)}, bf16[1,2048,384]{2,1,0:T(8,128)(2,1)}, u32[]{:S(2)}) copy-start(bf16[1,2048,384]{2,1,0:T(8,128)(2,1)} %param.11) | copy-start | bytes 4718596
  26.7 2.3 %copy-start.1 = (bf16[1,2048,384]{2,1,0:T(8,128)(2,1)S(1)}, bf16[1,2048,384]{2,1,0:T(8,128)(2,1)}, u32[]{:S(2)}) copy-start(bf16[1,2048,384]{2,1,0:T(8,128)(2,1)} %param.12) | copy-start | bytes 4718596
  26.7 4.8 %collective-permute-start.10 = (bf16[96,1024]{1,0:T(8,128)(2,1)}, bf16[96,1024]{1,0:T(8,128)(2,1)S(1)}, u32[]{:S(2)}, u32[]{:S(2)}) collective-permute-start(bf16[96,1024]{1,0:T(8,128)(2,1)} %get-tuple-element.32.refs_1_), channel_id=1, source_target_pairs={{0,1},{1,0},{2,3},{3,2},{4,5},{5,4},{6,7},{7,6},{8,9},{9,8},{10,11... | collective-permute-start | bytes 589832 | tf_op jit(solution)/shard_map/ppermute | solution.py:253
  27.3 4.2 %collective-permute-start.11 = (bf16[96,1024]{1,0:T(8,128)(2,1)S(1)}, bf16[96,1024]{1,0:T(8,128)(2,1)S(1)}, u32[]{:S(2)}, u32[]{:S(2)}) collective-permute-start(bf16[96,1024]{1,0:T(8,128)(2,1)S(1)} %collective-permute-done.7.refs_2_), channel_id=1, source_target_pairs={{0,1},{1,0},{2,3},{3,2},{4,5},{5,4},{6,7},{7,6},{8,9},{9,8},{10,11... | collective-permute-start | bytes 589832 | tf_op jit(solution)/shard_map/ppermute | solution.py:253
  27.4 4.2 %collective-permute-start.12 = (bf16[96,1024]{1,0:T(8,128)(2,1)S(1)}, bf16[96,1024]{1,0:T(8,128)(2,1)S(1)}, u32[]{:S(2)}, u32[]{:S(2)}) collective-permute-start(bf16[96,1024]{1,0:T(8,128)(2,1)S(1)} %collective-permute-done.8.refs_3_), channel_id=1, source_target_pairs={{0,1},{1,0},{2,3},{3,2},{4,5},{5,4},{6,7},{7,6},{8,9},{9,8},{10,11... | collective-permute-start | bytes 589832 | tf_op jit(solution)/shard_map/ppermute | solution.py:253
  27.8 3.7 %collective-permute-start.13 = (bf16[96,1024]{1,0:T(8,128)(2,1)S(1)}, bf16[96,1024]{1,0:T(8,128)(2,1)S(1)}, u32[]{:S(2)}, u32[]{:S(2)}) collective-permute-start(bf16[96,1024]{1,0:T(8,128)(2,1)S(1)} %collective-permute-done.9.refs_4_), channel_id=1, source_target_pairs={{0,1},{1,0},{2,3},{3,2},{4,5},{5,4},{6,7},{7,6},{8,9},{9,8},{10,11... | collective-permute-start | bytes 589832 | tf_op jit(solution)/shard_map/ppermute | solution.py:253
  27.9 0.9 %copy-start.5 = (bf16[96,1024]{1,0:T(8,128)(2,1)S(1)}, bf16[96,1024]{1,0:T(8,128)(2,1)}, u32[]{:S(2)}) copy-start(bf16[96,1024]{1,0:T(8,128)(2,1)} %get-tuple-element.27.refs_0_) | copy-start | bytes 589828
  29.0 2.4 %copy-start.4 = (bf16[96,1024]{1,0:T(8,128)(2,1)S(1)}, bf16[96,1024]{1,0:T(8,128)(2,1)}, u32[]{:S(2)}) copy-start(bf16[96,1024]{1,0:T(8,128)(2,1)} %get-tuple-element.32.refs_1_) | copy-start | bytes 589828
  31.5 2.3 %copy-start.2 = (bf16[1,384,2048]{2,1,0:T(8,128)(2,1)S(1)}, bf16[1,384,2048]{2,1,0:T(8,128)(2,1)}, u32[]{:S(2)}) copy-start(bf16[1,384,2048]{2,1,0:T(8,128)(2,1)} %param.13) | copy-start | bytes 4718596
  36.2 17.3 %collective-permute-start.14 = (bf16[384,1152]{1,0:T(8,128)(2,1)S(1)}, bf16[384,1152]{1,0:T(8,128)(2,1)S(1)}, u32[]{:S(2)}, u32[]{:S(2)}) collective-permute-start(bf16[384,1152]{1,0:T(8,128)(2,1)S(1)} %get-tuple-element.41), channel_id=1, source_target_pairs={{0,1},{1,0},{2,3},{3,2},{4,5},{5,4},{6,7},{7,6},{8,9},{9,8},{10,11... | collective-permute-start | bytes 2654216 | tf_op jit(solution)/shard_map/ppermute | solution.py:253
  36.7 11.1 %collective-permute-start.18 = (bf16[512,384]{1,0:T(8,128)(2,1)S(1)}, bf16[512,384]{1,0:T(8,128)(2,1)S(1)}, u32[]{:S(2)}, u32[]{:S(2)}) collective-permute-start(bf16[512,384]{1,0:T(8,128)(2,1)S(1)} %get-tuple-element.50), channel_id=1, source_target_pairs={{0,8},{8,0},{16,24},{24,16},{1,9},{9,1},{17,25},{25,17},{2,10},{10... | collective-permute-start | bytes 1179656 | tf_op jit(solution)/shard_map/ppermute | solution.py:300
  38.3 17.8 %collective-permute-start.20 = (bf16[512,384]{1,0:T(8,128)(2,1)S(1)}, bf16[512,384]{1,0:T(8,128)(2,1)S(1)}, u32[]{:S(2)}, u32[]{:S(2)}) collective-permute-start(bf16[512,384]{1,0:T(8,128)(2,1)S(1)} %get-tuple-element.36.refs_1_), channel_id=1, source_target_pairs={{8,16},{16,8},{9,17},{17,9},{10,18},{18,10},{11,19},{19,11},{12,20... | collective-permute-start | bytes 1179656 | tf_op jit(solution)/shard_map/ppermute | solution.py:302
  39.0 18.6 %collective-permute-start.19 = (bf16[512,384]{1,0:T(8,128)(2,1)S(1)}, bf16[512,384]{1,0:T(8,128)(2,1)S(1)}, u32[]{:S(2)}, u32[]{:S(2)}) collective-permute-start(bf16[512,384]{1,0:T(8,128)(2,1)S(1)} %get-tuple-element.36.refs_1_), channel_id=1, source_target_pairs={{0,8},{24,16},{1,9},{25,17},{2,10},{26,18},{3,11},{27,19},{4,12},{... | collective-permute-start | bytes 1179656 | tf_op jit(solution)/shard_map/ppermute | solution.py:301
  48.4 20.3 %collective-permute-start.21 = (bf16[512,384]{1,0:T(8,128)(2,1)S(1)}, bf16[512,384]{1,0:T(8,128)(2,1)S(1)}, u32[]{:S(2)}, u32[]{:S(2)}) collective-permute-start(bf16[512,384]{1,0:T(8,128)(2,1)S(1)} %shard_map.106), channel_id=1, source_target_pairs={{0,16},{16,0},{8,24},{24,8},{1,17},{17,1},{9,25},{25,9},{2,18},{18... | collective-permute-start | bytes 1179656 | tf_op jit(solution)/shard_map/ppermute | solution.py:305
  54.0 8.0 %collective-permute-start.15 = (bf16[96,1152]{1,0:T(8,128)(2,1)S(1)}, bf16[96,1152]{1,0:T(8,128)(2,1)S(1)}, u32[]{:S(2)}, u32[]{:S(2)}) collective-permute-start(bf16[96,1152]{1,0:T(8,128)(2,1)S(1)} %get-tuple-element.43), channel_id=1, source_target_pairs={{0,2},{2,0},{4,6},{6,4},{1,3},{3,1},{5,7},{7,5},{8,10},{10,8},{12,... | collective-permute-start | bytes 663560 | tf_op jit(solution)/shard_map/ppermute | solution.py:257
  54.8 10.7 %collective-permute-start.16 = (bf16[96,1152]{1,0:T(8,128)(2,1)S(1)}, bf16[96,1152]{1,0:T(8,128)(2,1)S(1)}, u32[]{:S(2)}, u32[]{:S(2)}) collective-permute-start(bf16[96,1152]{1,0:T(8,128)(2,1)S(1)} %get-tuple-element.44), channel_id=1, source_target_pairs={{0,4},{2,6},{4,0},{6,2},{1,5},{3,7},{5,1},{7,3},{8,12},{10,14},{12... | collective-permute-start | bytes 663560 | tf_op jit(solution)/shard_map/ppermute | solution.py:257
  56.1 9.4 %copy-start.7 = (s32[128,2]{0,1:T(2,128)S(1)}, s32[128,2]{0,1:T(2,128)}, u32[]{:S(2)}) copy-start(s32[128,2]{0,1:T(2,128)} %param.9) | copy-start | bytes 3076
  56.1 9.4 %copy-start.8 = (f32[128,2]{0,1:T(2,128)S(1)}, f32[128,2]{0,1:T(2,128)}, u32[]{:S(2)}) copy-start(f32[128,2]{0,1:T(2,128)} %param.10) | copy-start | bytes 3076
  56.1 9.4 %collective-permute-start.17 = (bf16[96,1152]{1,0:T(8,128)(2,1)S(1)}, bf16[96,1152]{1,0:T(8,128)(2,1)S(1)}, u32[]{:S(2)}, u32[]{:S(2)}) collective-permute-start(bf16[96,1152]{1,0:T(8,128)(2,1)S(1)} %get-tuple-element.45), channel_id=1, source_target_pairs={{0,6},{2,4},{4,2},{6,0},{1,7},{3,5},{5,3},{7,1},{8,14},{10,12},{12... | collective-permute-start | bytes 663560 | tf_op jit(solution)/shard_map/ppermute | solution.py:257
  68.7 1.0 %copy-start.3 = (bf16[128,1024]{1,0:T(8,128)(2,1)S(1)}, bf16[128,1024]{1,0:T(8,128)(2,1)}, u32[]{:S(2)}) copy-start(bf16[128,1024]{1,0:T(8,128)(2,1)} %get-tuple-element.24.refs_0_) | copy-start | bytes 786436

commit v3 on v2

--- a/solution.py
+++ b/solution.py
@@ -19,15 +19,14 @@
     return lax.dot_general(a, b, dims, preferred_element_type=F32)
 
 
-def call(body, out_shape, operands, scalars=None, after=(), hbm=(), scratch=(), vmem=VMEM_LIMIT):
+def call(body, out_shape, operands, located=False, after=(), hbm=(), scratch=(), vmem=VMEM_LIMIT):
     vm = pl.BlockSpec(memory_space=pltpu.VMEM)
-    lead = 0 if scalars is None else 1
-    specs = [pl.BlockSpec(memory_space=pltpu.SMEM)] * lead
-    specs += [pl.BlockSpec(memory_space=pl.ANY)] * len(after)
+    specs = [pl.BlockSpec(memory_space=pl.ANY)] * len(after)
     specs += [pl.BlockSpec(memory_space=pltpu.HBM) if i in hbm else vm for i in range(len(operands))]
 
     def run(*refs):
-        body(*refs[:lead], *refs[lead + len(after):])
+        place = [[lax.axis_index(axis) for axis in ("expert", "pair", "dp")]] if located else []
+        body(*place, *refs[len(after):])
 
     return pl.pallas_call(
         run,
@@ -36,7 +35,7 @@
         out_specs=jax.tree.map(lambda _: vm, out_shape),
         scratch_shapes=list(scratch),
         compiler_params=pltpu.CompilerParams(vmem_limit_bytes=vmem),
-    )(*([] if scalars is None else [scalars]), *after, *operands)
+    )(*after, *operands)
 
 
 def struct(shape, dtype):
@@ -94,6 +93,16 @@
         dy_out[m][...] = (p_col * dot(pick, dy)).astype(BF16)
 
 
+def copy_body(ref, out):
+    out[...] = ref[...]
+
+
+def load_body(gw, uw, out):
+    units = gw.shape[1]
+    out[:, :units] = gw[...]
+    out[:, units:] = uw[...]
+
+
 def stack_body(count, *refs):
     blocks, outs = refs[:count], refs[count:]
     cap = blocks[0].shape[0]
@@ -105,13 +114,14 @@
             low += out.shape[1]
 
 
-def forward_body(sc, own, oth, gw, uw, hid_ref, hid_b_ref, dgate_ref, act_ref):
+def forward_body(sc, own, oth, w, hid_ref, hid_b_ref, dgate_ref, act_ref):
     pair = sc[1]
     half = own.shape[1]
     mine = pl.ds(pl.multiple_of(pair * half, half), half)
     other = pl.ds(pl.multiple_of((1 - pair) * half, half), half)
-    gate = dot(own[...], gw[mine, :]) + dot(oth[...], gw[other, :])
-    up = dot(own[...], uw[mine, :]) + dot(oth[...], uw[other, :])
+    both = dot(own[...], w[mine, :]) + dot(oth[...], w[other, :])
+    units = w.shape[1] // 2
+    gate, up = both[:, :units], both[:, units:]
     sig = jax.nn.sigmoid(gate)
     act = gate * sig
     hid = act * up
@@ -121,7 +131,7 @@
     act_ref[...] = act
 
 
-def weight_body(sc, own, oth, hid_b, first, second, third, fourth):
+def weight_body(which, sc, own, oth, hid_b, *outs):
     group, pair = sc[2], sc[1]
     quarter = own.shape[1] // 2
     odd = group % 2
@@ -140,10 +150,9 @@
 
     same = pair == odd
     differ = jnp.logical_not(same)
-    block(first, differ, 1 - odd)
-    block(second, same, 1 - odd)
-    block(third, same, odd)
-    block(fourth, differ, odd)
+    places = [(differ, 1 - odd), (same, 1 - odd), (same, odd), (differ, odd)]
+    for out, index in zip(outs, which):
+        block(out, *places[index])
 
 
 def onward_body(sc, third, fourth, near, out):
@@ -170,11 +179,7 @@
         out[...] = third[...] + near[...].astype(F32)
 
 
-def total_body(part, far, out):
-    out[...] = part[...] + far[...].astype(F32)
-
-
-def backward_body(sc, own, oth, dw, gw, uw, hid_ref, dgate_ref, act_ref, send_ref, grads_ref):
+def backward_body(sc, own, oth, dw, gw, uw, hid_ref, dgate_ref, act_ref, grads_ref, *send):
     pair = sc[1]
     units = hid_ref.shape[1]
     half = own.shape[1]
@@ -187,15 +192,21 @@
     grads_ref[:, units:2 * units] = g_up
     tail = split_columns(jnp.sum(back * hid_ref[...], axis=1, keepdims=True))
     grads_ref[:, 2 * units:] = tail
-    send_ref[:, :half] = (dot(g_gate, gw[other, :], NT) + dot(g_up, uw[other, :], NT)).astype(BF16)
-    send_ref[:, half:] = tail
+    product = (dot(g_gate, gw[other, :], NT) + dot(g_up, uw[other, :], NT)).astype(BF16)
+    cap = send[0].shape[0]
+    for m, ref in enumerate(send):
+        rows = slice(m * cap, (m + 1) * cap)
+        ref[:, :half] = product[rows]
+        ref[:, half:] = tail[rows]
 
 
 def keep_body(sc, grads_ref, gw, uw, keep_ref):
     units = gw.shape[1]
     half = keep_ref.shape[1] - 128
     mine = pl.ds(pl.multiple_of(sc[1] * half, half), half)
-    product = dot(grads_ref[:, :units], gw[mine, :], NT) + dot(grads_ref[:, units:2 * units], uw[mine, :], NT)
+    product = (
+        dot(grads_ref[:, :units], gw[mine, :], NT) + dot(grads_ref[:, units:2 * units], uw[mine, :], NT)
+    )
     keep_ref[:, :half] = product.astype(BF16)
     keep_ref[:, half:] = grads_ref[:, 2 * units:]
 
@@ -207,13 +218,14 @@
     return jnp.where(lane == 0, high.astype(F32), jnp.where(lane == 1, low.astype(F32), 0.0)).astype(BF16)
 
 
-def merge_body(experts, keep_ref, recv_ref, *outs):
+def merge_body(experts, keep_ref, *refs):
+    received, outs = refs[:experts], refs[experts:]
     cap, wide = outs[0].shape
     half = wide - 128
     for m in range(experts):
         rows = slice(m * cap, (m + 1) * cap)
-        outs[m][:, :half] = (keep_ref[rows, :half].astype(F32) + recv_ref[rows, :half].astype(F32)).astype(BF16)
-        tail = keep_ref[rows, half:].astype(F32) + recv_ref[rows, half:].astype(F32)
+        outs[m][:, :half] = (keep_ref[rows, :half].astype(F32) + received[m][:, :half].astype(F32)).astype(BF16)
+        tail = keep_ref[rows, half:].astype(F32) + received[m][:, half:].astype(F32)
         outs[m][:, half:] = split_columns(tail[:, 0:1] + tail[:, 1:2])
 
 
@@ -246,8 +258,7 @@
     slots = experts * cap
     quarter = half // 2
     gw, uw, dw = gate_weight[0], up_weight[0], down_weight[0]
-    me, pair, group = lax.axis_index("expert"), lax.axis_index("pair"), lax.axis_index("dp")
-    scalars = jnp.stack([me, pair, group]).astype(jnp.int32)
+    group = lax.axis_index("dp")
 
     def swap(value):
         return lax.ppermute(value, "pair", [(0, 1), (1, 0)])
@@ -262,7 +273,7 @@
         functools.partial(pack_body, experts, cap),
         [struct((cap, half), BF16)] * (2 * experts),
         [*row_args, tokens, grad_out],
-        scalars,
+        located=True,
         hbm=(0, 1, 2, 3),
         scratch=(
             pltpu.VMEM((fanout, count), jnp.int32),
@@ -279,32 +290,33 @@
 
     x_parts = cross(packed[:experts])
     dy_parts = cross(packed[experts:])
+    (w_all,) = call(load_body, [struct((gw.shape[0], 2 * units), BF16)], [gw, uw])
+    x_parts[0] = call(copy_body, struct((cap, half), BF16), [x_parts[0]], after=[w_all])
     x_own, x_oth = stack(x_parts), stack([swap(v) for v in x_parts])
 
     square = struct((slots, units), F32)
     hid, hid_b, dgate, act = call(
         forward_body,
         [square, struct((slots, units), BF16), square, square],
-        [x_own, x_oth, gw, uw],
-        scalars,
+        [x_own, x_oth, w_all],
+        located=True,
     )
     dy_own, dy_oth = stack(dy_parts, [hid_b]), stack([swap(v) for v in dy_parts])
 
-    first, second, third, fourth = call(
-        weight_body,
-        [struct((quarter, units), BF16)] * 2 + [struct((quarter, units), F32)] * 2,
-        [dy_own, dy_oth, hid_b],
-        scalars,
-    )
+    blocks = [struct((quarter, units), t) for t in (BF16, BF16, F32, F32)]
+    w_args = [dy_own, dy_oth, hid_b]
+    first, second = call(functools.partial(weight_body, [0, 1]), blocks[:2], w_args, located=True)
+    third, fourth = call(functools.partial(weight_body, [2, 3]), blocks[2:], w_args, located=True, after=[first])
     if groups == 4:
         from_near = lax.ppermute(first, "dp", [(0, 1), (1, 0), (2, 3), (3, 2)])
         from_end = lax.ppermute(second, "dp", [(0, 1), (3, 2)])
         from_mid = lax.ppermute(second, "dp", [(1, 2), (2, 1)])
-        block = struct((quarter, units), F32)
-        onward = call(onward_body, struct((quarter, units), BF16), [third, fourth, from_near], scalars)
+        arrived_mid, arrived_end = [from_mid], [from_end]
+        onward = call(onward_body, struct((quarter, units), BF16), [third, fourth, from_near], located=True)
         from_far = lax.ppermute(onward, "dp", [(0, 2), (2, 0), (1, 3), (3, 1)])
-        part = call(partial_body, block, [third, fourth, from_near, from_end, from_mid], scalars)
+        part = call(partial_body, struct((quarter, units), F32), [third, fourth, from_near, from_end, from_mid], located=True)
     else:
+        arrived_mid, arrived_end = [], []
         odd = group % 2 == 1
         first, second = first.astype(F32), second.astype(F32)
         whole = jnp.concatenate(
@@ -318,27 +330,26 @@
         )
         grad_down = lax.psum_scatter(whole[None], "dp", scatter_dimension=1, tiled=True)
 
-    send, grads = call(
+    grads, *send = call(
         backward_body,
-        [struct((slots, half + 128), BF16), struct((slots, 2 * units + 128), BF16)],
+        [struct((slots, 2 * units + 128), BF16)] + [struct((cap, half + 128), BF16)] * experts,
         [dy_own, dy_oth, dw, gw, uw, hid, dgate, act],
-        scalars,
-        after=[second] if groups == 4 else [],
-    )
-    received = swap(send)
-    keep = call(keep_body, struct((slots, half + 128), BF16), [grads, gw, uw], scalars)
-    merged = call(functools.partial(merge_body, experts), [struct((cap, half + 128), BF16)] * experts, [keep, received])
+        located=True,
+        after=[second],
+    )
+    received = [swap(v) for v in send]
+    keep = call(keep_body, struct((slots, half + 128), BF16), [grads, gw, uw], located=True, after=arrived_mid)
+    merged = call(functools.partial(merge_body, experts), [struct((cap, half + 128), BF16)] * experts, [keep, *received], after=arrived_end)
     returned = cross(merged)
     grad_input, grad_probs = call(
         functools.partial(combine_body, experts, cap),
         [struct((count, half), BF16), struct((fanout, count), F32)],
         [*row_args, *returned],
-        scalars,
+        located=True,
     )
 
     if groups == 4:
-        grad_down = call(total_body, block, [part, from_far], after=[grad_input])[None]
-
+        grad_down = (part + from_far.astype(F32))[None]
     return grad_input, grad_probs.T, grad_down
 
 

time: 70.8 us -> 64.6 us (0.912)
  Pallas kernels: 16.5 us -> 10.9 us
  waiting for transfers between devices: 21.9 us -> 18.5 us
  local copies, waits for them, and re-layouts: 1.91 us -> 4.32 us
    pallas_call x14 -> x16, Pallas kernels: 16.5 us -> 10.9 us  [call(): pl.pallas_call(run, out_shape=out_shape, in_specs=specs, out_specs=jax.tr...]
    ppermute x1, waiting for transfers between devices: 2.53 us -> 0.01 us  [on_device(): from_near = lax.ppermute(first, 'dp', [(0, 1), (1, 0), (2, 3), (3, 2)])]
    unnamed x18 -> x24, local copies, waits for them, and re-layouts: 1.91 us -> 4.32 us
    ppermute x1, waiting for transfers between devices: 0.01 us -> 2.3 us  [on_device(): from_end = lax.ppermute(second, 'dp', [(0, 1), (3, 2)])]
    ppermute x9, waiting for transfers between devices: 18 us -> 16.2 us  [cross(): lax.ppermute(values[m], 'expert', [(i, i ^ m) for i in range(experts)])]
    ppermute x9, starting transfers between devices: 14.6 us -> 13.2 us  [cross(): lax.ppermute(values[m], 'expert', [(i, i ^ m) for i in range(experts)])]
    ppermute x1, waiting for transfers between devices: 1.33 us -> 0.01 us  [on_device(): from_far = lax.ppermute(onward, 'dp', [(0, 2), (2, 0), (1, 3), (3, 1)])]
    broadcast_in_dim x0 -> x1, other arithmetic: none -> 0.95 us  [on_device(): grad_down = (part + from_far.astype(F32))[None]]
  transfers between devices with their start and end apart: 22 -> 25, of which waited for: 8 -> 7; matrix products, arithmetic and copies ran while one was open for 0% -> 0% of each run, Pallas kernels for 11% -> 12%
where the time goes in v3:
time: 64.6 us; the launch traced here: 64.3 us
  starting transfers between devices  28.7 us (44%)
  waiting for transfers between devices  18.5 us (29%)
  Pallas kernels  10.9 us (17%)
  local copies, waits for them, and re-layouts  4.32 us (7%)
  other arithmetic  0.95 us (1%)
  between operations  0.91 us (1%)
    ppermute x9, waiting for transfers between devices, cross(): lax.ppermute(values[m], 'expert', [(i, i ^ m) for i in range(experts)])  16.2 us
    ppermute x9, starting transfers between devices, cross(): lax.ppermute(values[m], 'expert', [(i, i ^ m) for i in range(experts)])  13.2 us
    pallas_call x16, Pallas kernels, call(): pl.pallas_call(run, out_shape=out_shape, in_specs=specs, out_specs=jax.tr...  10.9 us
    ppermute x1, starting transfers between devices, on_device(): from_end = lax.ppermute(second, 'dp', [(0, 1), (3, 2)])  6.31 us
    unnamed x24, local copies, waits for them, and re-layouts  4.32 us
    ppermute x1, starting transfers between devices, on_device(): from_far = lax.ppermute(onward, 'dp', [(0, 2), (2, 0), (1, 3), (3, 1)])  4.25 us
    ppermute x12, starting transfers between devices, swap(): return lax.ppermute(value, 'pair', [(0, 1), (1, 0)])  2.45 us
    ppermute x1, waiting for transfers between devices, on_device(): from_end = lax.ppermute(second, 'dp', [(0, 1), (3, 2)])  2.3 us
  transfers between devices with their start and end apart: 25, of which 7 were waited for; matrix products, arithmetic and copies ran while one was open for 0% of the time, Pallas kernels for 12%

profile of v3, /device:TPU:0, one launch (start us, length us, event | category | flops | bytes accessed | tf_op | source)
XLA Modules:
  0.0 64.3 jit_solution(10665866190791306679)
XLA Ops:
  0.6 2.5 %shard_map.95 = (bf16[96,1024]{1,0:T(8,128)(2,1)}, bf16[96,1024]{1,0:T(8,128)(2,1)}, bf16[96,1024]{1,0:T(8,128)(2,1)}, bf16[96,1024]{1,0:T(8,128)(2,1)}, bf16[96...) custom-call(s32[2,128]{1,0:T(2,128)} %bitcast.15, ...), custom_call_target="tpu_custom_call" | custom-call | tf_op jit(solution)/shard_map/pallas_call | solution.py:31
  3.2 3.0 %collective-permute-start = (bf16[96,1024]{1,0:T(8,128)(2,1)}, bf16[96,1024]{1,0:T(8,128)(2,1)S(1)}, u32[]{:S(2)}, u32[]{:S(2)}) collective-permute-start(bf16[96,1024]{1,0:T(8,128)(2,1)} %get-tuple-element.31), channel_id=1, source_target_pairs={{0,2},{2,0},{4,6},{6,4},{1,3},{3,1},{5,7},{7,5},{8,10},{10,8},{12,... | collective-permute-start | bytes 589832 | tf_op jit(solution)/shard_map/ppermute | solution.py:268
  6.2 1.5 %collective-permute-start.1 = (bf16[96,1024]{1,0:T(8,128)(2,1)}, bf16[96,1024]{1,0:T(8,128)(2,1)S(1)}, u32[]{:S(2)}, u32[]{:S(2)}) collective-permute-start(bf16[96,1024]{1,0:T(8,128)(2,1)} %get-tuple-element.32), channel_id=1, source_target_pairs={{0,4},{2,6},{4,0},{6,2},{1,5},{3,7},{5,1},{7,3},{8,12},{10,14},{12... | collective-permute-start | bytes 589832 | tf_op jit(solution)/shard_map/ppermute | solution.py:268
  7.7 1.4 %copy-done = bf16[1,2048,384]{2,1,0:T(8,128)(2,1)S(1)} copy-done((bf16[1,2048,384]{2,1,0:T(8,128)(2,1)S(1)}, bf16[1,2048,384]{2,1,0:T(8,128)(2,1)}, u32[]{:S(2)}) %copy-start) | copy-done | bytes 1572888
  9.1 1.4 %copy-done.2 = bf16[1,2048,384]{2,1,0:T(8,128)(2,1)S(1)} copy-done((bf16[1,2048,384]{2,1,0:T(8,128)(2,1)S(1)}, bf16[1,2048,384]{2,1,0:T(8,128)(2,1)}, u32[]{:S(2)}) %copy-start.2) | copy-done | bytes 1572888
  10.8 0.7 %copy-done.6 = bf16[96,1024]{1,0:T(8,128)(2,1)S(1)} copy-done((bf16[96,1024]{1,0:T(8,128)(2,1)S(1)}, bf16[96,1024]{1,0:T(8,128)(2,1)}, u32[]{:S(2)}) %copy-start.6) | copy-done | bytes 196632
  11.6 0.8 %copy-done.11 = bf16[96,1024]{1,0:T(8,128)(2,1)S(1)} copy-done((bf16[96,1024]{1,0:T(8,128)(2,1)S(1)}, bf16[96,1024]{1,0:T(8,128)(2,1)}, u32[]{:S(2)}) %copy-start.11) | copy-done | bytes 196632
  12.4 1.9 %collective-permute-start.7 = (bf16[96,1024]{1,0:T(8,128)(2,1)S(1)}, bf16[96,1024]{1,0:T(8,128)(2,1)S(1)}, u32[]{:S(2)}, u32[]{:S(2)}) collective-permute-start(bf16[96,1024]{1,0:T(8,128)(2,1)S(1)} %copy-done.11), channel_id=1, source_target_pairs={{0,2},{2,0},{4,6},{6,4},{1,3},{3,1},{5,7},{7,5},{8,10},{10,8},{12,... | collective-permute-start | bytes 589832 | tf_op jit(solution)/shard_map/ppermute | solution.py:268
  14.4 1.5 %collective-permute-start.8 = (bf16[96,1024]{1,0:T(8,128)(2,1)S(1)}, bf16[96,1024]{1,0:T(8,128)(2,1)S(1)}, u32[]{:S(2)}, u32[]{:S(2)}) collective-permute-start(bf16[96,1024]{1,0:T(8,128)(2,1)S(1)} %copy-done.10), channel_id=1, source_target_pairs={{0,4},{2,6},{4,0},{6,2},{1,5},{3,7},{5,1},{7,3},{8,12},{10,14},{12... | collective-permute-start | bytes 589832 | tf_op jit(solution)/shard_map/ppermute | solution.py:268
  15.9 0.8 %collective-permute-done.1.refs_2_ = bf16[96,1024]{1,0:T(8,128)(2,1)S(1)} collective-permute-done((bf16[96,1024]{1,0:T(8,128)(2,1)}, bf16[96,1024]{1,0:T(8,128)(2,1)S(1)}, u32[]{:S(2)}, u32[]{:S(2)}) %collective-permute-start.1) | collective-permute-done | bytes 196640 | tf_op jit(solution)/shard_map/ppermute | solution.py:268
  16.7 1.6 %collective-permute-start.9 = (bf16[96,1024]{1,0:T(8,128)(2,1)S(1)}, bf16[96,1024]{1,0:T(8,128)(2,1)S(1)}, u32[]{:S(2)}, u32[]{:S(2)}) collective-permute-start(bf16[96,1024]{1,0:T(8,128)(2,1)S(1)} %copy-done.9), channel_id=1, source_target_pairs={{0,6},{2,4},{4,2},{6,0},{1,7},{3,5},{5,3},{7,1},{8,14},{10,12},{12... | collective-permute-start | bytes 589832 | tf_op jit(solution)/shard_map/ppermute | solution.py:268
  18.3 0.5 collective-permute-start.5
  18.8 1.6 %collective-permute-done.7.refs_2_ = bf16[96,1024]{1,0:T(8,128)(2,1)S(1)} collective-permute-done((bf16[96,1024]{1,0:T(8,128)(2,1)S(1)}, bf16[96,1024]{1,0:T(8,128)(2,1)S(1)}, u32[]{:S(2)}, u32[]{:S(2)}) %collective-permute-start.7) | collective-permute-done | bytes 196640 | tf_op jit(solution)/shard_map/ppermute | solution.py:268
  20.4 5.0 %collective-permute-done.8.refs_3_ = bf16[96,1024]{1,0:T(8,128)(2,1)S(1)} collective-permute-done((bf16[96,1024]{1,0:T(8,128)(2,1)S(1)}, bf16[96,1024]{1,0:T(8,128)(2,1)S(1)}, u32[]{:S(2)}, u32[]{:S(2)}) %collective-permute-start.8) | collective-permute-done | bytes 196640 | tf_op jit(solution)/shard_map/ppermute | solution.py:268
  26.6 1.4 %shard_map.99 = (f32[384,384]{1,0:T(8,128)S(1)}, bf16[384,384]{1,0:T(8,128)(2,1)S(1)}, f32[384,384]{1,0:T(8,128)S(1)}, f32[384,384]{1,0:T(8,128)S(1)}) custom-call(bf16[384,1024]{1,0:T(8,128)(2,1)S(1)} %shard_map.97.refs_0_, bf16[384,1024]{1,0:T(8,128)(2,1)S(1)} %shard_map.98.refs_1_, bf16[2048,768]{1,0:T(8,128)(2,1)S(1)} %shard_map.94.refs_0_.refs_2_), custom_call_target="tpu_custom_call" | custom-call | tf_op jit(solution)/shard_map/pallas_call | solution.py:31
  28.2 0.7 %shard_map.102 = (bf16[512,384]{1,0:T(8,128)(2,1)S(1)}, bf16[512,384]{1,0:T(8,128)(2,1)S(1)}) custom-call(bf16[384,1024]{1,0:T(8,128)(2,1)S(1)} %shard_map.100.refs_0_.refs_1_, bf16[384,1024]{1,0:T(8,128)(2,1)S(1)} %shard_map.101.refs_1_.refs_2_, bf16[384,384]{1,0:T(8,128)(2,1)S(1)} %get-tuple-element.34.refs_0_.refs_2_.refs_3_), custom_call_target="tpu_custom_call" | custom-call | tf_op jit(solution)/shard_map/pallas_call | solution.py:31
  28.9 1.9 %collective-permute-start.23 = (bf16[512,384]{1,0:T(8,128)(2,1)S(1)}, bf16[512,384]{1,0:T(8,128)(2,1)S(1)}, u32[]{:S(2)}, u32[]{:S(2)}) collective-permute-start(bf16[512,384]{1,0:T(8,128)(2,1)S(1)} %get-tuple-element.54.refs_0_), channel_id=1, source_target_pairs={{0,8},{8,0},{16,24},{24,16},{1,9},{9,1},{17,25},{25,17},{2,10},{10... | collective-permute-start | bytes 1179656 | tf_op jit(solution)/shard_map/ppermute | solution.py:311
  30.8 0.7 %collective-permute-start.15 = (bf16[512,384]{1,0:T(8,128)(2,1)S(1)}, bf16[512,384]{1,0:T(8,128)(2,1)S(1)}, u32[]{:S(2)}, u32[]{:S(2)}) collective-permute-start(bf16[512,384]{1,0:T(8,128)(2,1)S(1)} %get-tuple-element.39.refs_0_), channel_id=1, source_target_pairs={{8,16},{16,8},{9,17},{17,9},{10,18},{18,10},{11,19},{19,11},{12,20... | collective-permute-start | bytes 1179656 | tf_op jit(solution)/shard_map/ppermute | solution.py:313
  31.5 1.9 %shard_map.103 = (bf16[384,896]{1,0:T(8,128)(2,1)S(1)}, bf16[96,1152]{1,0:T(8,128)(2,1)S(1)}, bf16[96,1152]{1,0:T(8,128)(2,1)S(1)}, bf16[96,1152]{1,0:T(8,128)(2,1)S(1)}, bf16[96,1152]{1,0:T(8,128)(2,1)S(1)}) custom-call(bf16[512,384]{1,0:T(8,128)(2,1)S(1)} %get-tuple-element.39.refs_0_, bf16[384,1024]{1,0:T(8,128)(2,1)S(1)} %shard_map.100.refs_0_.refs_1_, ...), custom_call_target="tpu_custom_call" | custom-call | tf_op jit(solution)/shard_map/pallas_call | solution.py:31
  33.5 6.3 %collective-permute-start.14 = (bf16[512,384]{1,0:T(8,128)(2,1)S(1)}, bf16[512,384]{1,0:T(8,128)(2,1)S(1)}, u32[]{:S(2)}, u32[]{:S(2)}) collective-permute-start(bf16[512,384]{1,0:T(8,128)(2,1)S(1)} %get-tuple-element.39.refs_0_), channel_id=1, source_target_pairs={{0,8},{24,16},{1,9},{25,17},{2,10},{26,18},{3,11},{27,19},{4,12},{... | collective-permute-start | bytes 1179656 | tf_op jit(solution)/shard_map/ppermute | solution.py:312
  40.6 0.9 %shard_map.107 = (f32[512,384]{1,0:T(8,128)S(1)}, f32[512,384]{1,0:T(8,128)S(1)}) custom-call(bf16[512,384]{1,0:T(8,128)(2,1)S(1)} %get-tuple-element.54.refs_0_, bf16[384,1024]{1,0:T(8,128)(2,1)S(1)} %shard_map.100.refs_0_.refs_1_, bf16[384,1024]{1,0:T(8,128)(2,1)S(1)} %shard_map.101.refs_1_.refs_2_, ...), custom_call_target="tpu_custom_call" | custom-call | tf_op jit(solution)/shard_map/pallas_call | solution.py:31
  41.6 4.2 %collective-permute-start.24 = (bf16[512,384]{1,0:T(8,128)(2,1)S(1)}, bf16[512,384]{1,0:T(8,128)(2,1)S(1)}, u32[]{:S(2)}, u32[]{:S(2)}) collective-permute-start(bf16[512,384]{1,0:T(8,128)(2,1)S(1)} %shard_map.109), channel_id=1, source_target_pairs={{0,16},{16,0},{8,24},{24,8},{1,17},{17,1},{9,25},{25,9},{2,18},{18... | collective-permute-start | bytes 1179656 | tf_op jit(solution)/shard_map/ppermute | solution.py:316
  45.9 1.0 %shard_map.104.refs_1_ = bf16[384,1152]{1,0:T(8,128)(2,1)S(1)} custom-call(bf16[512,384]{1,0:T(8,128)(2,1)S(1)} %collective-permute-done.15.refs_0_.refs_4_, bf16[384,896]{1,0:T(8,128)(2,1)S(1)} %get-tuple-element.43.refs_1_, bf16[2048,384]{1,0:T(8,128)(2,1)S(1)} %bitcast.10, bf16[2048,384]{1,0:T(8,128)(2,1)S(1)} %bitcast.13), custom_call_target="tpu_custom_call" | custom-call | tf_op jit(solution)/shard_map/pallas_call | solution.py:31
  46.9 2.3 %collective-permute-done.14.refs_0_.refs_3_ = bf16[512,384]{1,0:T(8,128)(2,1)S(1)} collective-permute-done((bf16[512,384]{1,0:T(8,128)(2,1)S(1)}, bf16[512,384]{1,0:T(8,128)(2,1)S(1)}, u32[]{:S(2)}, u32[]{:S(2)}) %collective-permute-start.14) | collective-permute-done | bytes 393248 | tf_op jit(solution)/shard_map/ppermute | solution.py:312
  49.6 0.9 %collective-permute-start.20 = (bf16[96,1152]{1,0:T(8,128)(2,1)S(1)}, bf16[96,1152]{1,0:T(8,128)(2,1)S(1)}, u32[]{:S(2)}, u32[]{:S(2)}) collective-permute-start(bf16[96,1152]{1,0:T(8,128)(2,1)S(1)} %get-tuple-element.49), channel_id=1, source_target_pairs={{0,2},{2,0},{4,6},{6,4},{1,3},{3,1},{5,7},{7,5},{8,10},{10,8},{12,... | collective-permute-start | bytes 663560 | tf_op jit(solution)/shard_map/ppermute | solution.py:268
  50.5 1.3 %collective-permute-start.21 = (bf16[96,1152]{1,0:T(8,128)(2,1)S(1)}, bf16[96,1152]{1,0:T(8,128)(2,1)S(1)}, u32[]{:S(2)}, u32[]{:S(2)}) collective-permute-start(bf16[96,1152]{1,0:T(8,128)(2,1)S(1)} %get-tuple-element.50), channel_id=1, source_target_pairs={{0,4},{2,6},{4,0},{6,2},{1,5},{3,7},{5,1},{7,3},{8,12},{10,14},{12... | collective-permute-start | bytes 663560 | tf_op jit(solution)/shard_map/ppermute | solution.py:268
  51.8 1.4 %collective-permute-start.22 = (bf16[96,1152]{1,0:T(8,128)(2,1)S(1)}, bf16[96,1152]{1,0:T(8,128)(2,1)S(1)}, u32[]{:S(2)}, u32[]{:S(2)}) collective-permute-start(bf16[96,1152]{1,0:T(8,128)(2,1)S(1)} %get-tuple-element.51), channel_id=1, source_target_pairs={{0,6},{2,4},{4,2},{6,0},{1,7},{3,5},{5,3},{7,1},{8,14},{10,12},{12... | collective-permute-start | bytes 663560 | tf_op jit(solution)/shard_map/ppermute | solution.py:268
  53.3 4.8 %collective-permute-done.20.refs_3_ = bf16[96,1152]{1,0:T(8,128)(2,1)S(1)} collective-permute-done((bf16[96,1152]{1,0:T(8,128)(2,1)S(1)}, bf16[96,1152]{1,0:T(8,128)(2,1)S(1)}, u32[]{:S(2)}, u32[]{:S(2)}) %collective-permute-start.20) | collective-permute-done | bytes 221216 | tf_op jit(solution)/shard_map/ppermute | solution.py:268
  58.1 2.3 %collective-permute-done.21.refs_4_ = bf16[96,1152]{1,0:T(8,128)(2,1)S(1)} collective-permute-done((bf16[96,1152]{1,0:T(8,128)(2,1)S(1)}, bf16[96,1152]{1,0:T(8,128)(2,1)S(1)}, u32[]{:S(2)}, u32[]{:S(2)}) %collective-permute-start.21) | collective-permute-done | bytes 221216 | tf_op jit(solution)/shard_map/ppermute | solution.py:268
  60.4 1.6 %collective-permute-done.22.refs_5_ = bf16[96,1152]{1,0:T(8,128)(2,1)S(1)} collective-permute-done((bf16[96,1152]{1,0:T(8,128)(2,1)S(1)}, bf16[96,1152]{1,0:T(8,128)(2,1)S(1)}, u32[]{:S(2)}, u32[]{:S(2)}) %collective-permute-start.22) | collective-permute-done | bytes 221216 | tf_op jit(solution)/shard_map/ppermute | solution.py:268
  62.0 1.3 %shard_map.106 = (bf16[128,1024]{1,0:T(8,128)(2,1)}, f32[2,128]{1,0:T(2,128)}) custom-call(s32[2,128]{1,0:T(2,128)S(1)} %bitcast.16, f32[2,128]{1,0:T(2,128)S(1)} %bitcast.18, bf16[96,1152]{1,0:T(8,128)(2,1)S(1)} %get-tuple-element.48.refs_2_, bf16[96,1152]{1,0:T(8,128)(2,1)S(1)} %collective-permute-done.20.refs_3_, ...), custom_call_target="tpu_custom_call" | custom-call | tf_op jit(solution)/shard_map/pallas_call | solution.py:31
  63.4 1.0 %add_bitcast_fusion = f32[1,512,384]{2,1,0:T(8,128)} fusion(f32[512,384]{1,0:T(8,128)S(1)} %shard_map.108, bf16[512,384]{1,0:T(8,128)(2,1)S(1)} %collective-permute-done.24), kind=kLoop, calls=%fused_computation | loop fusion | flops 393216 | bytes 1966080 | tf_op jit(solution)/shard_map/broadcast_in_dim | solution.py:352
  (59 shorter events, 3.1 us)
Async XLA Ops:
  3.2 11.2 %collective-permute-start = (bf16[96,1024]{1,0:T(8,128)(2,1)}, bf16[96,1024]{1,0:T(8,128)(2,1)S(1)}, u32[]{:S(2)}, u32[]{:S(2)}) collective-permute-start(bf16[96,1024]{1,0:T(8,128)(2,1)} %get-tuple-element.31), channel_id=1, source_target_pairs={{0,2},{2,0},{4,6},{6,4},{1,3},{3,1},{5,7},{7,5},{8,10},{10,8},{12,... | collective-permute-start | bytes 589832 | tf_op jit(solution)/shard_map/ppermute | solution.py:268
  6.2 10.5 %collective-permute-start.1 = (bf16[96,1024]{1,0:T(8,128)(2,1)}, bf16[96,1024]{1,0:T(8,128)(2,1)S(1)}, u32[]{:S(2)}, u32[]{:S(2)}) collective-permute-start(bf16[96,1024]{1,0:T(8,128)(2,1)} %get-tuple-element.32), channel_id=1, source_target_pairs={{0,4},{2,6},{4,0},{6,2},{1,5},{3,7},{5,1},{7,3},{8,12},{10,14},{12... | collective-permute-start | bytes 589832 | tf_op jit(solution)/shard_map/ppermute | solution.py:268
  7.7 10.6 %collective-permute-start.2 = (bf16[96,1024]{1,0:T(8,128)(2,1)}, bf16[96,1024]{1,0:T(8,128)(2,1)S(1)}, u32[]{:S(2)}, u32[]{:S(2)}) collective-permute-start(bf16[96,1024]{1,0:T(8,128)(2,1)} %get-tuple-element.33), channel_id=1, source_target_pairs={{0,6},{2,4},{4,2},{6,0},{1,7},{3,5},{5,3},{7,1},{8,14},{10,12},{12... | collective-permute-start | bytes 589832 | tf_op jit(solution)/shard_map/ppermute | solution.py:268
  11.5 5.2 %copy-start.9 = (bf16[96,1024]{1,0:T(8,128)(2,1)S(1)}, bf16[96,1024]{1,0:T(8,128)(2,1)}, u32[]{:S(2)}) copy-start(bf16[96,1024]{1,0:T(8,128)(2,1)} %get-tuple-element.38) | copy-start | bytes 589828
  11.5 13.9 %copy-start.5 = (bf16[96,1024]{1,0:T(8,128)(2,1)S(1)}, bf16[96,1024]{1,0:T(8,128)(2,1)}, u32[]{:S(2)}) copy-start(bf16[96,1024]{1,0:T(8,128)(2,1)} %get-tuple-element.35.refs_1_) | copy-start | bytes 589828
  11.5 6.8 %collective-permute-start.3 = (bf16[96,1024]{1,0:T(8,128)(2,1)S(1)}, bf16[96,1024]{1,0:T(8,128)(2,1)S(1)}, u32[]{:S(2)}, u32[]{:S(2)}) collective-permute-start(bf16[96,1024]{1,0:T(8,128)(2,1)S(1)} %shard_map.96.refs_0_), channel_id=1, source_target_pairs={{0,1},{1,0},{2,3},{3,2},{4,5},{5,4},{6,7},{7,6},{8,9},{9,8},{10,11... | collective-permute-start | bytes 589832 | tf_op jit(solution)/shard_map/ppermute | solution.py:264
  12.4 8.0 %collective-permute-start.7 = (bf16[96,1024]{1,0:T(8,128)(2,1)S(1)}, bf16[96,1024]{1,0:T(8,128)(2,1)S(1)}, u32[]{:S(2)}, u32[]{:S(2)}) collective-permute-start(bf16[96,1024]{1,0:T(8,128)(2,1)S(1)} %copy-done.11), channel_id=1, source_target_pairs={{0,2},{2,0},{4,6},{6,4},{1,3},{3,1},{5,7},{7,5},{8,10},{10,8},{12,... | collective-permute-start | bytes 589832 | tf_op jit(solution)/shard_map/ppermute | solution.py:268
  14.4 11.0 %collective-permute-start.8 = (bf16[96,1024]{1,0:T(8,128)(2,1)S(1)}, bf16[96,1024]{1,0:T(8,128)(2,1)S(1)}, u32[]{:S(2)}, u32[]{:S(2)}) collective-permute-start(bf16[96,1024]{1,0:T(8,128)(2,1)S(1)} %copy-done.10), channel_id=1, source_target_pairs={{0,4},{2,6},{4,0},{6,2},{1,5},{3,7},{5,1},{7,3},{8,12},{10,14},{12... | collective-permute-start | bytes 589832 | tf_op jit(solution)/shard_map/ppermute | solution.py:268
  16.7 8.7 %collective-permute-start.9 = (bf16[96,1024]{1,0:T(8,128)(2,1)S(1)}, bf16[96,1024]{1,0:T(8,128)(2,1)S(1)}, u32[]{:S(2)}, u32[]{:S(2)}) collective-permute-start(bf16[96,1024]{1,0:T(8,128)(2,1)S(1)} %copy-done.9), channel_id=1, source_target_pairs={{0,6},{2,4},{4,2},{6,0},{1,7},{3,5},{5,3},{7,1},{8,14},{10,12},{12... | collective-permute-start | bytes 589832 | tf_op jit(solution)/shard_map/ppermute | solution.py:268
  18.3 7.6 %collective-permute-start.4 = (bf16[96,1024]{1,0:T(8,128)(2,1)S(1)}, bf16[96,1024]{1,0:T(8,128)(2,1)S(1)}, u32[]{:S(2)}, u32[]{:S(2)}) collective-permute-start(bf16[96,1024]{1,0:T(8,128)(2,1)S(1)} %collective-permute-done.refs_1_), channel_id=1, source_target_pairs={{0,1},{1,0},{2,3},{3,2},{4,5},{5,4},{6,7},{7,6},{8,9},{9,8},{10,11... | collective-permute-start | bytes 589832 | tf_op jit(solution)/shard_map/ppermute | solution.py:264
  18.3 7.7 %collective-permute-start.5 = (bf16[96,1024]{1,0:T(8,128)(2,1)S(1)}, bf16[96,1024]{1,0:T(8,128)(2,1)S(1)}, u32[]{:S(2)}, u32[]{:S(2)}) collective-permute-start(bf16[96,1024]{1,0:T(8,128)(2,1)S(1)} %collective-permute-done.1.refs_2_), channel_id=1, source_target_pairs={{0,1},{1,0},{2,3},{3,2},{4,5},{5,4},{6,7},{7,6},{8,9},{9,8},{10,11... | collective-permute-start | bytes 589832 | tf_op jit(solution)/shard_map/ppermute | solution.py:264
  20.4 6.1 %collective-permute-start.6 = (bf16[96,1024]{1,0:T(8,128)(2,1)S(1)}, bf16[96,1024]{1,0:T(8,128)(2,1)S(1)}, u32[]{:S(2)}, u32[]{:S(2)}) collective-permute-start(bf16[96,1024]{1,0:T(8,128)(2,1)S(1)} %collective-permute-done.2.refs_3_), channel_id=1, source_target_pairs={{0,1},{1,0},{2,3},{3,2},{4,5},{5,4},{6,7},{7,6},{8,9},{9,8},{10,11... | collective-permute-start | bytes 589832 | tf_op jit(solution)/shard_map/ppermute | solution.py:264
  25.4 2.7 %collective-permute-start.10 = (bf16[96,1024]{1,0:T(8,128)(2,1)S(1)}, bf16[96,1024]{1,0:T(8,128)(2,1)S(1)}, u32[]{:S(2)}, u32[]{:S(2)}) collective-permute-start(bf16[96,1024]{1,0:T(8,128)(2,1)S(1)} %copy-done.5), channel_id=1, source_target_pairs={{0,1},{1,0},{2,3},{3,2},{4,5},{5,4},{6,7},{7,6},{8,9},{9,8},{10,11... | collective-permute-start | bytes 589832 | tf_op jit(solution)/shard_map/ppermute | solution.py:264
  25.4 2.7 %collective-permute-start.11 = (bf16[96,1024]{1,0:T(8,128)(2,1)S(1)}, bf16[96,1024]{1,0:T(8,128)(2,1)S(1)}, u32[]{:S(2)}, u32[]{:S(2)}) collective-permute-start(bf16[96,1024]{1,0:T(8,128)(2,1)S(1)} %collective-permute-done.7.refs_2_), channel_id=1, source_target_pairs={{0,1},{1,0},{2,3},{3,2},{4,5},{5,4},{6,7},{7,6},{8,9},{9,8},{10,11... | collective-permute-start | bytes 589832 | tf_op jit(solution)/shard_map/ppermute | solution.py:264
  25.9 2.2 %collective-permute-start.12 = (bf16[96,1024]{1,0:T(8,128)(2,1)S(1)}, bf16[96,1024]{1,0:T(8,128)(2,1)S(1)}, u32[]{:S(2)}, u32[]{:S(2)}) collective-permute-start(bf16[96,1024]{1,0:T(8,128)(2,1)S(1)} %collective-permute-done.8.refs_3_), channel_id=1, source_target_pairs={{0,1},{1,0},{2,3},{3,2},{4,5},{5,4},{6,7},{7,6},{8,9},{9,8},{10,11... | collective-permute-start | bytes 589832 | tf_op jit(solution)/shard_map/ppermute | solution.py:264
  26.0 2.1 %collective-permute-start.13 = (bf16[96,1024]{1,0:T(8,128)(2,1)S(1)}, bf16[96,1024]{1,0:T(8,128)(2,1)S(1)}, u32[]{:S(2)}, u32[]{:S(2)}) collective-permute-start(bf16[96,1024]{1,0:T(8,128)(2,1)S(1)} %collective-permute-done.9.refs_4_), channel_id=1, source_target_pairs={{0,1},{1,0},{2,3},{3,2},{4,5},{5,4},{6,7},{7,6},{8,9},{9,8},{10,11... | collective-permute-start | bytes 589832 | tf_op jit(solution)/shard_map/ppermute | solution.py:264
  28.0 3.5 %copy-start.4 = (bf16[1,384,2048]{2,1,0:T(8,128)(2,1)S(1)}, bf16[1,384,2048]{2,1,0:T(8,128)(2,1)}, u32[]{:S(2)}) copy-start(bf16[1,384,2048]{2,1,0:T(8,128)(2,1)} %param.13) | copy-start | bytes 4718596
  28.1 3.4 %copy-start.1 = (bf16[1,2048,384]{2,1,0:T(8,128)(2,1)S(1)}, bf16[1,2048,384]{2,1,0:T(8,128)(2,1)}, u32[]{:S(2)}) copy-start(bf16[1,2048,384]{2,1,0:T(8,128)(2,1)} %param.11) | copy-start | bytes 4718596
  28.1 3.4 %copy-start.3 = (bf16[1,2048,384]{2,1,0:T(8,128)(2,1)S(1)}, bf16[1,2048,384]{2,1,0:T(8,128)(2,1)}, u32[]{:S(2)}) copy-start(bf16[1,2048,384]{2,1,0:T(8,128)(2,1)} %param.12) | copy-start | bytes 4718596
  28.9 11.5 %collective-permute-start.23 = (bf16[512,384]{1,0:T(8,128)(2,1)S(1)}, bf16[512,384]{1,0:T(8,128)(2,1)S(1)}, u32[]{:S(2)}, u32[]{:S(2)}) collective-permute-start(bf16[512,384]{1,0:T(8,128)(2,1)S(1)} %get-tuple-element.54.refs_0_), channel_id=1, source_target_pairs={{0,8},{8,0},{16,24},{24,16},{1,9},{9,1},{17,25},{25,17},{2,10},{10... | collective-permute-start | bytes 1179656 | tf_op jit(solution)/shard_map/ppermute | solution.py:311
  30.8 10.8 %collective-permute-start.15 = (bf16[512,384]{1,0:T(8,128)(2,1)S(1)}, bf16[512,384]{1,0:T(8,128)(2,1)S(1)}, u32[]{:S(2)}, u32[]{:S(2)}) collective-permute-start(bf16[512,384]{1,0:T(8,128)(2,1)S(1)} %get-tuple-element.39.refs_0_), channel_id=1, source_target_pairs={{8,16},{16,8},{9,17},{17,9},{10,18},{18,10},{11,19},{19,11},{12,20... | collective-permute-start | bytes 1179656 | tf_op jit(solution)/shard_map/ppermute | solution.py:313
  33.4 6.7 %collective-permute-start.16 = (bf16[96,1152]{1,0:T(8,128)(2,1)S(1)}, bf16[96,1152]{1,0:T(8,128)(2,1)S(1)}, u32[]{:S(2)}, u32[]{:S(2)}) collective-permute-start(bf16[96,1152]{1,0:T(8,128)(2,1)S(1)} %get-tuple-element.44), channel_id=1, source_target_pairs={{0,1},{1,0},{2,3},{3,2},{4,5},{5,4},{6,7},{7,6},{8,9},{9,8},{10,11... | collective-permute-start | bytes 663560 | tf_op jit(solution)/shard_map/ppermute | solution.py:264
  33.5 15.7 %collective-permute-start.14 = (bf16[512,384]{1,0:T(8,128)(2,1)S(1)}, bf16[512,384]{1,0:T(8,128)(2,1)S(1)}, u32[]{:S(2)}, u32[]{:S(2)}) collective-permute-start(bf16[512,384]{1,0:T(8,128)(2,1)S(1)} %get-tuple-element.39.refs_0_), channel_id=1, source_target_pairs={{0,8},{24,16},{1,9},{25,17},{2,10},{26,18},{3,11},{27,19},{4,12},{... | collective-permute-start | bytes 1179656 | tf_op jit(solution)/shard_map/ppermute | solution.py:312
  39.8 7.1 %collective-permute-start.17 = (bf16[96,1152]{1,0:T(8,128)(2,1)S(1)}, bf16[96,1152]{1,0:T(8,128)(2,1)S(1)}, u32[]{:S(2)}, u32[]{:S(2)}) collective-permute-start(bf16[96,1152]{1,0:T(8,128)(2,1)S(1)} %get-tuple-element.45), channel_id=1, source_target_pairs={{0,1},{1,0},{2,3},{3,2},{4,5},{5,4},{6,7},{7,6},{8,9},{9,8},{10,11... | collective-permute-start | bytes 663560 | tf_op jit(solution)/shard_map/ppermute | solution.py:264
  40.1 6.8 %collective-permute-start.18 = (bf16[96,1152]{1,0:T(8,128)(2,1)S(1)}, bf16[96,1152]{1,0:T(8,128)(2,1)S(1)}, u32[]{:S(2)}, u32[]{:S(2)}) collective-permute-start(bf16[96,1152]{1,0:T(8,128)(2,1)S(1)} %get-tuple-element.46), channel_id=1, source_target_pairs={{0,1},{1,0},{2,3},{3,2},{4,5},{5,4},{6,7},{7,6},{8,9},{9,8},{10,11... | collective-permute-start | bytes 663560 | tf_op jit(solution)/shard_map/ppermute | solution.py:264
  40.4 6.5 %collective-permute-start.19 = (bf16[96,1152]{1,0:T(8,128)(2,1)S(1)}, bf16[96,1152]{1,0:T(8,128)(2,1)S(1)}, u32[]{:S(2)}, u32[]{:S(2)}) collective-permute-start(bf16[96,1152]{1,0:T(8,128)(2,1)S(1)} %get-tuple-element.47), channel_id=1, source_target_pairs={{0,1},{1,0},{2,3},{3,2},{4,5},{5,4},{6,7},{7,6},{8,9},{9,8},{10,11... | collective-permute-start | bytes 663560 | tf_op jit(solution)/shard_map/ppermute | solution.py:264
  41.6 21.8 %collective-permute-start.24 = (bf16[512,384]{1,0:T(8,128)(2,1)S(1)}, bf16[512,384]{1,0:T(8,128)(2,1)S(1)}, u32[]{:S(2)}, u32[]{:S(2)}) collective-permute-start(bf16[512,384]{1,0:T(8,128)(2,1)S(1)} %shard_map.109), channel_id=1, source_target_pairs={{0,16},{16,0},{8,24},{24,8},{1,17},{17,1},{9,25},{25,9},{2,18},{18... | collective-permute-start | bytes 1179656 | tf_op jit(solution)/shard_map/ppermute | solution.py:316
  49.6 8.4 %collective-permute-start.20 = (bf16[96,1152]{1,0:T(8,128)(2,1)S(1)}, bf16[96,1152]{1,0:T(8,128)(2,1)S(1)}, u32[]{:S(2)}, u32[]{:S(2)}) collective-permute-start(bf16[96,1152]{1,0:T(8,128)(2,1)S(1)} %get-tuple-element.49), channel_id=1, source_target_pairs={{0,2},{2,0},{4,6},{6,4},{1,3},{3,1},{5,7},{7,5},{8,10},{10,8},{12,... | collective-permute-start | bytes 663560 | tf_op jit(solution)/shard_map/ppermute | solution.py:268
  50.5 9.9 %collective-permute-start.21 = (bf16[96,1152]{1,0:T(8,128)(2,1)S(1)}, bf16[96,1152]{1,0:T(8,128)(2,1)S(1)}, u32[]{:S(2)}, u32[]{:S(2)}) collective-permute-start(bf16[96,1152]{1,0:T(8,128)(2,1)S(1)} %get-tuple-element.50), channel_id=1, source_target_pairs={{0,4},{2,6},{4,0},{6,2},{1,5},{3,7},{5,1},{7,3},{8,12},{10,14},{12... | collective-permute-start | bytes 663560 | tf_op jit(solution)/shard_map/ppermute | solution.py:268
  51.8 10.3 %copy-start.7 = (s32[128,2]{0,1:T(2,128)S(1)}, s32[128,2]{0,1:T(2,128)}, u32[]{:S(2)}) copy-start(s32[128,2]{0,1:T(2,128)} %param.9) | copy-start | bytes 3076
  51.8 10.3 %copy-start.8 = (f32[128,2]{0,1:T(2,128)S(1)}, f32[128,2]{0,1:T(2,128)}, u32[]{:S(2)}) copy-start(f32[128,2]{0,1:T(2,128)} %param.10) | copy-start | bytes 3076
  51.8 10.3 %collective-permute-start.22 = (bf16[96,1152]{1,0:T(8,128)(2,1)S(1)}, bf16[96,1152]{1,0:T(8,128)(2,1)S(1)}, u32[]{:S(2)}, u32[]{:S(2)}) collective-permute-start(bf16[96,1152]{1,0:T(8,128)(2,1)S(1)} %get-tuple-element.51), channel_id=1, source_target_pairs={{0,6},{2,4},{4,2},{6,0},{1,7},{3,5},{5,3},{7,1},{8,14},{10,12},{12... | collective-permute-start | bytes 663560 | tf_op jit(solution)/shard_map/ppermute | solution.py:268
  (5 other events, 7.5 us)

commit v4 on v3

--- a/solution.py
+++ b/solution.py
@@ -131,52 +131,65 @@
     act_ref[...] = act
 
 
+def each_block(sc, own, oth, index, emit):
+    pair, odd = sc[1], sc[2] % 2
+    quarter = own.shape[1] // 2
+    flip = (0, 1, 1, 0)[index]
+    mine = (pair == odd) if flip else (pair != odd)
+    half = (1 - odd) if index < 2 else odd
+    columns = pl.ds(pl.multiple_of(half * quarter, quarter), quarter)
+
+    @pl.when(mine)
+    def _():
+        emit(own[:, columns])
+
+    @pl.when(jnp.logical_not(mine))
+    def _():
+        emit(oth[:, columns])
+
+
 def weight_body(which, sc, own, oth, hid_b, *outs):
-    group, pair = sc[2], sc[1]
-    quarter = own.shape[1] // 2
-    odd = group % 2
-    hid = hid_b[...]
-
-    def block(out, mine, index):
-        columns = pl.ds(pl.multiple_of(index * quarter, quarter), quarter)
-
-        @pl.when(mine)
-        def _():
-            out[...] = dot(own[:, columns], hid, TN).astype(out.dtype)
-
-        @pl.when(jnp.logical_not(mine))
-        def _():
-            out[...] = dot(oth[:, columns], hid, TN).astype(out.dtype)
-
-    same = pair == odd
-    differ = jnp.logical_not(same)
-    places = [(differ, 1 - odd), (same, 1 - odd), (same, odd), (differ, odd)]
     for out, index in zip(outs, which):
-        block(out, *places[index])
-
-
-def onward_body(sc, third, fourth, near, out):
+        def emit(rows, out=out):
+            out[...] = dot(rows, hid_b[...], TN).astype(out.dtype)
+
+        each_block(sc, own, oth, index, emit)
+
+
+def onward_body(sc, own, oth, hid_b, near, out):
     inner = (sc[2] == 1) | (sc[2] == 2)
 
     @pl.when(inner)
     def _():
-        out[...] = (third[...] + near[...].astype(F32)).astype(BF16)
+        def emit(rows):
+            out[...] = (dot(rows, hid_b[...], TN) + near[...].astype(F32)).astype(BF16)
+
+        each_block(sc, own, oth, 2, emit)
 
     @pl.when(jnp.logical_not(inner))
     def _():
-        out[...] = fourth[...].astype(BF16)
-
-
-def partial_body(sc, third, fourth, near, end, mid, out):
+        def emit(rows):
+            out[...] = dot(rows, hid_b[...], TN).astype(BF16)
+
+        each_block(sc, own, oth, 3, emit)
+
+
+def partial_body(sc, own, oth, hid_b, near, end, mid, out):
     inner = (sc[2] == 1) | (sc[2] == 2)
 
     @pl.when(inner)
     def _():
-        out[...] = fourth[...] + mid[...].astype(F32) + end[...].astype(F32)
+        def emit(rows):
+            out[...] = dot(rows, hid_b[...], TN) + (mid[...].astype(F32) + end[...].astype(F32))
+
+        each_block(sc, own, oth, 3, emit)
 
     @pl.when(jnp.logical_not(inner))
     def _():
-        out[...] = third[...] + near[...].astype(F32)
+        def emit(rows):
+            out[...] = dot(rows, hid_b[...], TN) + near[...].astype(F32)
+
+        each_block(sc, own, oth, 2, emit)
 
 
 def backward_body(sc, own, oth, dw, gw, uw, hid_ref, dgate_ref, act_ref, grads_ref, *send):
@@ -290,7 +303,7 @@
 
     x_parts = cross(packed[:experts])
     dy_parts = cross(packed[experts:])
-    (w_all,) = call(load_body, [struct((gw.shape[0], 2 * units), BF16)], [gw, uw])
+    (w_all,) = call(load_body, [struct((gw.shape[0], 2 * units), BF16)], [gw, uw], after=[x_parts[1]])
     x_parts[0] = call(copy_body, struct((cap, half), BF16), [x_parts[0]], after=[w_all])
     x_own, x_oth = stack(x_parts), stack([swap(v) for v in x_parts])
 
@@ -301,22 +314,37 @@
         [x_own, x_oth, w_all],
         located=True,
     )
-    dy_own, dy_oth = stack(dy_parts, [hid_b]), stack([swap(v) for v in dy_parts])
+    dy_own = stack(dy_parts, [hid_b])
+    dy_oth = stack([swap(v) for v in dy_parts])
 
     blocks = [struct((quarter, units), t) for t in (BF16, BF16, F32, F32)]
     w_args = [dy_own, dy_oth, hid_b]
-    first, second = call(functools.partial(weight_body, [0, 1]), blocks[:2], w_args, located=True)
-    third, fourth = call(functools.partial(weight_body, [2, 3]), blocks[2:], w_args, located=True, after=[first])
+
+    def weights(index):
+        return call(functools.partial(weight_body, index), [blocks[i] for i in index], w_args, located=True)
+
+    first, second = weights([0, 1])
+    if groups != 4:
+        third, fourth = weights([2, 3])
+
+    grads, *send = call(
+        backward_body,
+        [struct((slots, 2 * units + 128), BF16)] + [struct((cap, half + 128), BF16)] * experts,
+        [dy_own, dy_oth, dw, gw, uw, hid, dgate, act],
+        located=True,
+        after=[second],
+    )
+    received = [swap(v) for v in send]
+    arrived_mid, arrived_end = [], []
     if groups == 4:
         from_near = lax.ppermute(first, "dp", [(0, 1), (1, 0), (2, 3), (3, 2)])
         from_end = lax.ppermute(second, "dp", [(0, 1), (3, 2)])
         from_mid = lax.ppermute(second, "dp", [(1, 2), (2, 1)])
         arrived_mid, arrived_end = [from_mid], [from_end]
-        onward = call(onward_body, struct((quarter, units), BF16), [third, fourth, from_near], located=True)
+        onward = call(onward_body, struct((quarter, units), BF16), [*w_args, from_near], located=True)
         from_far = lax.ppermute(onward, "dp", [(0, 2), (2, 0), (1, 3), (3, 1)])
-        part = call(partial_body, struct((quarter, units), F32), [third, fourth, from_near, from_end, from_mid], located=True)
+        part = call(partial_body, struct((quarter, units), F32), [*w_args, from_near, from_end, from_mid], located=True)
     else:
-        arrived_mid, arrived_end = [], []
         odd = group % 2 == 1
         first, second = first.astype(F32), second.astype(F32)
         whole = jnp.concatenate(
@@ -330,22 +358,15 @@
         )
         grad_down = lax.psum_scatter(whole[None], "dp", scatter_dimension=1, tiled=True)
 
-    grads, *send = call(
-        backward_body,
-        [struct((slots, 2 * units + 128), BF16)] + [struct((cap, half + 128), BF16)] * experts,
-        [dy_own, dy_oth, dw, gw, uw, hid, dgate, act],
-        located=True,
-        after=[second],
-    )
-    received = [swap(v) for v in send]
     keep = call(keep_body, struct((slots, half + 128), BF16), [grads, gw, uw], located=True, after=arrived_mid)
-    merged = call(functools.partial(merge_body, experts), [struct((cap, half + 128), BF16)] * experts, [keep, *received], after=arrived_end)
+    merged = call(functools.partial(merge_body, experts), [struct((cap, half + 128), BF16)] * experts, [keep, *received])
     returned = cross(merged)
     grad_input, grad_probs = call(
         functools.partial(combine_body, experts, cap),
         [struct((count, half), BF16), struct((fanout, count), F32)],
         [*row_args, *returned],
         located=True,
+        after=arrived_end,
     )
 
     if groups == 4:

time: 64.6 us -> 63.2 us (0.978)
  the two profiles are of different devices: /device:TPU:0 before, /device:TPU:28 now
where the time goes in v4:
time: 63.2 us; the launch traced here: 62.9 us
  waiting for transfers between devices  29.5 us (47%)
  starting transfers between devices  16.9 us (27%)
  Pallas kernels  11 us (17%)
  local copies, waits for them, and re-layouts  3.74 us (6%)
  other arithmetic  0.95 us (2%)
  between operations  0.87 us (1%)
    ppermute x9, waiting for transfers between devices, cross(): lax.ppermute(values[m], 'expert', [(i, i ^ m) for i in range(experts)])  13.4 us
    pallas_call x15, Pallas kernels, call(): pl.pallas_call(run, out_shape=out_shape, in_specs=specs, out_specs=jax.tr...  11 us
    ppermute x9, starting transfers between devices, cross(): lax.ppermute(values[m], 'expert', [(i, i ^ m) for i in range(experts)])  10.5 us
    ppermute x1, waiting for transfers between devices, on_device(): from_near = lax.ppermute(first, 'dp', [(0, 1), (1, 0), (2, 3), (3, 2)])  6.18 us
    ppermute x1, waiting for transfers between devices, on_device(): from_far = lax.ppermute(onward, 'dp', [(0, 2), (2, 0), (1, 3), (3, 1)])  5.1 us
    unnamed x18, local copies, waits for them, and re-layouts  3.74 us
    ppermute x1, waiting for transfers between devices, on_device(): from_end = lax.ppermute(second, 'dp', [(0, 1), (3, 2)])  3.73 us
    ppermute x1, starting transfers between devices, on_device(): from_end = lax.ppermute(second, 'dp', [(0, 1), (3, 2)])  2.63 us
  transfers between devices with their start and end apart: 25, of which 11 were waited for; matrix products, arithmetic and copies ran while one was open for 0% of the time, Pallas kernels for 12%

profile of v4, /device:TPU:28, one launch (start us, length us, event | category | flops | bytes accessed | tf_op | source)
XLA Modules:
  0.0 62.9 jit_solution(12553425342879160684)
XLA Ops:
  0.6 2.5 %shard_map.94 = (bf16[96,1024]{1,0:T(8,128)(2,1)}, bf16[96,1024]{1,0:T(8,128)(2,1)}, bf16[96,1024]{1,0:T(8,128)(2,1)}, bf16[96,1024]{1,0:T(8,128)(2,1)}, bf16[96...) custom-call(s32[2,128]{1,0:T(2,128)} %bitcast.15, ...), custom_call_target="tpu_custom_call" | custom-call | tf_op jit(solution)/shard_map/pallas_call | solution.py:31
  3.2 1.6 %collective-permute-start = (bf16[96,1024]{1,0:T(8,128)(2,1)}, bf16[96,1024]{1,0:T(8,128)(2,1)S(1)}, u32[]{:S(2)}, u32[]{:S(2)}) collective-permute-start(bf16[96,1024]{1,0:T(8,128)(2,1)} %get-tuple-element.28), channel_id=1, source_target_pairs={{0,2},{2,0},{4,6},{6,4},{1,3},{3,1},{5,7},{7,5},{8,10},{10,8},{12,... | collective-permute-start | bytes 589832 | tf_op jit(solution)/shard_map/ppermute | solution.py:281
  4.7 0.5 collective-permute-start.1
  5.2 1.5 %collective-permute-start.2 = (bf16[96,1024]{1,0:T(8,128)(2,1)}, bf16[96,1024]{1,0:T(8,128)(2,1)S(1)}, u32[]{:S(2)}, u32[]{:S(2)}) collective-permute-start(bf16[96,1024]{1,0:T(8,128)(2,1)} %get-tuple-element.31), channel_id=1, source_target_pairs={{0,6},{2,4},{4,2},{6,0},{1,7},{3,5},{5,3},{7,1},{8,14},{10,12},{12... | collective-permute-start | bytes 589832 | tf_op jit(solution)/shard_map/ppermute | solution.py:281
  6.7 1.5 %collective-permute-start.7 = (bf16[96,1024]{1,0:T(8,128)(2,1)}, bf16[96,1024]{1,0:T(8,128)(2,1)S(1)}, u32[]{:S(2)}, u32[]{:S(2)}) collective-permute-start(bf16[96,1024]{1,0:T(8,128)(2,1)} %get-tuple-element.34), channel_id=1, source_target_pairs={{0,2},{2,0},{4,6},{6,4},{1,3},{3,1},{5,7},{7,5},{8,10},{10,8},{12,... | collective-permute-start | bytes 589832 | tf_op jit(solution)/shard_map/ppermute | solution.py:281
  8.2 0.5 collective-permute-start.8
  8.7 2.5 %collective-permute-done.refs_0_.refs_1_ = bf16[96,1024]{1,0:T(8,128)(2,1)S(1)} collective-permute-done((bf16[96,1024]{1,0:T(8,128)(2,1)}, bf16[96,1024]{1,0:T(8,128)(2,1)S(1)}, u32[]{:S(2)}, u32[]{:S(2)}) %collective-permute-start) | collective-permute-done | bytes 196640 | tf_op jit(solution)/shard_map/ppermute | solution.py:281
  11.3 1.4 %collective-permute-start.9 = (bf16[96,1024]{1,0:T(8,128)(2,1)}, bf16[96,1024]{1,0:T(8,128)(2,1)S(1)}, u32[]{:S(2)}, u32[]{:S(2)}) collective-permute-start(bf16[96,1024]{1,0:T(8,128)(2,1)} %get-tuple-element.36), channel_id=1, source_target_pairs={{0,6},{2,4},{4,2},{6,0},{1,7},{3,5},{5,3},{7,1},{8,14},{10,12},{12... | collective-permute-start | bytes 589832 | tf_op jit(solution)/shard_map/ppermute | solution.py:281
  12.7 1.4 %copy-done = bf16[1,2048,384]{2,1,0:T(8,128)(2,1)S(1)} copy-done((bf16[1,2048,384]{2,1,0:T(8,128)(2,1)S(1)}, bf16[1,2048,384]{2,1,0:T(8,128)(2,1)}, u32[]{:S(2)}) %copy-start) | copy-done | bytes 1572888
  14.1 1.4 %copy-done.2 = bf16[1,2048,384]{2,1,0:T(8,128)(2,1)S(1)} copy-done((bf16[1,2048,384]{2,1,0:T(8,128)(2,1)S(1)}, bf16[1,2048,384]{2,1,0:T(8,128)(2,1)}, u32[]{:S(2)}) %copy-start.2) | copy-done | bytes 1572888
  15.8 0.7 %copy-done.6 = bf16[96,1024]{1,0:T(8,128)(2,1)S(1)} copy-done((bf16[96,1024]{1,0:T(8,128)(2,1)S(1)}, bf16[96,1024]{1,0:T(8,128)(2,1)}, u32[]{:S(2)}) %copy-start.6) | copy-done | bytes 196632
  16.4 0.5 collective-permute-done.1.refs_2_
  17.0 0.5 collective-permute-start.4
  17.5 2.2 %collective-permute-done.7.refs_2_ = bf16[96,1024]{1,0:T(8,128)(2,1)S(1)} collective-permute-done((bf16[96,1024]{1,0:T(8,128)(2,1)}, bf16[96,1024]{1,0:T(8,128)(2,1)S(1)}, u32[]{:S(2)}, u32[]{:S(2)}) %collective-permute-start.7) | collective-permute-done | bytes 196640 | tf_op jit(solution)/shard_map/ppermute | solution.py:281
  19.7 4.2 %collective-permute-done.8.refs_3_ = bf16[96,1024]{1,0:T(8,128)(2,1)S(1)} collective-permute-done((bf16[96,1024]{1,0:T(8,128)(2,1)}, bf16[96,1024]{1,0:T(8,128)(2,1)S(1)}, u32[]{:S(2)}, u32[]{:S(2)}) %collective-permute-start.8) | collective-permute-done | bytes 196640 | tf_op jit(solution)/shard_map/ppermute | solution.py:281
  25.4 1.4 %shard_map.99 = (f32[384,384]{1,0:T(8,128)S(1)}, bf16[384,384]{1,0:T(8,128)(2,1)S(1)}, f32[384,384]{1,0:T(8,128)S(1)}, f32[384,384]{1,0:T(8,128)S(1)}) custom-call(bf16[384,1024]{1,0:T(8,128)(2,1)S(1)} %shard_map.97.refs_0_, bf16[384,1024]{1,0:T(8,128)(2,1)S(1)} %shard_map.98.refs_1_, bf16[2048,768]{1,0:T(8,128)(2,1)S(1)} %shard_map.95.refs_0_.refs_2_), custom_call_target="tpu_custom_call" | custom-call | tf_op jit(solution)/shard_map/pallas_call | solution.py:31
  27.1 0.9 %shard_map.102 = (bf16[512,384]{1,0:T(8,128)(2,1)S(1)}, bf16[512,384]{1,0:T(8,128)(2,1)S(1)}) custom-call(bf16[384,1024]{1,0:T(8,128)(2,1)S(1)} %shard_map.100.refs_0_.refs_1_, bf16[384,1024]{1,0:T(8,128)(2,1)S(1)} %shard_map.101.refs_1_.refs_2_, bf16[384,384]{1,0:T(8,128)(2,1)S(1)} %get-tuple-element.32.refs_0_.refs_2_), custom_call_target="tpu_custom_call" | custom-call | tf_op jit(solution)/shard_map/pallas_call | solution.py:31
  28.3 0.7 %collective-permute-start.15 = (bf16[512,384]{1,0:T(8,128)(2,1)S(1)}, bf16[512,384]{1,0:T(8,128)(2,1)S(1)}, u32[]{:S(2)}, u32[]{:S(2)}) collective-permute-start(bf16[512,384]{1,0:T(8,128)(2,1)S(1)} %get-tuple-element.37.refs_0_), channel_id=1, source_target_pairs={{8,16},{16,8},{9,17},{17,9},{10,18},{18,10},{11,19},{19,11},{12,20... | collective-permute-start | bytes 1179656 | tf_op jit(solution)/shard_map/ppermute | solution.py:342
  29.3 1.9 %shard_map.103 = (bf16[384,896]{1,0:T(8,128)(2,1)S(1)}, bf16[96,1152]{1,0:T(8,128)(2,1)S(1)}, bf16[96,1152]{1,0:T(8,128)(2,1)S(1)}, bf16[96,1152]{1,0:T(8,128)(2,1)S(1)}, bf16[96,1152]{1,0:T(8,128)(2,1)S(1)}) custom-call(bf16[512,384]{1,0:T(8,128)(2,1)S(1)} %get-tuple-element.37.refs_0_, bf16[384,1024]{1,0:T(8,128)(2,1)S(1)} %shard_map.100.refs_0_.refs_1_, ...), custom_call_target="tpu_custom_call" | custom-call | tf_op jit(solution)/shard_map/pallas_call | solution.py:31
  31.9 0.8 %collective-permute-done.16.refs_1_ = bf16[96,1152]{1,0:T(8,128)(2,1)S(1)} collective-permute-done((bf16[96,1152]{1,0:T(8,128)(2,1)S(1)}, bf16[96,1152]{1,0:T(8,128)(2,1)S(1)}, u32[]{:S(2)}, u32[]{:S(2)}) %collective-permute-start.16) | collective-permute-done | bytes 221216 | tf_op jit(solution)/shard_map/ppermute | solution.py:277
  32.9 6.2 %collective-permute-done.23.refs_3_ = bf16[512,384]{1,0:T(8,128)(2,1)S(1)} collective-permute-done((bf16[512,384]{1,0:T(8,128)(2,1)S(1)}, bf16[512,384]{1,0:T(8,128)(2,1)S(1)}, u32[]{:S(2)}, u32[]{:S(2)}) %collective-permute-start.23) | collective-permute-done | bytes 393248 | tf_op jit(solution)/shard_map/ppermute | solution.py:340
  39.1 2.6 %collective-permute-start.14 = (bf16[512,384]{1,0:T(8,128)(2,1)S(1)}, bf16[512,384]{1,0:T(8,128)(2,1)S(1)}, u32[]{:S(2)}, u32[]{:S(2)}) collective-permute-start(bf16[512,384]{1,0:T(8,128)(2,1)S(1)} %get-tuple-element.37.refs_0_), channel_id=1, source_target_pairs={{0,8},{24,16},{1,9},{25,17},{2,10},{26,18},{3,11},{27,19},{4,12},{... | collective-permute-start | bytes 1179656 | tf_op jit(solution)/shard_map/ppermute | solution.py:341
  42.4 1.0 %shard_map.104.refs_0_ = bf16[384,1152]{1,0:T(8,128)(2,1)S(1)} custom-call(bf16[512,384]{1,0:T(8,128)(2,1)S(1)} %collective-permute-done.15.refs_0_.refs_5_, bf16[384,896]{1,0:T(8,128)(2,1)S(1)} %get-tuple-element.41.refs_1_, bf16[2048,384]{1,0:T(8,128)(2,1)S(1)} %bitcast.10, bf16[2048,384]{1,0:T(8,128)(2,1)S(1)} %bitcast.13), custom_call_target="tpu_custom_call" | custom-call | tf_op jit(solution)/shard_map/pallas_call | solution.py:31
  43.9 0.6 collective-permute-start.20
  44.5 0.8 %collective-permute-start.21 = (bf16[96,1152]{1,0:T(8,128)(2,1)S(1)}, bf16[96,1152]{1,0:T(8,128)(2,1)S(1)}, u32[]{:S(2)}, u32[]{:S(2)}) collective-permute-start(bf16[96,1152]{1,0:T(8,128)(2,1)S(1)} %get-tuple-element.48), channel_id=1, source_target_pairs={{0,4},{2,6},{4,0},{6,2},{1,5},{3,7},{5,1},{7,3},{8,12},{10,14},{12... | collective-permute-start | bytes 663560 | tf_op jit(solution)/shard_map/ppermute | solution.py:281
  45.3 2.1 %collective-permute-start.22 = (bf16[96,1152]{1,0:T(8,128)(2,1)S(1)}, bf16[96,1152]{1,0:T(8,128)(2,1)S(1)}, u32[]{:S(2)}, u32[]{:S(2)}) collective-permute-start(bf16[96,1152]{1,0:T(8,128)(2,1)S(1)} %get-tuple-element.49), channel_id=1, source_target_pairs={{0,6},{2,4},{4,2},{6,0},{1,7},{3,5},{5,3},{7,1},{8,14},{10,12},{12... | collective-permute-start | bytes 663560 | tf_op jit(solution)/shard_map/ppermute | solution.py:281
  47.5 3.7 %collective-permute-done.14.refs_0_.refs_4_ = bf16[512,384]{1,0:T(8,128)(2,1)S(1)} collective-permute-done((bf16[512,384]{1,0:T(8,128)(2,1)S(1)}, bf16[512,384]{1,0:T(8,128)(2,1)S(1)}, u32[]{:S(2)}, u32[]{:S(2)}) %collective-permute-start.14) | collective-permute-done | bytes 393248 | tf_op jit(solution)/shard_map/ppermute | solution.py:341
  51.7 0.7 %collective-permute-done.20.refs_4_ = bf16[96,1152]{1,0:T(8,128)(2,1)S(1)} collective-permute-done((bf16[96,1152]{1,0:T(8,128)(2,1)S(1)}, bf16[96,1152]{1,0:T(8,128)(2,1)S(1)}, u32[]{:S(2)}, u32[]{:S(2)}) %collective-permute-start.20) | collective-permute-done | bytes 221216 | tf_op jit(solution)/shard_map/ppermute | solution.py:281
  52.3 3.2 %collective-permute-done.21.refs_5_ = bf16[96,1152]{1,0:T(8,128)(2,1)S(1)} collective-permute-done((bf16[96,1152]{1,0:T(8,128)(2,1)S(1)}, bf16[96,1152]{1,0:T(8,128)(2,1)S(1)}, u32[]{:S(2)}, u32[]{:S(2)}) %collective-permute-start.21) | collective-permute-done | bytes 221216 | tf_op jit(solution)/shard_map/ppermute | solution.py:281
  55.5 1.3 %shard_map.106 = (bf16[128,1024]{1,0:T(8,128)(2,1)}, f32[2,128]{1,0:T(2,128)}) custom-call(bf16[512,384]{1,0:T(8,128)(2,1)S(1)} %collective-permute-done.14.refs_0_.refs_4_, s32[2,128]{1,0:T(2,128)S(1)} %bitcast.16, f32[2,128]{1,0:T(2,128)S(1)} %bitcast.18, bf16[96,1152]{1,0:T(8,128)(2,1)S(1)} %get-tuple-element.46.refs_3_, ...), custom_call_target="tpu_custom_call" | custom-call | tf_op jit(solution)/shard_map/pallas_call | solution.py:31
  56.9 5.1 %collective-permute-done.24 = bf16[512,384]{1,0:T(8,128)(2,1)S(1)} collective-permute-done((bf16[512,384]{1,0:T(8,128)(2,1)S(1)}, bf16[512,384]{1,0:T(8,128)(2,1)S(1)}, u32[]{:S(2)}, u32[]{:S(2)}) %collective-permute-start.24) | collective-permute-done | bytes 393248 | tf_op jit(solution)/shard_map/ppermute | solution.py:345
  62.0 0.9 %add_bitcast_fusion = f32[1,512,384]{2,1,0:T(8,128)} fusion(f32[512,384]{1,0:T(8,128)S(1)} %shard_map.107, bf16[512,384]{1,0:T(8,128)(2,1)S(1)} %collective-permute-done.24), kind=kLoop, calls=%fused_computation | loop fusion | flops 393216 | bytes 1966080 | tf_op jit(solution)/shard_map/broadcast_in_dim | solution.py:373
  (52 shorter events, 5.0 us)
Async XLA Ops:
  3.2 8.1 %collective-permute-start = (bf16[96,1024]{1,0:T(8,128)(2,1)}, bf16[96,1024]{1,0:T(8,128)(2,1)S(1)}, u32[]{:S(2)}, u32[]{:S(2)}) collective-permute-start(bf16[96,1024]{1,0:T(8,128)(2,1)} %get-tuple-element.28), channel_id=1, source_target_pairs={{0,2},{2,0},{4,6},{6,4},{1,3},{3,1},{5,7},{7,5},{8,10},{10,8},{12,... | collective-permute-start | bytes 589832 | tf_op jit(solution)/shard_map/ppermute | solution.py:281
  4.7 12.3 %collective-permute-start.1 = (bf16[96,1024]{1,0:T(8,128)(2,1)}, bf16[96,1024]{1,0:T(8,128)(2,1)S(1)}, u32[]{:S(2)}, u32[]{:S(2)}) collective-permute-start(bf16[96,1024]{1,0:T(8,128)(2,1)} %get-tuple-element.30), channel_id=1, source_target_pairs={{0,4},{2,6},{4,0},{6,2},{1,5},{3,7},{5,1},{7,3},{8,12},{10,14},{12... | collective-permute-start | bytes 589832 | tf_op jit(solution)/shard_map/ppermute | solution.py:281
  5.2 11.7 %collective-permute-start.2 = (bf16[96,1024]{1,0:T(8,128)(2,1)}, bf16[96,1024]{1,0:T(8,128)(2,1)S(1)}, u32[]{:S(2)}, u32[]{:S(2)}) collective-permute-start(bf16[96,1024]{1,0:T(8,128)(2,1)} %get-tuple-element.31), channel_id=1, source_target_pairs={{0,6},{2,4},{4,2},{6,0},{1,7},{3,5},{5,3},{7,1},{8,14},{10,12},{12... | collective-permute-start | bytes 589832 | tf_op jit(solution)/shard_map/ppermute | solution.py:281
  6.7 13.0 %collective-permute-start.7 = (bf16[96,1024]{1,0:T(8,128)(2,1)}, bf16[96,1024]{1,0:T(8,128)(2,1)S(1)}, u32[]{:S(2)}, u32[]{:S(2)}) collective-permute-start(bf16[96,1024]{1,0:T(8,128)(2,1)} %get-tuple-element.34), channel_id=1, source_target_pairs={{0,2},{2,0},{4,6},{6,4},{1,3},{3,1},{5,7},{7,5},{8,10},{10,8},{12,... | collective-permute-start | bytes 589832 | tf_op jit(solution)/shard_map/ppermute | solution.py:281
  8.2 15.7 %collective-permute-start.8 = (bf16[96,1024]{1,0:T(8,128)(2,1)}, bf16[96,1024]{1,0:T(8,128)(2,1)S(1)}, u32[]{:S(2)}, u32[]{:S(2)}) collective-permute-start(bf16[96,1024]{1,0:T(8,128)(2,1)} %get-tuple-element.35), channel_id=1, source_target_pairs={{0,4},{2,6},{4,0},{6,2},{1,5},{3,7},{5,1},{7,3},{8,12},{10,14},{12... | collective-permute-start | bytes 589832 | tf_op jit(solution)/shard_map/ppermute | solution.py:281
  11.3 12.7 %collective-permute-start.9 = (bf16[96,1024]{1,0:T(8,128)(2,1)}, bf16[96,1024]{1,0:T(8,128)(2,1)S(1)}, u32[]{:S(2)}, u32[]{:S(2)}) collective-permute-start(bf16[96,1024]{1,0:T(8,128)(2,1)} %get-tuple-element.36), channel_id=1, source_target_pairs={{0,6},{2,4},{4,2},{6,0},{1,7},{3,5},{5,3},{7,1},{8,14},{10,12},{12... | collective-permute-start | bytes 589832 | tf_op jit(solution)/shard_map/ppermute | solution.py:281
  12.7 1.4 %copy-start = (bf16[1,2048,384]{2,1,0:T(8,128)(2,1)S(1)}, bf16[1,2048,384]{2,1,0:T(8,128)(2,1)}, u32[]{:S(2)}) copy-start(bf16[1,2048,384]{2,1,0:T(8,128)(2,1)} %param.11) | copy-start | bytes 4718596
  16.4 7.5 %copy-start.5 = (bf16[96,1024]{1,0:T(8,128)(2,1)S(1)}, bf16[96,1024]{1,0:T(8,128)(2,1)}, u32[]{:S(2)}) copy-start(bf16[96,1024]{1,0:T(8,128)(2,1)} %get-tuple-element.33.refs_1_) | copy-start | bytes 589828
  17.0 7.5 %collective-permute-start.3 = (bf16[96,1024]{1,0:T(8,128)(2,1)S(1)}, bf16[96,1024]{1,0:T(8,128)(2,1)S(1)}, u32[]{:S(2)}, u32[]{:S(2)}) collective-permute-start(bf16[96,1024]{1,0:T(8,128)(2,1)S(1)} %shard_map.96.refs_0_), channel_id=1, source_target_pairs={{0,1},{1,0},{2,3},{3,2},{4,5},{5,4},{6,7},{7,6},{8,9},{9,8},{10,11... | collective-permute-start | bytes 589832 | tf_op jit(solution)/shard_map/ppermute | solution.py:277
  17.0 7.6 %collective-permute-start.4 = (bf16[96,1024]{1,0:T(8,128)(2,1)S(1)}, bf16[96,1024]{1,0:T(8,128)(2,1)S(1)}, u32[]{:S(2)}, u32[]{:S(2)}) collective-permute-start(bf16[96,1024]{1,0:T(8,128)(2,1)S(1)} %collective-permute-done.refs_0_.refs_1_), channel_id=1, source_target_pairs={{0,1},{1,0},{2,3},{3,2},{4,5},{5,4},{6,7},{7,6},{8,9},{9,8},{10,11... | collective-permute-start | bytes 589832 | tf_op jit(solution)/shard_map/ppermute | solution.py:277
  19.7 5.3 %collective-permute-start.5 = (bf16[96,1024]{1,0:T(8,128)(2,1)S(1)}, bf16[96,1024]{1,0:T(8,128)(2,1)S(1)}, u32[]{:S(2)}, u32[]{:S(2)}) collective-permute-start(bf16[96,1024]{1,0:T(8,128)(2,1)S(1)} %collective-permute-done.1.refs_2_), channel_id=1, source_target_pairs={{0,1},{1,0},{2,3},{3,2},{4,5},{5,4},{6,7},{7,6},{8,9},{9,8},{10,11... | collective-permute-start | bytes 589832 | tf_op jit(solution)/shard_map/ppermute | solution.py:277
  23.9 1.4 %collective-permute-start.6 = (bf16[96,1024]{1,0:T(8,128)(2,1)S(1)}, bf16[96,1024]{1,0:T(8,128)(2,1)S(1)}, u32[]{:S(2)}, u32[]{:S(2)}) collective-permute-start(bf16[96,1024]{1,0:T(8,128)(2,1)S(1)} %collective-permute-done.2.refs_3_), channel_id=1, source_target_pairs={{0,1},{1,0},{2,3},{3,2},{4,5},{5,4},{6,7},{7,6},{8,9},{9,8},{10,11... | collective-permute-start | bytes 589832 | tf_op jit(solution)/shard_map/ppermute | solution.py:277
  24.0 3.0 %collective-permute-start.10 = (bf16[96,1024]{1,0:T(8,128)(2,1)S(1)}, bf16[96,1024]{1,0:T(8,128)(2,1)S(1)}, u32[]{:S(2)}, u32[]{:S(2)}) collective-permute-start(bf16[96,1024]{1,0:T(8,128)(2,1)S(1)} %copy-done.5), channel_id=1, source_target_pairs={{0,1},{1,0},{2,3},{3,2},{4,5},{5,4},{6,7},{7,6},{8,9},{9,8},{10,11... | collective-permute-start | bytes 589832 | tf_op jit(solution)/shard_map/ppermute | solution.py:277
  24.5 2.5 %collective-permute-start.11 = (bf16[96,1024]{1,0:T(8,128)(2,1)S(1)}, bf16[96,1024]{1,0:T(8,128)(2,1)S(1)}, u32[]{:S(2)}, u32[]{:S(2)}) collective-permute-start(bf16[96,1024]{1,0:T(8,128)(2,1)S(1)} %collective-permute-done.7.refs_2_), channel_id=1, source_target_pairs={{0,1},{1,0},{2,3},{3,2},{4,5},{5,4},{6,7},{7,6},{8,9},{9,8},{10,11... | collective-permute-start | bytes 589832 | tf_op jit(solution)/shard_map/ppermute | solution.py:277
  24.6 2.5 %collective-permute-start.12 = (bf16[96,1024]{1,0:T(8,128)(2,1)S(1)}, bf16[96,1024]{1,0:T(8,128)(2,1)S(1)}, u32[]{:S(2)}, u32[]{:S(2)}) collective-permute-start(bf16[96,1024]{1,0:T(8,128)(2,1)S(1)} %collective-permute-done.8.refs_3_), channel_id=1, source_target_pairs={{0,1},{1,0},{2,3},{3,2},{4,5},{5,4},{6,7},{7,6},{8,9},{9,8},{10,11... | collective-permute-start | bytes 589832 | tf_op jit(solution)/shard_map/ppermute | solution.py:277
  25.0 2.0 %collective-permute-start.13 = (bf16[96,1024]{1,0:T(8,128)(2,1)S(1)}, bf16[96,1024]{1,0:T(8,128)(2,1)S(1)}, u32[]{:S(2)}, u32[]{:S(2)}) collective-permute-start(bf16[96,1024]{1,0:T(8,128)(2,1)S(1)} %collective-permute-done.9.refs_4_), channel_id=1, source_target_pairs={{0,1},{1,0},{2,3},{3,2},{4,5},{5,4},{6,7},{7,6},{8,9},{9,8},{10,11... | collective-permute-start | bytes 589832 | tf_op jit(solution)/shard_map/ppermute | solution.py:277
  26.9 2.1 %copy-start.4 = (bf16[1,384,2048]{2,1,0:T(8,128)(2,1)S(1)}, bf16[1,384,2048]{2,1,0:T(8,128)(2,1)}, u32[]{:S(2)}) copy-start(bf16[1,384,2048]{2,1,0:T(8,128)(2,1)} %param.13) | copy-start | bytes 4718596
  27.0 2.1 %copy-start.1 = (bf16[1,2048,384]{2,1,0:T(8,128)(2,1)S(1)}, bf16[1,2048,384]{2,1,0:T(8,128)(2,1)}, u32[]{:S(2)}) copy-start(bf16[1,2048,384]{2,1,0:T(8,128)(2,1)} %param.11) | copy-start | bytes 4718596
  27.0 2.3 %copy-start.3 = (bf16[1,2048,384]{2,1,0:T(8,128)(2,1)S(1)}, bf16[1,2048,384]{2,1,0:T(8,128)(2,1)}, u32[]{:S(2)}) copy-start(bf16[1,2048,384]{2,1,0:T(8,128)(2,1)} %param.12) | copy-start | bytes 4718596
  28.0 11.1 %collective-permute-start.23 = (bf16[512,384]{1,0:T(8,128)(2,1)S(1)}, bf16[512,384]{1,0:T(8,128)(2,1)S(1)}, u32[]{:S(2)}, u32[]{:S(2)}) collective-permute-start(bf16[512,384]{1,0:T(8,128)(2,1)S(1)} %get-tuple-element.52), channel_id=1, source_target_pairs={{0,8},{8,0},{16,24},{24,16},{1,9},{9,1},{17,25},{25,17},{2,10},{10... | collective-permute-start | bytes 1179656 | tf_op jit(solution)/shard_map/ppermute | solution.py:340
  28.3 13.9 %collective-permute-start.15 = (bf16[512,384]{1,0:T(8,128)(2,1)S(1)}, bf16[512,384]{1,0:T(8,128)(2,1)S(1)}, u32[]{:S(2)}, u32[]{:S(2)}) collective-permute-start(bf16[512,384]{1,0:T(8,128)(2,1)S(1)} %get-tuple-element.37.refs_0_), channel_id=1, source_target_pairs={{8,16},{16,8},{9,17},{17,9},{10,18},{18,10},{11,19},{19,11},{12,20... | collective-permute-start | bytes 1179656 | tf_op jit(solution)/shard_map/ppermute | solution.py:342
  31.2 1.5 %collective-permute-start.16 = (bf16[96,1152]{1,0:T(8,128)(2,1)S(1)}, bf16[96,1152]{1,0:T(8,128)(2,1)S(1)}, u32[]{:S(2)}, u32[]{:S(2)}) collective-permute-start(bf16[96,1152]{1,0:T(8,128)(2,1)S(1)} %get-tuple-element.42), channel_id=1, source_target_pairs={{0,1},{1,0},{2,3},{3,2},{4,5},{5,4},{6,7},{7,6},{8,9},{9,8},{10,11... | collective-permute-start | bytes 663560 | tf_op jit(solution)/shard_map/ppermute | solution.py:277
  31.4 12.0 %collective-permute-start.17 = (bf16[96,1152]{1,0:T(8,128)(2,1)S(1)}, bf16[96,1152]{1,0:T(8,128)(2,1)S(1)}, u32[]{:S(2)}, u32[]{:S(2)}) collective-permute-start(bf16[96,1152]{1,0:T(8,128)(2,1)S(1)} %get-tuple-element.43), channel_id=1, source_target_pairs={{0,1},{1,0},{2,3},{3,2},{4,5},{5,4},{6,7},{7,6},{8,9},{9,8},{10,11... | collective-permute-start | bytes 663560 | tf_op jit(solution)/shard_map/ppermute | solution.py:277
  31.7 11.7 %collective-permute-start.18 = (bf16[96,1152]{1,0:T(8,128)(2,1)S(1)}, bf16[96,1152]{1,0:T(8,128)(2,1)S(1)}, u32[]{:S(2)}, u32[]{:S(2)}) collective-permute-start(bf16[96,1152]{1,0:T(8,128)(2,1)S(1)} %get-tuple-element.44), channel_id=1, source_target_pairs={{0,1},{1,0},{2,3},{3,2},{4,5},{5,4},{6,7},{7,6},{8,9},{9,8},{10,11... | collective-permute-start | bytes 663560 | tf_op jit(solution)/shard_map/ppermute | solution.py:277
  32.7 10.8 %collective-permute-start.19 = (bf16[96,1152]{1,0:T(8,128)(2,1)S(1)}, bf16[96,1152]{1,0:T(8,128)(2,1)S(1)}, u32[]{:S(2)}, u32[]{:S(2)}) collective-permute-start(bf16[96,1152]{1,0:T(8,128)(2,1)S(1)} %get-tuple-element.45), channel_id=1, source_target_pairs={{0,1},{1,0},{2,3},{3,2},{4,5},{5,4},{6,7},{7,6},{8,9},{9,8},{10,11... | collective-permute-start | bytes 663560 | tf_op jit(solution)/shard_map/ppermute | solution.py:277
  39.1 12.1 %collective-permute-start.14 = (bf16[512,384]{1,0:T(8,128)(2,1)S(1)}, bf16[512,384]{1,0:T(8,128)(2,1)S(1)}, u32[]{:S(2)}, u32[]{:S(2)}) collective-permute-start(bf16[512,384]{1,0:T(8,128)(2,1)S(1)} %get-tuple-element.37.refs_0_), channel_id=1, source_target_pairs={{0,8},{24,16},{1,9},{25,17},{2,10},{26,18},{3,11},{27,19},{4,12},{... | collective-permute-start | bytes 1179656 | tf_op jit(solution)/shard_map/ppermute | solution.py:341
  42.2 19.8 %collective-permute-start.24 = (bf16[512,384]{1,0:T(8,128)(2,1)S(1)}, bf16[512,384]{1,0:T(8,128)(2,1)S(1)}, u32[]{:S(2)}, u32[]{:S(2)}) collective-permute-start(bf16[512,384]{1,0:T(8,128)(2,1)S(1)} %shard_map.108), channel_id=1, source_target_pairs={{0,16},{16,0},{8,24},{24,8},{1,17},{17,1},{9,25},{25,9},{2,18},{18... | collective-permute-start | bytes 1179656 | tf_op jit(solution)/shard_map/ppermute | solution.py:345
  43.9 8.4 %collective-permute-start.20 = (bf16[96,1152]{1,0:T(8,128)(2,1)S(1)}, bf16[96,1152]{1,0:T(8,128)(2,1)S(1)}, u32[]{:S(2)}, u32[]{:S(2)}) collective-permute-start(bf16[96,1152]{1,0:T(8,128)(2,1)S(1)} %get-tuple-element.47), channel_id=1, source_target_pairs={{0,2},{2,0},{4,6},{6,4},{1,3},{3,1},{5,7},{7,5},{8,10},{10,8},{12,... | collective-permute-start | bytes 663560 | tf_op jit(solution)/shard_map/ppermute | solution.py:281
  44.5 11.0 %collective-permute-start.21 = (bf16[96,1152]{1,0:T(8,128)(2,1)S(1)}, bf16[96,1152]{1,0:T(8,128)(2,1)S(1)}, u32[]{:S(2)}, u32[]{:S(2)}) collective-permute-start(bf16[96,1152]{1,0:T(8,128)(2,1)S(1)} %get-tuple-element.48), channel_id=1, source_target_pairs={{0,4},{2,6},{4,0},{6,2},{1,5},{3,7},{5,1},{7,3},{8,12},{10,14},{12... | collective-permute-start | bytes 663560 | tf_op jit(solution)/shard_map/ppermute | solution.py:281
  45.3 10.2 %copy-start.7 = (s32[128,2]{0,1:T(2,128)S(1)}, s32[128,2]{0,1:T(2,128)}, u32[]{:S(2)}) copy-start(s32[128,2]{0,1:T(2,128)} %param.9) | copy-start | bytes 3076
  45.3 10.2 %copy-start.8 = (f32[128,2]{0,1:T(2,128)S(1)}, f32[128,2]{0,1:T(2,128)}, u32[]{:S(2)}) copy-start(f32[128,2]{0,1:T(2,128)} %param.10) | copy-start | bytes 3076
  45.3 10.2 %collective-permute-start.22 = (bf16[96,1152]{1,0:T(8,128)(2,1)S(1)}, bf16[96,1152]{1,0:T(8,128)(2,1)S(1)}, u32[]{:S(2)}, u32[]{:S(2)}) collective-permute-start(bf16[96,1152]{1,0:T(8,128)(2,1)S(1)} %get-tuple-element.49), channel_id=1, source_target_pairs={{0,6},{2,4},{4,2},{6,0},{1,7},{3,5},{5,3},{7,1},{8,14},{10,12},{12... | collective-permute-start | bytes 663560 | tf_op jit(solution)/shard_map/ppermute | solution.py:281
  (2 other events, 2.3 us)
